TPU v7x, 32 devices: a whole 2x2x4 slice. The times are simulated.
32 devices in a mesh: tile: 16 (over z, x, core), grp: 2 (over y).
Axes of the slice: x: 2, y: 2, z: 4, core: 2. Of those that a mesh axis runs over, the one named last changes fastest.
Arguments:
- features: bfloat16 [2, 8192, 64], P('grp', 'tile'), may hold values from -6 to 6
- cotangent: float32 [2, 8192, 64], P('grp', 'tile'), may hold values from -6 to 6
- geom_fine: bfloat16 [2, 8192, 3], P('grp', 'tile'), may hold values from -1 to 1
- geom_mid: bfloat16 [2, 2048, 3], P('grp'), may hold values from -1 to 1
- geom_coarse: bfloat16 [2, 512, 3], P('grp'), may hold values from -1 to 1
- links_fine: int32 [2, 8192, 16], P('grp', 'tile'), may hold values from 0 to 639
- slots_fine: int32 [2, 8192], P('grp', 'tile'), may hold values from 1 to 16, as said below
- send_lists: int32 [2, 2048], P('grp', 'tile'), may hold values from 0 to 511, as said below
- parent_fine: int32 [2, 8192], P('grp', 'tile'), may hold values from 0 to 2047, as said below
- parent_mid: int32 [2, 2048], P('grp'), may hold values from 0 to 511, as said below
- links_mid: int32 [2, 2048, 32], P('grp', 'tile'), may hold values from 0 to 2047
- slots_mid: int32 [2, 2048], P('grp', 'tile'), may hold values from 1 to 32, as said below
- links_coarse: int32 [2, 512, 32], P('grp', 'tile'), may hold values from 0 to 511
- slots_coarse: int32 [2, 512], P('grp', 'tile'), may hold values from 1 to 32, as said below
- kernel_in: float32 [3, 6, 256], P(None, None, ('tile', 'grp')), may hold values from -3 to 3
- kernel_bias: float32 [3, 2, 256], P(None, None, ('tile', 'grp')), may hold values from -0.5 to 0.5
- kernel_mid: float32 [3, 256, 256], P(None, ('tile', 'grp')), may hold values from -0.375 to 0.375
- kernel_out: float32 [3, 256, 4096], P(None, ('tile', 'grp')), may hold values from -0.02734375 to 0.02734375
- first_in: float32 [3, 6, 256], P(None, None, ('tile', 'grp')), may hold values from -0.768 to 0.768
- first_bias: float32 [3, 2, 256], P(None, None, ('tile', 'grp')), may hold values from -1.6384 to 1.6384
- first_mid: float32 [3, 256, 256], P(None, ('tile', 'grp')), may hold values from -8.704 to 8.704
- first_out: float32 [3, 256, 4096], P(None, ('tile', 'grp')), may hold values from -80.384 to 80.384
- second_in: float32 [3, 6, 256], P(None, None, ('tile', 'grp')), may hold values from 0.131072 to 0.524288
- second_bias: float32 [3, 2, 256], P(None, None, ('tile', 'grp')), may hold values from 0.524288 to 2.097152
- second_mid: float32 [3, 256, 256], P(None, ('tile', 'grp')), may hold values from 15.72864 to 62.91456
- second_out: float32 [3, 256, 4096], P(None, ('tile', 'grp')), may hold values from 1284.5056 to 5138.0225
Outputs:
- layer_out: bfloat16 [2, 8192, 64], P('grp', 'tile')
- grad_features: bfloat16 [2, 8192, 64], P('grp', 'tile')
- master_in: float32 [3, 6, 256], P(None, None, ('tile', 'grp'))
- master_bias: float32 [3, 2, 256], P(None, None, ('tile', 'grp'))
- master_mid: float32 [3, 256, 256], P(None, ('tile', 'grp'))
- master_out: float32 [3, 256, 4096], P(None, ('tile', 'grp'))
- moment_in: float32 [3, 6, 256], P(None, None, ('tile', 'grp'))
- moment_bias: float32 [3, 2, 256], P(None, None, ('tile', 'grp'))
- moment_mid: float32 [3, 256, 256], P(None, ('tile', 'grp'))
- moment_out: float32 [3, 256, 4096], P(None, ('tile', 'grp'))
- square_in: float32 [3, 6, 256], P(None, None, ('tile', 'grp'))
- square_bias: float32 [3, 2, 256], P(None, None, ('tile', 'grp'))
- square_mid: float32 [3, 256, 256], P(None, ('tile', 'grp'))
- square_out: float32 [3, 256, 4096], P(None, ('tile', 'grp'))
Inputs may be any that keep to these rules, and one draw needn't show every extreme that they name: `slots_fine`: in every tile's rows of each group some node uses all 16 slots. `send_lists`: the first 64 entries of a tile name rows among its first quarter, the last 64 rows among its last quarter. `parent_fine`: the parent of fine node i differs from i // 4 by at most 8, and by exactly that much for some node; a middle node may have no children. `parent_mid`: the parent of middle node j differs from j // 4 by at most 4, and by exactly that much for some node; a coarsest node may have no children. `slots_mid`: among the rows of one index of tile some node uses all 32 slots. `slots_coarse`: among the rows of one index of tile some node uses all 32 slots.
All inputs are finite; a program needn't handle non-finite values.
Results may differ from a plain program's by a relative error of at most 0.0087.
The roundings to bfloat16 on the way count: a program that leaves them out, or rounds other values in their place, can miss the bound.
Values may be sent and summed in bfloat16 or wider, within the bound.
A program may use at most 128 MiB of HBM per device.

v0:
```python
import jax
import jax.numpy as jnp
from jax import lax
from jax.sharding import PartitionSpec as P

STEP = 5


PRECISE = lax.Precision.HIGHEST
B_ONE = 0.9
B_TWO = 0.95
EPSILON = 1e-08
WEIGHT_DECAY = 0.1
RATE_FIRST = 0.4
RATE_MAIN = 0.02


def extended_2(cells, sides, width):
    for axis, dim in sides:
        count = lax.axis_size(axis)
        ends = count - 1
        head = lax.slice_in_dim(cells, 0, width, axis=dim)
        tail = lax.slice_in_dim(cells, cells.shape[dim] - width, cells.shape[dim], axis=dim)
        cells = jnp.concatenate(
            [
                lax.ppermute(tail, axis, [(i, (i + 1) % count) for i in range(ends)]),
                cells,
                lax.ppermute(head, axis, [((i + 1) % count, i) for i in range(ends)]),
            ],
            axis=dim,
        )
    return cells


def silu_grad(field_value):
    sigmoid_value = jax.nn.sigmoid(field_value)
    return sigmoid_value * (1.0 + field_value * (1.0 - sigmoid_value))


def edge_inputs(geom_dst, geom_src):
    return jnp.concatenate(
        [jnp.broadcast_to(geom_dst[:, None, :], geom_src.shape), geom_src], axis=2
    ).astype(jnp.float32)


def kernel_forward(weights, inputs):
    w_first, bias_pair, w_second, w_third = weights
    pre_one = jnp.einsum(
        "bki,ih->bkh", inputs, w_first.astype(jnp.float32), precision=PRECISE
    ) + bias_pair[0].astype(jnp.float32)
    act_one = jax.nn.silu(pre_one).astype(jnp.bfloat16)
    pre_two = jnp.einsum(
        "bkh,hj->bkj", act_one, w_second, preferred_element_type=jnp.float32
    ) + bias_pair[1].astype(jnp.float32)
    act_two = jax.nn.silu(pre_two).astype(jnp.bfloat16)
    kernel = jnp.einsum("bkj,jq->bkq", act_two, w_third, preferred_element_type=jnp.float32).astype(
        jnp.bfloat16
    )
    return (pre_one, act_one, pre_two, act_two, kernel)


def block_layout(lengths, slot_count):
    row_count = lengths.shape[0]
    block_rows = min(row_count, max(1, 512 // slot_count))
    return (row_count // block_rows, block_rows)


def slot_masks(lengths, slot_count):
    return (
        lax.broadcasted_iota(jnp.int32, (lengths.shape[0], slot_count), 1) < lengths[:, None]
    ).astype(jnp.float32)


def level_messages(weights, geom_dst, geom_src, sources, lengths):
    slot_count = geom_src.shape[1]
    feat_width = sources.shape[2]
    block_count, block_rows = block_layout(lengths, slot_count)

    def block_sum(block_data):
        part_dst, part_src, part_sources, part_lengths = block_data
        kernel = kernel_forward(weights, edge_inputs(part_dst, part_src))[4]
        kernel = kernel.reshape(part_dst.shape[0], slot_count, feat_width, feat_width)
        applied = jnp.einsum(
            "bkoc,bkc->bko", kernel, part_sources, preferred_element_type=jnp.float32
        )
        return jnp.sum(applied * slot_masks(part_lengths, slot_count)[:, :, None], axis=1)

    def to_blocks(array):
        return array.reshape((block_count, block_rows) + array.shape[1:])

    totals = lax.map(
        block_sum,
        (to_blocks(geom_dst), to_blocks(geom_src), to_blocks(sources), to_blocks(lengths)),
    )
    return totals.reshape(lengths.shape[0], feat_width) / lengths.astype(jnp.float32)[:, None]


def level_backward(weights, geom_dst, geom_src, sources, lengths, grad_sums):
    w_first, bias_pair, w_second, w_third = weights
    slot_count = geom_src.shape[1]
    feat_width = sources.shape[2]
    hidden_width = w_second.shape[0]
    block_count, block_rows = block_layout(lengths, slot_count)

    def block_grad(carry, block_data):
        part_dst, part_src, part_sources, part_lengths, part_grads = block_data
        inputs = edge_inputs(part_dst, part_src)
        pre_one, act_one, pre_two, act_two, kernel = kernel_forward(weights, inputs)
        edge_rows = part_dst.shape[0]
        kernel = kernel.reshape(edge_rows, slot_count, feat_width, feat_width)
        slot_mask = slot_masks(part_lengths, slot_count)
        weighted = (part_grads.astype(jnp.float32)[:, None, :] * slot_mask[:, :, None]).astype(
            jnp.bfloat16
        )
        grad_source = jnp.einsum(
            "bkoc,bko->bkc", kernel, weighted, preferred_element_type=jnp.float32
        )
        grad_kernel = (
            weighted.astype(jnp.float32)[:, :, :, None]
            * part_sources.astype(jnp.float32)[:, :, None, :]
        )
        grad_kernel = grad_kernel.reshape(edge_rows, slot_count, feat_width * feat_width).astype(
            jnp.bfloat16
        )
        acc_first, acc_bias, acc_second, acc_third = carry
        acc_third = acc_third + jnp.einsum(
            "bkj,bkq->jq", act_two, grad_kernel, preferred_element_type=jnp.float32
        )
        grad_act_two = jnp.einsum(
            "bkq,jq->bkj", grad_kernel, w_third, preferred_element_type=jnp.float32
        )
        grad_pre_two = (grad_act_two * silu_grad(pre_two)).astype(jnp.bfloat16)
        acc_second = acc_second + jnp.einsum(
            "bkh,bkj->hj", act_one, grad_pre_two, preferred_element_type=jnp.float32
        )
        grad_act_one = jnp.einsum(
            "bkj,hj->bkh", grad_pre_two, w_second, preferred_element_type=jnp.float32
        )
        grad_pre_one = grad_act_one * silu_grad(pre_one)
        acc_first = acc_first + jnp.einsum("bki,bkh->ih", inputs, grad_pre_one, precision=PRECISE)
        bias_terms = jnp.stack(
            [
                jnp.sum(grad_pre_one, axis=(0, 1)),
                jnp.sum(grad_pre_two.astype(jnp.float32), axis=(0, 1)),
            ]
        )
        acc_bias = acc_bias + bias_terms
        return ((acc_first, acc_bias, acc_second, acc_third), grad_source)

    def to_blocks(array):
        return array.reshape((block_count, block_rows) + array.shape[1:])

    initial = (
        jnp.zeros(w_first.shape, jnp.float32),
        jnp.zeros(bias_pair.shape, jnp.float32),
        jnp.zeros((hidden_width, hidden_width), jnp.float32),
        jnp.zeros(w_third.shape, jnp.float32),
    )
    weight_sums, grad_sources = lax.scan(
        block_grad,
        initial,
        (
            to_blocks(geom_dst),
            to_blocks(geom_src),
            to_blocks(sources),
            to_blocks(lengths),
            to_blocks(grad_sums),
        ),
    )
    return (weight_sums, grad_sources.reshape(lengths.shape[0], slot_count, feat_width))


def adamw(master, moment, square, grad, learn_rate):
    moment_new = B_ONE * moment + (1.0 - B_ONE) * grad
    square_new = B_TWO * square + (1.0 - B_TWO) * grad * grad
    fix_one = 1.0 - B_ONE**STEP
    fix_two = 1.0 - B_TWO**STEP
    master_new = master - learn_rate * (
        moment_new / fix_one / (jnp.sqrt(square_new / fix_two) + EPSILON) + WEIGHT_DECAY * master
    )
    return (master_new, moment_new, square_new)


def add_edges(window, padded, margin):
    own = window[margin : window.shape[0] - margin]
    own = own.at[:margin].add(padded[:margin])
    return own.at[own.shape[0] - margin :].add(padded[padded.shape[0] - margin :])


def replicate_rows(own_rows):
    return lax.all_gather(own_rows, "tile", axis=0, tiled=True)


def per_device(
    features,
    cotangent,
    geom_fine,
    geom_mid,
    geom_coarse,
    links_fine,
    slots_fine,
    send_lists,
    parent_fine,
    parent_mid,
    links_mid,
    slots_mid,
    links_coarse,
    slots_coarse,
    kernel_in,
    kernel_bias,
    kernel_mid,
    kernel_out,
    first_in,
    first_bias,
    first_mid,
    first_out,
    second_in,
    second_bias,
    second_mid,
    second_out,
):
    full_in, full_bias, full_mid, full_out = (
        lax.all_gather(kernel_in.astype(jnp.bfloat16), ("tile", "grp"), axis=2, tiled=True),
        lax.all_gather(kernel_bias.astype(jnp.bfloat16), ("tile", "grp"), axis=2, tiled=True),
        lax.all_gather(kernel_mid.astype(jnp.bfloat16), ("tile", "grp"), axis=1, tiled=True),
        lax.all_gather(kernel_out.astype(jnp.bfloat16), ("tile", "grp"), axis=1, tiled=True),
    )

    def level_weights(level_index):
        return (
            full_in[level_index],
            full_bias[level_index],
            full_mid[level_index],
            full_out[level_index],
        )

    feats = features[0]
    row_count = feats.shape[0]
    feat_width = feats.shape[1]
    send_list = send_lists[0]
    halo_rows = send_list.shape[0] // 2
    fine_geom = geom_fine[0]
    node_table = jnp.concatenate([feats, fine_geom], axis=1)
    padded = extended_2(node_table[send_list], (("tile", 0),), halo_rows)
    extended = jnp.concatenate([node_table, padded[:halo_rows], padded[3 * halo_rows :]], axis=0)
    fine_links = links_fine[0]
    fine_lengths = slots_fine[0]
    gathered = extended[fine_links]
    fine_sources = gathered[:, :, :feat_width]
    fine_src_geom = gathered[:, :, feat_width:]
    base = feats.astype(jnp.float32) + level_messages(
        level_weights(0), fine_geom, fine_src_geom, fine_sources, fine_lengths
    )
    mid_geom = geom_mid[0]
    mid_total = mid_geom.shape[0]
    parents = parent_fine[0]
    mid_links = links_mid[0]
    mid_lengths = slots_mid[0]
    coarse_geom = geom_coarse[0]
    coarse_total = coarse_geom.shape[0]
    mid_parents = parent_mid[0]
    coarse_links = links_coarse[0]
    coarse_lengths = slots_coarse[0]
    coarse_scale = jnp.maximum(
        jax.ops.segment_sum(
            jnp.ones((mid_total,), jnp.float32), mid_parents, num_segments=coarse_total
        ),
        1.0,
    )
    mid_rows = mid_lengths.shape[0]
    coarse_rows = coarse_lengths.shape[0]
    mid_start = lax.axis_index("tile") * mid_rows
    coarse_start = lax.axis_index("tile") * coarse_rows
    mid_geom_own = lax.dynamic_slice_in_dim(mid_geom, mid_start, mid_rows, 0)
    coarse_geom_own = lax.dynamic_slice_in_dim(coarse_geom, coarse_start, coarse_rows, 0)
    margin_mid = min(8, mid_rows)
    local_mid = parents - (mid_start - margin_mid)
    window_count = mid_rows + 2 * margin_mid

    def back_own(level_index, sources, geom_all, geom_own, own_links, own_lengths, grad_own):
        grad_sums = (grad_own / own_lengths.astype(jnp.float32)[:, None]).astype(jnp.bfloat16)
        weight_sums, grad_sources = level_backward(
            level_weights(level_index),
            geom_own,
            geom_all[own_links],
            sources[own_links],
            own_lengths,
            grad_sums,
        )
        partial_value = jax.ops.segment_sum(
            grad_sources.reshape(-1, feat_width),
            own_links.reshape(-1),
            num_segments=sources.shape[0],
        )
        return (weight_sums, partial_value)

    part_sum = jax.ops.segment_sum(base, parents, num_segments=mid_total)
    part_count = jax.ops.segment_sum(
        jnp.ones((row_count,), jnp.float32), parents, num_segments=mid_total
    )
    mid_sum, mid_count = lax.psum((part_sum, part_count), "tile")
    mid_scale = jnp.maximum(mid_count, 1.0)
    mid_value = mid_sum / mid_scale[:, None]

    def coarse_level(level_index, field_value, geom_all, geom_own, own_links, own_lengths):
        sources = field_value.astype(jnp.bfloat16)
        own_messages = level_messages(
            level_weights(level_index),
            geom_own,
            geom_all[own_links],
            sources[own_links],
            own_lengths,
        )
        return field_value + replicate_rows(own_messages)

    mid_out = coarse_level(1, mid_value, mid_geom, mid_geom_own, mid_links, mid_lengths)
    coarse_value = (
        jax.ops.segment_sum(mid_out, mid_parents, num_segments=coarse_total) / coarse_scale[:, None]
    )
    coarse_out = coarse_level(
        2, coarse_value, coarse_geom, coarse_geom_own, coarse_links, coarse_lengths
    )
    up_mid = mid_out + coarse_out[mid_parents]
    up_fine = base + up_mid[parents]
    layer_value = jax.nn.silu(up_fine).astype(jnp.bfloat16)
    grad_top = cotangent[0] * silu_grad(up_fine)
    win_grad = jax.ops.segment_sum(grad_top, local_mid, num_segments=window_count)
    grad_edges = jnp.concatenate(
        [win_grad[:margin_mid], win_grad[window_count - margin_mid :]], axis=0
    )
    pad_grad = extended_2(grad_edges, (("tile", 0),), margin_mid)
    grad_up_mid = replicate_rows(add_edges(win_grad, pad_grad, margin_mid))
    grad_coarse_out = jax.ops.segment_sum(grad_up_mid, mid_parents, num_segments=coarse_total)

    def coarse_back(
        level_index, field_value, geom_all, geom_own, own_links, own_lengths, grad_output, own_start
    ):
        grad_own = lax.dynamic_slice_in_dim(grad_output, own_start, own_lengths.shape[0], 0)
        weight_sums, partial_value = back_own(
            level_index,
            field_value.astype(jnp.bfloat16),
            geom_all,
            geom_own,
            own_links,
            own_lengths,
            grad_own,
        )
        return (grad_output + lax.psum(partial_value, "tile"), weight_sums)

    grad_coarse_value, sums_coarse = coarse_back(
        2,
        coarse_value,
        coarse_geom,
        coarse_geom_own,
        coarse_links,
        coarse_lengths,
        grad_coarse_out,
        coarse_start,
    )
    grad_mid_out = grad_up_mid + (grad_coarse_value / coarse_scale[:, None])[mid_parents]
    grad_mid_value, sums_mid = coarse_back(
        1, mid_value, mid_geom, mid_geom_own, mid_links, mid_lengths, grad_mid_out, mid_start
    )
    grad_base = grad_top + (grad_mid_value / mid_scale[:, None])[parents]
    fine_grad_sums = (grad_base / fine_lengths.astype(jnp.float32)[:, None]).astype(jnp.bfloat16)
    sums_fine, fine_grad_sources = level_backward(
        level_weights(0), fine_geom, fine_src_geom, fine_sources, fine_lengths, fine_grad_sums
    )
    grad_extended = jax.ops.segment_sum(
        fine_grad_sources.reshape(-1, feat_width),
        fine_links.reshape(-1),
        num_segments=row_count + 2 * halo_rows,
    )
    returned = extended_2(grad_extended[row_count:], (("tile", 0),), halo_rows)
    back_rows = jnp.concatenate([returned[:halo_rows], returned[3 * halo_rows :]], axis=0)
    grad_feats = (
        grad_base
        + grad_extended[:row_count]
        + jax.ops.segment_sum(back_rows, send_list, num_segments=row_count)
    )
    reduced = (
        lax.psum_scatter(
            jnp.stack([sums_fine[0], sums_mid[0], sums_coarse[0]]),
            ("tile", "grp"),
            scatter_dimension=2,
            tiled=True,
        ),
        lax.psum_scatter(
            jnp.stack([sums_fine[1], sums_mid[1], sums_coarse[1]]),
            ("tile", "grp"),
            scatter_dimension=2,
            tiled=True,
        ),
        lax.psum_scatter(
            jnp.stack([sums_fine[2], sums_mid[2], sums_coarse[2]]),
            ("tile", "grp"),
            scatter_dimension=1,
            tiled=True,
        ),
        lax.psum_scatter(
            jnp.stack([sums_fine[3], sums_mid[3], sums_coarse[3]]),
            ("tile", "grp"),
            scatter_dimension=1,
            tiled=True,
        ),
    )
    new_in = adamw(kernel_in, first_in, second_in, reduced[0], RATE_FIRST)
    new_bias = adamw(kernel_bias, first_bias, second_bias, reduced[1], RATE_MAIN)
    new_mid = adamw(kernel_mid, first_mid, second_mid, reduced[2], RATE_MAIN)
    new_out = adamw(kernel_out, first_out, second_out, reduced[3], RATE_MAIN)
    return (
        layer_value[None],
        grad_feats.astype(jnp.bfloat16)[None],
        new_in[0],
        new_bias[0],
        new_mid[0],
        new_out[0],
        new_in[1],
        new_bias[1],
        new_mid[1],
        new_out[1],
        new_in[2],
        new_bias[2],
        new_mid[2],
        new_out[2],
    )


def solution(mesh):
    return jax.shard_map(
        per_device,
        mesh=mesh,
        in_specs=(
            P("grp", "tile", None),
            P("grp", "tile", None),
            P("grp", "tile", None),
            P("grp", None, None),
            P("grp", None, None),
            P("grp", "tile", None),
            P("grp", "tile"),
            P("grp", "tile"),
            P("grp", "tile"),
            P("grp", None),
            P("grp", "tile", None),
            P("grp", "tile"),
            P("grp", "tile", None),
            P("grp", "tile"),
            P(None, None, ("tile", "grp")),
            P(None, None, ("tile", "grp")),
            P(None, ("tile", "grp"), None),
            P(None, ("tile", "grp"), None),
            P(None, None, ("tile", "grp")),
            P(None, None, ("tile", "grp")),
            P(None, ("tile", "grp"), None),
            P(None, ("tile", "grp"), None),
            P(None, None, ("tile", "grp")),
            P(None, None, ("tile", "grp")),
            P(None, ("tile", "grp"), None),
            P(None, ("tile", "grp"), None),
        ),
        out_specs=(
            P("grp", "tile", None),
            P("grp", "tile", None),
            P(None, None, ("tile", "grp")),
            P(None, None, ("tile", "grp")),
            P(None, ("tile", "grp"), None),
            P(None, ("tile", "grp"), None),
            P(None, None, ("tile", "grp")),
            P(None, None, ("tile", "grp")),
            P(None, ("tile", "grp"), None),
            P(None, ("tile", "grp"), None),
            P(None, None, ("tile", "grp")),
            P(None, None, ("tile", "grp")),
            P(None, ("tile", "grp"), None),
            P(None, ("tile", "grp"), None),
        ),
        check_vma=False,
    )
```

profile of v0, /device:TPU:1, one launch (start us, length us, event | category | flops | bytes accessed | tf_op | source)
XLA Modules:
  0.0 3445.5 jit_solution(13848545432971826311)
XLA Ops:
  28.2 14.8 scatter_custom_fusion.3
  43.0 65.5 %all_gather.22 = bf16[3,2,256]{0,1,2:T(2,128)(2,1)S(1)} all-gather(bf16[3,2,8]{0,1,2:T(2,128)(2,1)S(1)} %copy.279), channel_id=1, replica_groups=mesh['tile'=16,'grp'=2] {'tile','grp'}, dimensions={2}, use_global_device_ids=true | all-gather | bytes 3168 | tf_op jit(solution)/shard_map/all_gather | solution.py:224
  108.5 32.8 psum.29
  141.3 62.2 %all_gather.21 = bf16[3,6,256]{1,0,2:T(4,128)(2,1)S(1)} all-gather(bf16[3,6,8]{1,0,2:T(4,128)(2,1)S(1)} %copy.277), channel_id=1, replica_groups=mesh['tile'=16,'grp'=2] {'tile','grp'}, dimensions={2}, use_global_device_ids=true | all-gather | bytes 9504 | tf_op jit(solution)/shard_map/all_gather | solution.py:223
  205.4 67.8 %all_gather.23 = bf16[3,256,256]{2,1,0:T(8,128)(2,1)S(1)} all-gather(bf16[3,8,256]{2,1,0:T(8,128)(2,1)S(1)} %convert_element_type.454), channel_id=1, replica_groups=mesh['tile'=16,'grp'=2] {'tile','grp'}, dimensions={1}, use_global_device_ids=true | all-gather | bytes 405504 | tf_op jit(solution)/shard_map/all_gather | solution.py:225
  282.6 24.0 gather_fusion.1
  317.3 437.1 %while.89 = (s32[]{:T(128)}, f32[16,32,64]{2,1,0:T(8,128)S(1)}, bf16[16,32,3]{1,2,0:T(4,128)(2,1)S(1)}, bf16[16,32,16,3]{1,2,3,0:T(8,128)(2,1)S(1)}, bf16[6,256]...) while((s32[]{:T(128)}, f32[16,32,64]{2,1,0:T(8,128)S(1)}, ...), condition=%wide.region_2.3_spmd, body=%wide.region_0.2_spmd.sunk | while | flops 1150355968 | bytes 20082752 | solution.py:91
  323.1 12.6 reshape.1018
  350.4 12.6 reshape.1018
  432.3 12.6 reshape.1018
  778.4 71.5 %all-reduce.7.cloned.1.call-done = f32[2048,64]{1,0:T(8,128)} async-done(((f32[2048,64]{1,0:T(8,128)}), f32[2048,64]{1,0:T(8,128)}) %all-reduce.7.cloned.1.call-update) | async-done | bytes 524304 | tf_op jit(solution)/shard_map/psum | solution.py:301
  851.5 15.0 gather_fusion.3
  866.5 211.0 %while.90 = (s32[]{:T(128)}, f32[8,16,64]{2,1,0:T(8,128)S(1)}, bf16[8,16,3]{1,2,0:T(4,128)(2,1)S(1)}, bf16[8,16,32,3]{2,3,1,0:T(4,128)(2,1)S(1)}, bf16[6,256]{1,...) while((s32[]{:T(128)}, f32[8,16,64]{2,1,0:T(8,128)S(1)}, ...), condition=%wide.region_9.10_spmd, body=%wide.region_7.9_spmd.sunk | while | flops 1150366208 | bytes 20037408 | solution.py:91
  1055.3 12.6 reshape.1019
  1078.3 23.8 all_gather.25
  1102.1 14.2 scatter_custom_fusion.2
  1120.6 49.6 %while.91 = (s32[]{:T(128)}, f32[2,16,64]{2,1,0:T(8,128)S(1)}, bf16[2,16,3]{1,2,0:T(4,128)(2,1)S(1)}, bf16[2,16,32,3]{2,3,1,0:T(4,128)(2,1)S(1)}, bf16[6,256]{1,...) while((s32[]{:T(128)}, f32[2,16,64]{2,1,0:T(8,128)S(1)}, ...), condition=%wide.region_14.15_spmd, body=%wide.region_12.14_spmd.sunk | while | flops 1150366208 | bytes 20037408 | solution.py:91
  1170.3 18.1 all_gather.26
  1212.8 22.5 all_gather.27
  1248.0 108.8 %while.92 = (s32[]{:T(128)}, f32[6,256]{1,0:T(8,128)S(1)}, f32[2,256]{1,0:T(2,128)S(1)}, f32[256,256]{1,0:T(8,128)}, f32[256,4096]{1,0:T(8,128)}, /*index=5*/f32...) while((s32[]{:T(128)}, f32[6,256]{1,0:T(8,128)S(1)}, ...), condition=%wide.region_20.21_spmd.clone, body=%wide.region_17.20_spmd.clone.sunk | while | flops 3451943424 | bytes 81133624 | solution.py:159
  1364.6 85.7 %all-reduce.9.cloned.1.call-done = f32[512,64]{1,0:T(8,128)} async-done(((f32[512,64]{1,0:T(8,128)}), f32[512,64]{1,0:T(8,128)}) %all-reduce.9.cloned.1.call-update) | async-done | bytes 131088 | tf_op jit(solution)/shard_map/psum | solution.py:348
  1461.7 451.3 %while.93 = (s32[]{:T(128)}, f32[6,256]{1,0:T(8,128)S(1)}, f32[2,256]{1,0:T(2,128)S(1)}, f32[256,256]{1,0:T(8,128)}, f32[256,4096]{1,0:T(8,128)}, /*index=5*/f32...) while((s32[]{:T(128)}, f32[6,256]{1,0:T(8,128)S(1)}, ...), condition=%wide.region_26.27_spmd.clone, body=%wide.region_23.26_spmd.clone.sunk | while | flops 3451943424 | bytes 77857224 | solution.py:159
  1913.0 23.7 scatter_custom_fusion.7
  1936.8 92.4 %all-reduce.11.cloned.1.call-done = f32[2048,64]{1,0:T(8,128)} async-done(((f32[2048,64]{1,0:T(8,128)}), f32[2048,64]{1,0:T(8,128)}) %all-reduce.11.cloned.1.call-update) | async-done | bytes 524304 | tf_op jit(solution)/shard_map/psum | solution.py:348
  2034.3 997.3 %while.94 = (s32[]{:T(128)}, f32[6,256]{1,0:T(8,128)S(1)}, f32[2,256]{1,0:T(2,128)S(1)}, f32[256,256]{1,0:T(8,128)}, f32[256,4096]{1,0:T(8,128)}, /*index=5*/f32...) while((s32[]{:T(128)}, f32[6,256]{1,0:T(8,128)S(1)}, ...), condition=%wide.region_32.33_spmd.clone, body=%wide.region_29.32_spmd.clone.sunk | while | flops 3451922944 | bytes 63343392 | solution.py:159
  2440.5 12.6 reshape.1023
  2565.3 12.6 reshape.1023
  2627.7 12.6 reshape.1023
  3046.8 44.4 %scatter_custom_fusion.8 = f32[640,64]{1,0:T(8,128)S(1)} fusion(s32[8192]{0:T(1024)S(1)} %reshape.879, f32[8192,64]{1,0:T(8,128)} %bitcast.91, f32[]{:T(128)} %constant.260.clone.1), kind=kCustom, calls=%fused_computation.268 | custom fusion | flops 524288 | bytes 164352 | tf_op jit(solution)/shard_map/scatter-add | solution.py:369
  3097.2 40.7 %all-reduce.2 = (f32[3,6,256]{2,1,0:T(8,128)S(1)}, f32[3,2,256]{2,1,0:T(2,128)S(1)}) all-reduce(f32[3,6,256]{2,1,0:T(8,128)S(1)} %pad_maximum_fusion.12, f32[3,2,256]{2,1,0:T(2,128)S(1)} %pad_maximum_fusion.13), channel_id=2, replica_groups=mesh['tile'=16,'grp'=2] {'tile','grp'}, use_global_device_ids=true, to_apply=%region_35.36.clone | all-reduce | flops 6144 | bytes 49152
  3141.7 24.2 reduce-scatter.5.cloned.1.call-done
  3167.3 269.0 %reduce-scatter.7.cloned.1.call-done = f32[3,8,4096]{2,1,0:T(8,128)} async-done(((f32[3,256,4096]{2,1,0:T(8,128)}), f32[3,8,4096]{2,1,0:T(8,128)}) %reduce-scatter.7.cloned.1.call-update) | async-done | bytes 393232 | tf_op jit(solution)/shard_map/reduce_scatter | solution.py:400
  (1632 shorter events, 2324.1 us)
Async XLA Ops:
  7.2 274.9 %copy-start.75 = (bf16[1,512,3]{1,2,0:T(4,128)(2,1)S(1)}, bf16[1,512,3]{1,2,0:T(4,128)(2,1)}, u32[]{:S(2)}) copy-start(bf16[1,512,3]{1,2,0:T(4,128)(2,1)} %param.44) | copy-start | bytes 9220
  7.2 274.3 %copy-start.81 = (s32[1,2048]{1,0:T(1,128)S(1)}, s32[1,2048]{1,0:T(1,128)}, u32[]{:S(2)}) copy-start(s32[1,2048]{1,0:T(1,128)} %param.51) | copy-start | bytes 24580
  7.2 274.3 %copy-start.72 = (bf16[1,2048,3]{1,2,0:T(4,128)(2,1)S(1)}, bf16[1,2048,3]{1,2,0:T(4,128)(2,1)}, u32[]{:S(2)}) copy-start(bf16[1,2048,3]{1,2,0:T(4,128)(2,1)} %param.45) | copy-start | bytes 36868
  7.2 304.6 %all-gather.2.cloned.1.call-start = ((), (), s32[]{:S(2)}) async-start(), calls=%async_computation.2 | async-start | bytes 6488064 | tf_op jit(solution)/shard_map/all_gather | solution.py:226
  9.0 840.9 %all-reduce.7.cloned.1.call-start = ((), (), s32[]{:S(2)}) async-start(), calls=%async_computation.3 | async-start | bytes 2097152 | tf_op jit(solution)/shard_map/psum | solution.py:301
  10.0 745.1 %copy-start.11 = (bf16[1,512,64]{2,1,0:T(8,128)(2,1)}, bf16[1,512,64]{2,1,0:T(8,128)(2,1)S(1)}, u32[]{:S(2)}) copy-start(bf16[1,512,64]{2,1,0:T(8,128)(2,1)S(1)} %copy.273) | copy-start | bytes 196612
  12.4 270.1 %collective-permute-start = (bf16[64,67]{1,0:T(8,128)(2,1)S(1)}, bf16[64,67]{1,0:T(8,128)(2,1)S(1)}, u32[]{:S(2)}, u32[]{:S(2)}) collective-permute-start(bf16[64,67]{1,0:T(8,128)(2,1)S(1)} %get-tuple-element.1329), channel_id=1, source_target_pairs={{0,2},{2,4},{4,6},{6,8},{8,10},{10,12},{12,14},{14,16},{16,18},{18... | collective-permute-start | bytes 25736 | tf_op jit(solution)/shard_map/ppermute | solution.py:26
  16.9 265.6 %collective-permute-start.1 = (bf16[64,67]{1,0:T(8,128)(2,1)S(1)}, bf16[64,67]{1,0:T(8,128)(2,1)S(1)}, u32[]{:S(2)}, u32[]{:S(2)}) collective-permute-start(bf16[64,67]{1,0:T(8,128)(2,1)S(1)} %get-tuple-element.1330), channel_id=1, source_target_pairs={{2,0},{4,2},{6,4},{8,6},{10,8},{12,10},{14,12},{16,14},{18,16},{20... | collective-permute-start | bytes 25736 | tf_op jit(solution)/shard_map/ppermute | solution.py:28
  279.9 475.2 %copy-start.73 = (f32[1,512]{1,0:T(1,128)}, f32[1,512]{1,0:T(1,128)S(1)}, u32[]{:S(2)}) copy-start(f32[1,512]{1,0:T(1,128)S(1)} %get-tuple-element.1333) | copy-start | bytes 6148
  280.0 916.2 %copy-start.46 = (f32[2048]{0:T(1024)}, f32[2048]{0:T(1024)S(1)}, u32[]{:S(2)}) copy-start(f32[2048]{0:T(1024)S(1)} %broadcast_maximum_fusion) | copy-start | bytes 24580
  317.3 441.7 %copy-start.82 = (bf16[1,512,3]{1,2,0:T(4,128)(2,1)S(1)}, bf16[1,512,3]{1,2,0:T(4,128)(2,1)}, u32[]{:S(2)}) copy-start(bf16[1,512,3]{1,2,0:T(4,128)(2,1)} %param.46) | copy-start | bytes 9220
  317.3 442.3 %copy-start.86 = (bf16[1,128,3]{1,2,0:T(4,128)(2,1)S(1)}, bf16[1,128,3]{1,2,0:T(4,128)(2,1)}, u32[]{:S(2)}) copy-start(bf16[1,128,3]{1,2,0:T(4,128)(2,1)} %constant_dynamic-slice_fusion.14) | copy-start | bytes 2308
  317.3 442.4 %copy-start.89 = (s32[128]{0:T(128)S(1)}, s32[128]{0:T(128)}, u32[]{:S(2)}) copy-start(s32[128]{0:T(128)} %get-tuple-element.1338) | copy-start | bytes 1540
  758.7 691.6 %all-reduce.9.cloned.1.call-start = ((), (), s32[]{:S(2)}) async-start(), calls=%async_computation.4 | async-start | bytes 524288 | tf_op jit(solution)/shard_map/psum | solution.py:348
  866.5 211.7 %copy-start.83 = (f32[128]{0:T(128)S(1)}, f32[128]{0:T(128)}, u32[]{:S(2)}) copy-start(f32[128]{0:T(128)} %get-tuple-element.1337) | copy-start | bytes 1540
  1204.4 5.4 collective-permute-start.2
  1207.8 4.9 collective-permute-start.3
  1363.9 665.4 %all-reduce.11.cloned.1.call-start = ((), (), s32[]{:S(2)}) async-start(), calls=%async_computation.5 | async-start | bytes 2097152 | tf_op jit(solution)/shard_map/psum | solution.py:348
  1461.7 475.1 %copy-start.69 = (s32[16,32]{1,0:T(8,128)S(1)}, s32[16,32]{1,0:T(8,128)}, u32[]{:S(2)}) copy-start(s32[16,32]{1,0:T(8,128)} %copy-done.68) | copy-start | bytes 6148
  1461.7 567.6 %copy-start.47 = (f32[2048]{0:T(1024)S(1)}, f32[2048]{0:T(1024)}, u32[]{:S(2)}) copy-start(f32[2048]{0:T(1024)} %copy-done.46) | copy-start | bytes 24580
  1913.0 118.2 %copy-start.77 = (s32[1024]{0:T(1024)S(1)}, s32[1024]{0:T(1024)}, u32[]{:S(2)}) copy-start(s32[1024]{0:T(1024)} %pad_clamp_fusion) | copy-start | bytes 12292
  1913.0 119.8 %copy-start.12 = (bf16[1,512,64]{2,1,0:T(8,128)(2,1)S(1)}, bf16[1,512,64]{2,1,0:T(8,128)(2,1)}, u32[]{:S(2)}) copy-start(bf16[1,512,64]{2,1,0:T(8,128)(2,1)} %copy-done.11) | copy-start | bytes 196612
  1936.7 1229.2 %reduce-scatter.5.cloned.1.call-start = ((), (), s32[]{:S(2)}) async-start(), calls=%async_computation.6 | async-start | bytes 811008 | tf_op jit(solution)/shard_map/reduce_scatter | solution.py:394
  3033.7 402.5 %reduce-scatter.7.cloned.1.call-start = ((), (), s32[]{:S(2)}) async-start(), calls=%async_computation.7 | async-start | bytes 12976128 | tf_op jit(solution)/shard_map/reduce_scatter | solution.py:400
  3044.9 121.0 %copy-start.59 = (f32[3,8,256]{2,1,0:T(8,128)S(1)}, f32[3,8,256]{2,1,0:T(8,128)}, u32[]{:S(2)}) copy-start(f32[3,8,256]{2,1,0:T(8,128)} %param.58) | copy-start | bytes 73732
  3044.9 121.0 %copy-start.70 = (f32[3,8,256]{2,1,0:T(8,128)S(1)}, f32[3,8,256]{2,1,0:T(8,128)}, u32[]{:S(2)}) copy-start(f32[3,8,256]{2,1,0:T(8,128)} %param.62) | copy-start | bytes 73732
  3045.0 121.0 %copy-start.71 = (f32[3,8,256]{2,1,0:T(8,128)S(1)}, f32[3,8,256]{2,1,0:T(8,128)}, u32[]{:S(2)}) copy-start(f32[3,8,256]{2,1,0:T(8,128)} %param.66) | copy-start | bytes 73732
  3045.0 391.3 %copy-start.22 = (f32[3,8,4096]{2,1,0:T(8,128)S(1)}, f32[3,8,4096]{2,1,0:T(8,128)}, u32[]{:S(2)}) copy-start(f32[3,8,4096]{2,1,0:T(8,128)} %param.59) | copy-start | bytes 1179652
  3045.0 391.3 %copy-start.34 = (f32[3,8,4096]{2,1,0:T(8,128)S(1)}, f32[3,8,4096]{2,1,0:T(8,128)}, u32[]{:S(2)}) copy-start(f32[3,8,4096]{2,1,0:T(8,128)} %param.63) | copy-start | bytes 1179652
  3045.0 391.3 %copy-start.35 = (f32[3,8,4096]{2,1,0:T(8,128)S(1)}, f32[3,8,4096]{2,1,0:T(8,128)}, u32[]{:S(2)}) copy-start(f32[3,8,4096]{2,1,0:T(8,128)} %param.67) | copy-start | bytes 1179652
  3091.2 48.3 %collective-permute-start.4 = (f32[64,64]{1,0:T(8,128)S(1)}, f32[64,64]{1,0:T(8,128)S(1)}, u32[]{:S(2)}, u32[]{:S(2)}) collective-permute-start(f32[64,64]{1,0:T(8,128)S(1)} %get-tuple-element.1319), channel_id=1, source_target_pairs={{0,2},{2,4},{4,6},{6,8},{8,10},{10,12},{12,14},{14,16},{16,18},{18... | collective-permute-start | bytes 49160 | tf_op jit(solution)/shard_map/ppermute | solution.py:26
  3095.2 44.2 %collective-permute-start.5 = (f32[64,64]{1,0:T(8,128)S(1)}, f32[64,64]{1,0:T(8,128)S(1)}, u32[]{:S(2)}, u32[]{:S(2)}) collective-permute-start(f32[64,64]{1,0:T(8,128)S(1)} %get-tuple-element.1320), channel_id=1, source_target_pairs={{2,0},{4,2},{6,4},{8,6},{10,8},{12,10},{14,12},{16,14},{18,16},{20... | collective-permute-start | bytes 49160 | tf_op jit(solution)/shard_map/ppermute | solution.py:28
  (202 other events, 2600.3 us)
Sparse Core Ops, SparseCore 0:
  11.7 72.8 all-gather.1
  758.9 90.9 all-reduce.6
  1364.0 86.2 all-reduce.8
  1936.8 92.3 all-reduce.10
  3033.8 132.0 reduce-scatter.4
  3168.2 268.0 reduce-scatter.6
where the time goes:
time: 3480 us; the launch traced here: 3450 us
  local copies, waits for them, and re-layouts  1210 us (35%)
  matrix products  931 us (27%)
  waiting for transfers between devices  546 us (16%)
  other arithmetic  388 us (11%)
  blocking collectives  333 us (10%)
    reshape x26, local copies, waits for them, and re-layouts, block_grad(): kernel = kernel.reshape(edge_rows, slot_count, feat_width, feat_width)  327 us
    reshape x26, local copies, waits for them, and re-layouts, block_sum(): kernel.reshape(part_dst.shape[0], slot_count, feat_width, feat_width)  327 us
    convert_element_type x26, local copies, waits for them, and re-layouts, block_grad(): grad_kernel.reshape(edge_rows, slot_count, feat_width * feat_width)  313 us
    reduce_scatter x1, waiting for transfers between devices, per_device(): lax.psum_scatter(jnp.stack([sums_fine[3], sums_mid[3], sums_coarse[3]]),...  269 us
    dot_general x26, matrix products, block_grad(): jnp.einsum('bkj,bkq->jq', act_two, grad_kernel, preferred_element_type=jn...  203 us
    dot_general x26, matrix products, block_sum(): jnp.einsum('bkoc,bkc->bko', kernel, part_sources, preferred_element_type=...  202 us
    convert_element_type x26, other arithmetic, block_grad(): grad_kernel.reshape(edge_rows, slot_count, feat_width * feat_width)  193 us
    dot_general x52, matrix products, kernel_forward(): jnp.einsum('bkj,jq->bkq', act_two, w_third, preferred_element_type=jnp.fl...  192 us
  transfers between devices with their start and end apart: 12, of which 6 were waited for; matrix products, arithmetic and copies ran while one was open for 4% of the time, Pallas kernels for 0%

commit v1 on v0

v1 whole, which is shorter than its diff:
```python
import functools

import jax
import jax.numpy as jnp
from jax import lax
from jax.experimental import pallas as pl
from jax.experimental.pallas import tpu as pltpu
from jax.sharding import PartitionSpec as P

STEP = 5
B_ONE = 0.9
B_TWO = 0.95
EPSILON = 1e-08
WEIGHT_DECAY = 0.1
RATE_FIRST = 0.4
RATE_MAIN = 0.02

BF = jnp.bfloat16
F32 = jnp.float32
I32 = jnp.int32
MESH = pl.DeviceIdType.MESH
NN = ((1,), (0,))
NT = ((1,), (1,))
TN = ((0,), (0,))
LANES = 512
GROUP = 16


def dot(a, b, dims=NN):
    return lax.dot_general(a, b, (dims, ((), ())), preferred_element_type=F32)


def sig(v):
    return 0.5 + 0.5 * jnp.tanh(0.5 * v)


def split3(v):
    high = v.astype(BF)
    rest = v - high.astype(F32)
    mid = rest.astype(BF)
    low = (rest - mid.astype(F32)).astype(BF)
    return jnp.concatenate([high, mid, low], axis=0)


def join3(v):
    n = v.shape[0] // 3
    return v[:n] + v[n : 2 * n] + v[2 * n :]


def iota(shape, dim):
    return lax.broadcasted_iota(I32, shape, dim)


def group_mask(width):
    slots = width // GROUP
    return (iota((GROUP, width), 1) // slots == iota((GROUP, width), 0)).astype(F32)


def one_hot(row, start, rows):
    return (iota((rows, row.shape[1]), 0) + start == row).astype(F32).astype(BF)


def spread(x, mask):
    return (x[:, None, :] * mask[None]).reshape(x.shape[0] * GROUP, mask.shape[1]).astype(BF)


class Level:
    def __init__(self, index, nodes, slots, sources):
        self.index, self.nodes, self.slots, self.sources = index, nodes, slots, sources
        self.steps = nodes * slots // LANES
        self.width = GROUP * slots
        self.blocks = LANES // self.width
        self.chunk = sources if sources <= 1024 else 512


def make_kernel(T, NG, C, KW, fine, mid, coarse, halo, inside):
    H = T // 4
    NCH = T // 2 * NG
    A = KW // (32 * NG)
    NB = KW // 16
    HALF = C * C // 2
    QH = HALF // 2
    SMW = KW + 128
    levels = (fine, mid, coarse)
    NM, NC = mid.nodes, coarse.nodes

    def kernel(
        tab, cot, send, lkf, lkm, lkc, zdf, zdm, zdc, nf, nm, nc, pf, pw, gm, gc, wsm, wc,
        layer, gradf, gwc, gsmall,
        ext, extT, agbuf, wt, s0buf, smbuf, waT, wbT, wbr, bbc,
        mt0, mt1, mt2, xs0, xs1, xs2, zs0, zs1, zs2,
        ohp, tx_s, rx_s, tx_w, rx_w, tx_q, rx_q, tx_u, rx_u, tx_g, rx_g, tx_c, rx_c, tx_b, rx_b, tx_f, rx_f, tx_h, rx_h,
        x1T, x2b, acc0, acc1, acc2, acc1b, acc2b, rs1buf, rs2buf, v0s, gys,
        rsr0, rsr1, rsr2, rsr3, rsf, rsr4, gsb, rcA, rcB, sems,
    ):
        t = lax.axis_index("tile")
        g = lax.axis_index("grp")
        core = lax.rem(t, 2)
        r = t // 2
        lo = lax.rem(r, 2)
        hi = r // 2
        ch = r * NG + g
        ocore, olo, og = 1 - core, 1 - lo, 1 - g

        def tile_of(hi_, lo_, core_):
            return (hi_ * 2 + lo_) * 2 + core_

        partner = {"tile": tile_of(hi, lo, ocore), "grp": g}
        xn = {"tile": tile_of(hi, olo, core), "grp": g}
        yn = {"tile": t, "grp": og}

        counter = [0]

        def sem_block(n):
            base = counter[0]
            counter[0] += n
            return base

        def copy(src, dst, ssem, rsem, dev):
            return pltpu.make_async_remote_copy(
                src_ref=src, dst_ref=dst, send_sem=sems.at[ssem], recv_sem=sems.at[rsem],
                device_id=dev, device_id_type=MESH,
            )

        local = sem_block(1)

        def own_copy(src, dst):
            c = pltpu.make_async_copy(src, dst, sems.at[local])
            c.start()
            c.wait()

        class One:
            def __init__(self, src, dst, dev):
                self.s, self.r = sem_block(1), sem_block(1)
                self.d = None
                self.parts = (src, dst, self.s, self.r, dev)

            def start(self):
                self.d = copy(*self.parts)
                self.d.start()

            def recv(self):
                self.d.wait_recv()

            def sent(self):
                self.d.wait_send()

        class Ring:
            def __init__(self, n, src, dst, dev):
                self.n, self.src, self.dst, self.dev = n, src, dst, dev
                self.s, self.r = sem_block(n - 1), sem_block(n - 1)

            def each(self, f):
                def body(i, _):
                    d = i + 1
                    f(copy(self.src(d), self.dst(d), self.s + i, self.r + i, self.dev(d)))
                    return 0

                lax.fori_loop(0, self.n - 1, body, 0)

            def start(self):
                self.each(lambda c: c.start())

            def recv(self):
                self.each(lambda c: c.wait_recv())

            def sent(self):
                self.each(lambda c: c.wait_send())

        class Sides:
            def __init__(self, src_left, src_right, rx):
                self.ls, self.lr, self.rs, self.rr = (sem_block(1) for _ in range(4))
                self.rx = rx
                self.to_left = copy(src_left, rx.at[1], self.ls, self.lr, {"tile": t - 1, "grp": g})
                self.to_right = copy(src_right, rx.at[0], self.rs, self.rr, {"tile": t + 1, "grp": g})

            def start(self):
                @pl.when(t > 0)
                def _():
                    self.to_left.start()

                @pl.when(t < T - 1)
                def _():
                    self.to_right.start()

                @pl.when(t == 0)
                def _():
                    self.rx[0] = jnp.zeros(self.rx.shape[1:], self.rx.dtype)

                @pl.when(t == T - 1)
                def _():
                    self.rx[1] = jnp.zeros(self.rx.shape[1:], self.rx.dtype)

            def recv(self):
                @pl.when(t < T - 1)
                def _():
                    self.to_left.wait_recv()

                @pl.when(t > 0)
                def _():
                    self.to_right.wait_recv()

            def sent(self):
                @pl.when(t > 0)
                def _():
                    self.to_left.wait_send()

                @pl.when(t < T - 1)
                def _():
                    self.to_right.wait_send()

        pending = []

        def started(c):
            c.start()
            pending.append(c)
            return c

        barrier = pltpu.get_barrier_semaphore()
        total = T * NG
        me = t * NG + g

        def greet(i, _):
            other = lax.rem(me + i + 1, total)
            pl.semaphore_signal(
                barrier, inc=1, device_id={"tile": other // NG, "grp": lax.rem(other, NG)}, device_id_type=MESH
            )
            return 0

        lax.fori_loop(0, total - 1, greet, 0)

        ohs = one_hot(send[...], 0, fine.nodes)
        sent_rows = dot(ohs, tab[...], TN).astype(BF)
        ext[0 : fine.nodes] = tab[...]
        tx_s[...] = sent_rows
        ohp[...] = one_hot(pf[...], 0, 2 * NM)
        if inside:
            smbuf[:, ch, core] = wsm[...]
        else:
            smbuf[...] = wsm[...].reshape(smbuf.shape)
            own_copy(wc, agbuf)
        pl.semaphore_wait(barrier, total - 1)

        def chip_dev(d):
            o = lax.rem(ch + d, NCH)
            return {"tile": (o // NG) * 2 + core, "grp": lax.rem(o, NG)}

        if inside:
            sm_a0 = started(Ring(NCH, lambda d: smbuf.at[0, ch, core], lambda d: smbuf.at[0, ch, core], chip_dev))
        halo_x = started(Sides(tx_s.at[0:halo], tx_s.at[halo : 2 * halo], rx_s))
        if inside:
            s0c = [started(One(wc.at[l, ocore], s0buf.at[l], partner)) for l in range(3)]
            sm_a12 = started(Ring(NCH, lambda d: smbuf.at[1:3, ch, core], lambda d: smbuf.at[1:3, ch, core], chip_dev))

        ag = [[] for _ in range(3)]

        def ag_s1(l):
            if not inside:
                return
            s0c[l].recv()
            mine, theirs = wc[l, core], s0buf[l]
            first = core == 0
            agbuf[l, core, hi, lo, g] = jnp.concatenate(
                [jnp.where(first, mine, theirs), jnp.where(first, theirs, mine)], axis=0
            ).astype(BF)
            c = Ring(
                H,
                lambda d: agbuf.at[l, core, hi, lo, g],
                lambda d: agbuf.at[l, core, hi, lo, g],
                lambda d: {"tile": tile_of(lax.rem(hi + d, H), lo, core), "grp": g},
            )
            c.start()
            ag[l].append([c])

        def ag_next(l, *copies):
            if not inside:
                return
            for c in ag[l][-1]:
                c.recv()
            for c in copies:
                c.start()
            ag[l].append(copies)

        def ag_s2(l):
            part = agbuf.at[l, core, :, lo, g]
            ag_next(l, One(part, part, xn), One(part, part, yn))

        def ag_s3(l):
            a = agbuf.at[l, core, :, olo, g, :, 0:QH]
            b = agbuf.at[l, core, :, lo, og, :, QH:HALF]
            ag_next(l, One(a, a, yn), One(b, b, xn))

        def ag_s4(l):
            part = agbuf.at[l, core]
            ag_next(l, One(part, part, partner))

        def ag_fin(l):
            if inside:
                for c in ag[l][-1]:
                    c.recv()
                for cs in ag[l]:
                    for c in cs:
                        c.sent()
            n = HALF // 128

            def body(i, _):
                half, k = i // n, lax.rem(i, n)
                block = agbuf[l, half, :, :, :, :, pl.ds(pl.multiple_of(k * 128, 128), 128)].reshape(KW, 128)
                wt[l, pl.ds(i * 2, 2)] = block.T.reshape(2, C, KW)
                return 0

            lax.fori_loop(0, 2 * n, body, 0)

        def unpack_small(l):
            block = smbuf[l].reshape(KW, SMW)
            second = block[:, 0:KW]
            wbr[l] = second.astype(BF)
            wbT[l] = second.T.astype(BF)
            waT[l] = block[:, KW : KW + 8].astype(BF)
            bbc[l] = jnp.broadcast_to(block[:, KW + 8 : KW + 9], (KW, 128))

        lks, zds, mts, xss, zss = (lkf, lkm, lkc), (zdf, zdm, zdc), (mt0, mt1, mt2), (xs0, xs1, xs2), (zs0, zs1, zs2)

        def pair(ref, lv, i):
            if lv.blocks == 1:
                return ref[i]
            return jnp.concatenate([ref[lv.blocks * i + k] for k in range(lv.blocks)], axis=1)

        def take(table, row, lv):
            rows = lv.chunk
            if lv.sources == rows:
                return dot(table[...], one_hot(row, 0, rows))
            n = lv.sources // rows

            def body(k, acc):
                start = pl.multiple_of(k * rows, rows)
                return acc + dot(table[:, pl.ds(start, rows)], one_hot(row, start, rows))

            return lax.fori_loop(0, n, body, jnp.zeros((table.shape[0], LANES), F32))

        def put(acc, values, row, lv):
            rows = lv.chunk
            if lv.sources == rows:
                acc[...] += dot(values, one_hot(row, 0, rows), NT)
                return
            n = lv.sources // rows

            def body(k, _):
                start = pl.multiple_of(k * rows, rows)
                at = pl.ds(start, rows)
                acc[:, at] += dot(values, one_hot(row, start, rows), NT)
                return 0

            lax.fori_loop(0, n, body, 0)

        def edges_forward(lv, x_table, g_table, first, last):
            l = lv.index
            mask = group_mask(lv.width)

            def body(i, _):
                row = pair(lks[l], lv, i)
                if g_table is None:
                    got = take(x_table, row, lv)
                    x, z = got[0:C], got[C : C + 8] + pair(zds[l], lv, i)
                else:
                    x = take(x_table, row, lv)
                    z = take(g_table, row, lv)[0:8] + pair(zds[l], lv, i)
                xss[l][i] = x.astype(BF)
                zss[l][i] = z
                t1 = dot(waT[l], z.astype(BF))
                a1 = (t1 * sig(t1)).astype(BF)
                t2 = dot(wbT[l], a1) + bbc[l][:, 0:1]
                a2 = (t2 * sig(t2)).astype(BF)
                for k in range(lv.blocks):
                    sl = slice(lv.width * k, lv.width * (k + 1))
                    m = dot(spread(x[:, sl], mask), a2[:, sl], NT)
                    at = pl.ds(pl.multiple_of((lv.blocks * i + k) * GROUP, GROUP), GROUP)
                    mts[l][:, at, :] = m.astype(BF).reshape(C, GROUP, KW)
                return 0

            lax.fori_loop(first, last, body, 0)

        def node_sums(lv):
            l = lv.index

            def body(i, acc):
                for u in range(4):
                    acc = acc + dot(wt[l, 4 * i + u], mts[l][4 * i + u], NT)
                return acc

            return lax.fori_loop(0, C // 4, body, jnp.zeros((C, lv.nodes), F32))

        def third_grad(lv, gsT):
            l = lv.index
            n = C // 4

            def body(i, _):
                both = jnp.concatenate([dot(gsT, mts[l][2 * i]), dot(gsT, mts[l][2 * i + 1])], axis=0)
                out = both.T.astype(BF).reshape(A, 2, NG, 16, 128)
                agbuf[l, i // n, :, :, :, :, pl.ds(pl.multiple_of(lax.rem(i, n) * 128, 128), 128)] = out
                return 0

            lax.fori_loop(0, C // 2, body, 0)

        def node_weights(lv, gs):
            l = lv.index

            def body(c, _):
                mts[l][c] = dot(gs, wt[l, c]).astype(BF)
                return 0

            lax.fori_loop(0, C, body, 0)

        def edges_backward(lv, acc, first, last):
            l = lv.index
            mask = group_mask(lv.width)
            fold = (iota((C, C * GROUP), 1) // GROUP == iota((C, C * GROUP), 0)).astype(F32).astype(BF)

            def body(i, _):
                zb = zss[l][i].astype(BF)
                t1 = dot(waT[l], zb)
                s1 = sig(t1)
                f1 = t1 * s1
                d1 = s1 + f1 * (1.0 - s1)
                a1 = f1.astype(BF)
                t2 = dot(wbT[l], a1) + bbc[l][:, 0:1]
                s2 = sig(t2)
                f2 = t2 * s2
                d2 = s2 + f2 * (1.0 - s2)
                a2 = f2.astype(BF)
                x = xss[l][i].astype(F32)
                g2s, gxs = [], []
                for k in range(lv.blocks):
                    sl = slice(lv.width * k, lv.width * (k + 1))
                    at = pl.ds(pl.multiple_of((lv.blocks * i + k) * GROUP, GROUP), GROUP)
                    q = mts[l][:, at, :].reshape(C * GROUP, KW)
                    g2s.append((dot(q, spread(x[:, sl], mask), TN) * d2[:, sl]).astype(BF))
                    every = dot(q, a2[:, sl])
                    own = (every.reshape(C, GROUP, lv.width) * mask[None]).reshape(C * GROUP, lv.width).astype(BF)
                    gxs.append(dot(fold, own).astype(BF))
                g2 = jnp.concatenate(g2s, axis=1)
                gx = jnp.concatenate(gxs, axis=1)
                g1 = (dot(wbr[l], g2) * d1).astype(BF)
                sm2 = dot(a1, g2, NT)
                p1 = dot(g1, zb, NT)
                p2 = dot(g2, zb, NT)
                gsb[l, :, :, :, 0:KW] += sm2.reshape(NB, 2, 8, KW)
                gsb[l, :, :, :, KW : KW + 8] += p1.reshape(NB, 2, 8, 8)
                gsb[l, :, :, :, KW + 8 : KW + 16] += p2.reshape(NB, 2, 8, 8)
                put(acc, gx, pair(lks[l], lv, i), lv)
                return 0

            lax.fori_loop(first, last, body, 0)

        def roll_pick(left, right, n_left, left_lane, right_lane):
            lane = iota((1, 128), 1)
            a = pltpu.roll(left, (left_lane - (n_left - 8)) % 128, 1)
            b = pltpu.roll(right, right_lane % 128, 1)
            return jnp.where((lane >= left_lane) & (lane < left_lane + 8), a, 0.0) + jnp.where(
                (lane >= right_lane) & (lane < right_lane + 8), b, 0.0
            )

        def margin_pick(from_left, from_right, n_own, left_at, right_at):
            lane = iota((1, 128), 1)
            a = pltpu.roll(from_left, (0 - right_at) % 128, 1)
            b = pltpu.roll(from_right, (n_own - 8 - left_at) % 128, 1)
            return jnp.where(lane < 8, a, 0.0) + jnp.where((lane >= n_own - 8) & (lane < n_own), b, 0.0)

        ag_s1(0)
        halo_x.recv()
        ext[fine.nodes : fine.nodes + halo] = rx_s[0]
        ext[fine.nodes + halo :] = rx_s[1]
        extT[...] = ext[...].T[0:80]
        ag_s1(1)
        ag_s1(2)
        if inside:
            sm_a0.recv()
            sm_b0 = started(One(smbuf.at[0, :, core], smbuf.at[0, :, core], partner))
            ag_s2(0)
            sm_a12.recv()
            sm_b12 = started(One(smbuf.at[1:3, :, core], smbuf.at[1:3, :, core], partner))
            sm_b0.recv()
        unpack_small(0)
        quarter = fine.steps // 4
        edges_forward(fine, extT, None, 0, quarter)
        ag_s3(0)
        ag_s2(1)
        edges_forward(fine, extT, None, quarter, 2 * quarter)
        ag_s4(0)
        ag_s3(1)
        ag_s2(2)
        edges_forward(fine, extT, None, 2 * quarter, 3 * quarter)
        ag_s4(1)
        ag_s3(2)
        edges_forward(fine, extT, None, 3 * quarter, fine.steps)
        ag_s4(2)
        ag_fin(0)
        v0 = extT[0:C, 0 : fine.nodes].astype(F32) + node_sums(fine) / nf[...]
        v0s[...] = v0

        ones8 = jnp.ones((8, fine.nodes), BF)
        part = dot(jnp.concatenate([split3(v0), ones8], axis=0), ohp[...], NT)
        sums = jnp.concatenate([join3(part[0 : 3 * C]), part[3 * C :]], axis=0)
        tx_w[0] = sums[:, NM:]
        ex_w = started(Sides(tx_w.at[0], tx_w.at[0], rx_w))
        if inside:
            sm_b12.recv()
        unpack_small(1)
        ag_fin(1)
        ex_w.recv()
        own = sums[:, 0:NM] + margin_pick(rx_w[0], rx_w[1], NM, 0, 8)
        inv1 = 1.0 / jnp.maximum(own[C : C + 1], 1.0)
        v1 = own[0:C] / jnp.maximum(own[C : C + 1], 1.0)
        x1T[:, pl.ds(pl.multiple_of(t * NM, NM), NM)] = v1.astype(BF)

        def tile_dev(d):
            return {"tile": lax.rem(t + d, T), "grp": g}

        x1own = x1T.at[:, pl.ds(pl.multiple_of(t * NM, NM), NM)]
        ag1 = started(Ring(T, lambda d: x1own, lambda d: x1own, tile_dev))
        unpack_small(2)
        ag_fin(2)
        ag1.recv()

        edges_forward(mid, x1T, gm, 0, mid.steps)
        w1 = v1 + node_sums(mid) / nm[...]
        tx_q[0, 0:C] = w1
        ohq = one_hot(pw[...], 0, 128)
        part = dot(jnp.concatenate([split3(w1), jnp.ones((8, NM), BF)], axis=0), ohq[:, 0:NM], NT)
        tx_q[0, C : 2 * C + 8] = jnp.concatenate([join3(part[0 : 3 * C]), part[3 * C :]], axis=0)
        ex_q = started(Sides(tx_q.at[0], tx_q.at[0], rx_q))
        ex_q.recv()
        own = tx_q[0, C : 2 * C + 8] + margin_pick(rx_q[0, C : 2 * C + 8], rx_q[1, C : 2 * C + 8], NC, NC, NC + 8)
        w1m = roll_pick(rx_q[0, 0:C], rx_q[1, 0:C], NM, 0, 8)
        w1win = jnp.concatenate([w1, w1m], axis=1)
        lane = iota((1, 128), 1)
        mine = lane < NC
        cnt2 = jnp.maximum(own[C : C + 1], 1.0)
        v2 = jnp.where(mine, own[0:C] / cnt2, 0.0)

        x2b[t] = v2.astype(BF)
        ag2 = started(Ring(T, lambda d: x2b.at[t], lambda d: x2b.at[t], tile_dev))
        ag2.recv()
        per = 128 // NC
        cols = []
        for k in range(coarse.sources // 128):
            block = x2b[per * k].astype(F32)
            for u in range(1, per):
                block = block + pltpu.roll(x2b[per * k + u].astype(F32), NC * u, 1)
            cols.append(block.astype(BF))
        for k, block in enumerate(cols):
            acc2[:, 128 * k : 128 * k + 128] = block.astype(F32)
        x2T = acc2[...].astype(BF)
        acc2b[0:C] = x2T
        edges_forward(coarse, acc2b.at[0:C], gc, 0, coarse.steps)
        sc = node_sums(coarse)
        sc = jnp.concatenate([sc, jnp.zeros((C, 128 - NC), F32)], axis=1)
        w2 = v2 + jnp.where(mine, sc / nc[...], 0.0)
        tx_u[0] = w2
        ex_u = started(Sides(tx_u.at[0], tx_u.at[0], rx_u))
        ex_u.recv()
        w2win = w2 + roll_pick(rx_u[0], rx_u[1], NC, NC, NC + 8)

        y1win = w1win + join3(dot(split3(w2win), ohq))
        y0 = v0s[...] + join3(dot(split3(y1win), ohp[...]))
        s0 = sig(y0)
        f0 = y0 * s0
        layer[...] = f0.T.astype(BF)
        gy0 = cot[...].T * (s0 + f0 * (1.0 - s0))
        gys[...] = gy0
        gy1p = join3(dot(split3(gy0), ohp[...], NT))
        gw2p = join3(dot(split3(gy1p), ohq, NT))
        tx_g[0, 0:C] = gy1p[:, NM:]
        tx_g[0, C : 2 * C] = gw2p
        ex_g = started(Sides(tx_g.at[0], tx_g.at[0], rx_g))
        ex_g.recv()
        gy1 = gy1p[:, 0:NM] + margin_pick(rx_g[0, 0:C], rx_g[1, 0:C], NM, 0, 8)
        gw2 = jnp.where(mine, gw2p + margin_pick(rx_g[0, C:], rx_g[1, C:], NC, NC, NC + 8), 0.0)

        rs = [[] for _ in range(3)]

        def rs_step(l, fix, *copies):
            if not inside:
                return
            if rs[l]:
                for c in rs[l][-1]:
                    c.recv()
            fix()
            for c in copies:
                c.start()
            rs[l].append(copies)
            pending.extend(copies)

        def rs_s0(l):
            rs_step(l, lambda: None, One(agbuf.at[l, ocore], rsr0.at[l], partner))

        def rs_s1(l):
            def fix():
                def body(i, _):
                    both = agbuf[l, core, i].astype(F32) + rsr0[l, i].astype(F32)
                    agbuf[l, core, i] = both.astype(BF)
                    return 0

                lax.fori_loop(0, H, body, 0)

            rs_step(
                l, fix,
                One(agbuf.at[l, core, :, olo, og, :, 0:QH], rsr1.at[l, 0], xn),
                One(agbuf.at[l, core, :, olo, og, :, QH:HALF], rsr1.at[l, 1], yn),
            )

        def rs_s2(l):
            def fix():
                def body(i, _):
                    a = agbuf[l, core, i, lo, og, :, 0:QH].astype(F32) + rsr1[l, 0, i].astype(F32)
                    agbuf[l, core, i, lo, og, :, 0:QH] = a.astype(BF)
                    b = agbuf[l, core, i, olo, g, :, QH:HALF].astype(F32) + rsr1[l, 1, i].astype(F32)
                    agbuf[l, core, i, olo, g, :, QH:HALF] = b.astype(BF)
                    return 0

                lax.fori_loop(0, H, body, 0)

            rs_step(
                l, fix,
                One(agbuf.at[l, core, :, lo, og], rsr2.at[l, 0], yn),
                One(agbuf.at[l, core, :, olo, g], rsr2.at[l, 1], xn),
            )

        def rs_s3(l):
            def fix():
                def body(i, _):
                    a = agbuf[l, core, i, lo, g].astype(F32) + rsr2[l, 0, i].astype(F32) + rsr2[l, 1, i].astype(F32)
                    agbuf[l, core, i, lo, g] = a.astype(BF)
                    return 0

                lax.fori_loop(0, H, body, 0)

            rs_step(
                l, fix,
                Ring(
                    H,
                    lambda d: agbuf.at[l, core, lax.rem(hi + d, H), lo, g],
                    lambda d: rsr3.at[l, d - 1],
                    lambda d: {"tile": tile_of(lax.rem(hi + d, H), lo, core), "grp": g},
                ),
            )

        def rs_s4(l):
            def fix():
                tot = agbuf[l, core, hi, lo, g].astype(F32)
                for k in range(H - 1):
                    tot = tot + rsr3[l, k].astype(F32)
                rsf[l, 0] = tot[0:8]
                rsf[l, 1] = tot[8:16]

            rs_step(l, fix, One(rsf.at[l, ocore], rsr4.at[l], partner))

        def rs_s5(l):
            if not inside:
                own_copy(agbuf.at[l], gwc.at[l])
                return
            for c in rs[l][-1]:
                c.recv()
            gwc[l, core] = rsf[l, core]
            gwc[l, ocore] = rsr4[l]

        gsb[...] = jnp.zeros(gsb.shape, F32)

        gs2T = jnp.where(mine, gw2 / nc[...], 0.0).astype(BF)
        third_grad(coarse, gs2T[:, 0:NC])
        rs_s0(2)
        node_weights(coarse, gs2T.astype(F32).T[0:NC].astype(BF))
        acc2[...] = jnp.zeros(acc2.shape, F32)
        edges_backward(coarse, acc2, 0, coarse.steps)
        a2rows = jnp.concatenate([acc2[...], jnp.zeros(acc2.shape, F32)], axis=0)
        tx_c[...] = a2rows.T.astype(BF)
        ag_r2 = started(
            Ring(
                T,
                lambda d: tx_c.at[pl.ds(pl.multiple_of(lax.rem(t + d, T) * NC, NC), NC)],
                lambda d: rs2buf.at[d - 1],
                tile_dev,
            )
        )
        rs_s1(2)
        ag_r2.recv()

        def add2(k, acc):
            return acc + rs2buf[k].astype(F32)

        own2 = lax.fori_loop(
            0, T - 1, add2, tx_c[pl.ds(pl.multiple_of(t * NC, NC), NC)].astype(F32)
        )
        own2 = jnp.concatenate([own2, jnp.zeros((128 - NC, 128), F32)], axis=0).T[0:C]
        gv2 = jnp.where(mine, (gw2 + own2) / cnt2, 0.0)
        tx_b[0, 0:C] = gv2
        ex_b = started(Sides(tx_b.at[0, 0:C], tx_b.at[0, 0:C], rx_b))
        rs_s2(2)
        ex_b.recv()
        gv2win = gv2 + roll_pick(rx_b[0], rx_b[1], NC, NC, NC + 8)
        gw1 = gy1 + join3(dot(split3(gv2win), ohq[:, 0:NM]))

        gs1T = (gw1 / nm[...]).astype(BF)
        third_grad(mid, gs1T)
        rs_s0(1)
        rs_s3(2)
        node_weights(mid, gs1T.astype(F32).T.astype(BF))
        acc1[...] = jnp.zeros(acc1.shape, F32)
        edges_backward(mid, acc1, 0, mid.steps)
        acc1b[...] = acc1[...].astype(BF)
        ag_r1 = started(
            Ring(
                T,
                lambda d: acc1b.at[:, pl.ds(pl.multiple_of(lax.rem(t + d, T) * NM, NM), NM)],
                lambda d: rs1buf.at[d - 1],
                tile_dev,
            )
        )
        rs_s1(1)
        rs_s4(2)
        ag_r1.recv()

        def add1(k, acc):
            return acc + rs1buf[k].astype(F32)

        own1 = lax.fori_loop(0, T - 1, add1, acc1[:, pl.ds(pl.multiple_of(t * NM, NM), NM)])
        gv1 = (gw1 + own1) * inv1
        tx_f[0] = gv1
        ex_f = started(Sides(tx_f.at[0], tx_f.at[0], rx_f))
        rs_s2(1)
        rs_s5(2)
        ex_f.recv()
        gv1win = jnp.concatenate([gv1, roll_pick(rx_f[0], rx_f[1], NM, 0, 8)], axis=1)
        gv0 = gys[...] + join3(dot(split3(gv1win), ohp[...]))
        gys[...] = gv0

        gs0 = gv0 / nf[...]
        gs0T = gs0.astype(BF)
        third_grad(fine, gs0T)
        rs_s0(0)
        rs_s3(1)
        node_weights(fine, gs0T.astype(F32).T.astype(BF))
        acc0[...] = jnp.zeros(acc0.shape, F32)
        rs_s1(0)
        rs_s4(1)
        edges_backward(fine, acc0, 0, quarter)
        rs_s2(0)
        rs_s5(1)
        edges_backward(fine, acc0, quarter, 2 * quarter)
        rs_s3(0)
        edges_backward(fine, acc0, 2 * quarter, 3 * quarter)
        rs_s4(0)
        edges_backward(fine, acc0, 3 * quarter, fine.steps)
        tx_h[0] = acc0[:, fine.nodes : fine.nodes + 2 * halo]
        ex_h = started(Sides(tx_h.at[0], tx_h.at[0], rx_h))

        if inside:
            gs_a = started(One(gsb.at[:, :, ocore], rcA, partner))
        rs_s5(0)
        ex_h.recv()
        lane1 = iota((1, 128), 1)
        back = jnp.where(lane1 < halo, pltpu.roll(rx_h[0], halo, 1), pltpu.roll(rx_h[1], halo, 1))
        ohs2 = one_hot(send[...], 0, fine.nodes)
        gf = gys[...] + acc0[:, 0 : fine.nodes] + join3(dot(split3(back), ohs2, NT))
        gradf[...] = gf.T.astype(BF)
        if inside:
            gs_a.recv()
            for l in range(3):
                gsb[l, :, core] += rcA[l]
            gs_b = started(
                Ring(
                    NCH,
                    lambda d: gsb.at[:, lax.rem(ch + d, NCH), core],
                    lambda d: rcB.at[d - 1],
                    chip_dev,
                )
            )
            gs_b.recv()

            def add3(k, acc):
                return acc + rcB[k]

            gsmall[...] = lax.fori_loop(0, NCH - 1, add3, gsb[:, ch, core])
        else:
            gsmall[...] = gsb[...]

        for c in pending:
            c.sent()

    n_sems = (
        2 * (2 * (NCH - 1)) + 4 + 2 * 3 + 3 * (2 * (H - 1) + 4 + 4 + 2) + 4
        + 4 * 7 + 4 * (2 * (T - 1)) + 3 * (2 + 4 + 4 + 2 * (H - 1) + 2) + 2 + 2 * (NCH - 1) + 9
    )
    V = pltpu.VMEM
    ls = 3 if inside else 1
    nf, nm_, nc_ = fine.nodes, NM, NC
    scratch = [
        V((nf + 2 * halo, 128), BF), V((80, nf + 2 * halo), BF),
        V((3, 2, A, 2, NG, 16, HALF), BF), V((3, C, C, KW), BF), V((3, 8, HALF), F32),
        V((3, NB, 2, 8, SMW), F32), V((3, KW, 8), BF), V((3, KW, KW), BF), V((3, KW, KW), BF), V((3, KW, 128), F32),
        V((C, nf, KW), BF), V((C, nm_, KW), BF), V((C, nc_, KW), BF),
        V((fine.steps, C, LANES), BF), V((mid.steps, C, LANES), BF), V((coarse.steps, C, LANES), BF),
        V((fine.steps, 8, LANES), F32), V((mid.steps, 8, LANES), F32), V((coarse.steps, 8, LANES), F32),
        V((2 * NM, nf), BF),
        V((2 * halo, 128), BF), V((2, halo, 128), BF),
        V((1, C + 8, 128), F32), V((2, C + 8, 128), F32),
        V((1, 2 * C + 8, 128), F32), V((2, 2 * C + 8, 128), F32),
        V((1, C, 128), F32), V((2, C, 128), F32),
        V((1, 2 * C, 128), F32), V((2, 2 * C, 128), F32),
        V((coarse.sources, 128), BF), V((1, 8, 128), F32),
        V((1, C, 128), F32), V((2, C, 128), F32),
        V((1, C, 128), F32), V((2, C, 128), F32),
        V((1, C, 128), F32), V((2, C, 128), F32),
        V((C, mid.sources), BF), V((T, C, 128), BF),
        V((C, nf + 2 * halo), F32), V((C, mid.sources), F32), V((C, coarse.sources), F32),
        V((C, mid.sources), BF), V((C, coarse.sources), BF),
        V((T - 1, C, 128), BF), V((T, NC, 128), BF), V((C, nf), F32), V((C, nf), F32),
        V((ls, A, 2, NG, 16, HALF), BF), V((ls, 2, A, 16, QH), BF), V((ls, 2, A, 16, HALF), BF),
        V((ls, A - 1, 16, HALF), BF), V((ls, 2, 8, HALF), F32), V((ls, 8, HALF), F32),
        V((3, NB, 2, 8, SMW), F32), V((ls, NB, 8, SMW), F32), V((NB - 1, ls, 8, SMW), F32),
        pltpu.SemaphoreType.DMA((n_sems,)),
    ]
    return kernel, scratch


def adamw(master, moment, square, grad, learn_rate):
    moment_new = B_ONE * moment + (1.0 - B_ONE) * grad
    square_new = B_TWO * square + (1.0 - B_TWO) * grad * grad
    fix_one = 1.0 - B_ONE**STEP
    fix_two = 1.0 - B_TWO**STEP
    master_new = master - learn_rate * (
        moment_new / fix_one / (jnp.sqrt(square_new / fix_two) + EPSILON) + WEIGHT_DECAY * master
    )
    return (master_new, moment_new, square_new)


def per_device(
    T, NG,
    features, cotangent, geom_fine, geom_mid, geom_coarse, links_fine, slots_fine, send_lists, parent_fine,
    parent_mid, links_mid, slots_mid, links_coarse, slots_coarse, kernel_in, kernel_bias, kernel_mid, kernel_out,
    first_in, first_bias, first_mid, first_out, second_in, second_bias, second_mid, second_out,
):
    C = features.shape[2]
    KW = kernel_mid.shape[2]
    R = T // 2
    NM, NC = links_mid.shape[1], links_coarse.shape[1]
    halo = send_lists.shape[1] // 2
    nf = features.shape[1]
    fine = Level(0, nf, links_fine.shape[2], nf + 2 * halo)
    mid = Level(1, NM, links_mid.shape[2], geom_mid.shape[1])
    coarse = Level(2, NC, links_coarse.shape[2], geom_coarse.shape[1])
    t = lax.axis_index("tile")

    def edge_rows(links, slots, lv):
        used = lax.broadcasted_iota(I32, links.shape, 1) < slots[:, None]
        return jnp.where(used, links, -1).reshape(-1, 1, lv.width)

    def edge_geom(geom, lv):
        n = geom.shape[0]
        rows = jnp.concatenate(
            [jnp.zeros((n, 1), F32), geom.astype(F32), jnp.ones((n, 1), F32), jnp.zeros((n, 3), F32)], axis=1
        )
        rows = rows.reshape(n // GROUP, GROUP, 8).transpose(0, 2, 1)
        return jnp.broadcast_to(rows[..., None], rows.shape + (lv.slots,)).reshape(n // GROUP, 8, lv.width)

    def source_geom(geom):
        return jnp.pad(geom.T, ((5, 8), (0, 0)))

    tab = jnp.concatenate(
        [features[0], jnp.zeros((nf, 5), BF), geom_fine[0], jnp.zeros((nf, 128 - C - 8), BF)], axis=1
    )
    mid_start, coarse_start = t * NM, t * NC
    own_geom_mid = lax.dynamic_slice_in_dim(geom_mid[0], mid_start, NM, 0)
    own_geom_coarse = lax.dynamic_slice_in_dim(geom_coarse[0], coarse_start, NC, 0)

    def window(index, start, n, at):
        off = index - start
        return jnp.where(off < 0, off + at + 8, jnp.where(off >= n, off - n + at + 8, off))

    pf = window(parent_fine[0], mid_start, NM, NM)[None]
    padded = jnp.pad(parent_mid[0], (8, 8), constant_values=-(1 << 20))
    around = lax.dynamic_slice_in_dim(padded, mid_start, NM + 16, 0)
    around = jnp.concatenate([around[8 : 8 + NM], around[:8], around[8 + NM :]])
    pw = jnp.where(around < 0, -1, window(around, coarse_start, NC, NC))
    pw = jnp.pad(pw, (0, 2 * NM - pw.shape[0]), constant_values=-1)[None]
    row = lambda s, n: jnp.pad(s.astype(F32), (0, n - s.shape[0]), constant_values=1.0)[None]

    def columns(v):
        return v.reshape(v.shape[:-1] + (R, 2, NG, 8)).swapaxes(-3, -2).reshape(v.shape)

    turned = kernel_in.swapaxes(1, 2)
    biases = kernel_bias.swapaxes(1, 2)
    per = kernel_mid.shape[1]
    inside = per == 8
    zero = jnp.zeros((3, per, 1), F32)
    wsm = jnp.concatenate(
        [columns(kernel_mid) if inside else kernel_mid, zero, turned[..., 0:3], biases[..., 0:1], turned[..., 3:6], biases[..., 1:2],
         jnp.zeros((3, per, 119), F32)], axis=2
    )
    wc = kernel_out.reshape(3, per, C, C).transpose(0, 3, 2, 1).reshape(3, 2, C * C // 2, per).swapaxes(2, 3)
    everyone = ("tile", "grp")
    grid = (3, 2, KW // (32 * NG), 2, NG, 16, C * C // 2)
    if not inside:
        wsm = lax.all_gather(wsm, everyone, axis=1, tiled=True)
        wc = lax.all_gather(wc.astype(BF), everyone, axis=2, tiled=True).reshape(grid)

    kernel, scratch = make_kernel(T, NG, C, KW, fine, mid, coarse, halo, inside)
    S = jax.ShapeDtypeStruct
    vm = pl.BlockSpec(memory_space=pltpu.VMEM)
    far = pl.BlockSpec(memory_space=pl.ANY)
    operands = (
        tab, cotangent[0], send_lists,
        edge_rows(links_fine[0], slots_fine[0], fine), edge_rows(links_mid[0], slots_mid[0], mid),
        edge_rows(links_coarse[0], slots_coarse[0], coarse),
        edge_geom(geom_fine[0], fine), edge_geom(own_geom_mid, mid), edge_geom(own_geom_coarse, coarse),
        row(slots_fine[0], nf), row(slots_mid[0], NM), row(slots_coarse[0], 128),
        pf, pw, source_geom(geom_mid[0]), source_geom(geom_coarse[0]), wsm, wc,
    )
    layer, gradf, gwc, gsmall = pl.pallas_call(
        kernel,
        out_shape=(S((nf, C), BF), S((nf, C), BF), S((3, 2, 8, C * C // 2), F32) if inside else S(grid, BF),
                   S((3, 8, KW + 128) if inside else (3, KW // 16, 2, 8, KW + 128), F32)),
        in_specs=[vm] * (len(operands) - 1) + [vm if inside else far],
        out_specs=(vm, vm, vm if inside else far, vm),
        scratch_shapes=scratch,
        compiler_params=pltpu.CompilerParams(
            collective_id=0, has_side_effects=True, vmem_limit_bytes=63 << 20
        ),
        name="layer",
    )(*operands)

    def uncolumns(v):
        return v.reshape(v.shape[:-1] + (R, NG, 2, 8)).swapaxes(-3, -2).reshape(v.shape)

    if not inside:
        gwc = gwc.astype(F32).reshape(3, 2, KW, C * C // 2)
        gwc = lax.psum_scatter(gwc, everyone, scatter_dimension=2, tiled=True)
        gsmall = lax.psum_scatter(gsmall.reshape(3, KW, KW + 128), everyone, scatter_dimension=1, tiled=True)
    grad_out = gwc.swapaxes(1, 2).reshape(3, per, C, C).swapaxes(2, 3).reshape(3, per, C * C)
    grad_mid = uncolumns(gsmall[..., 0:KW]) if inside else gsmall[..., 0:KW]
    small = gsmall[..., KW:].swapaxes(1, 2)
    grad_in = jnp.concatenate([small[:, 1:4], small[:, 5:8]], axis=1)
    grad_bias = jnp.concatenate([small[:, 4:5], small[:, 12:13]], axis=1)
    new_in = adamw(kernel_in, first_in, second_in, grad_in, RATE_FIRST)
    new_bias = adamw(kernel_bias, first_bias, second_bias, grad_bias, RATE_MAIN)
    new_mid = adamw(kernel_mid, first_mid, second_mid, grad_mid, RATE_MAIN)
    new_out = adamw(kernel_out, first_out, second_out, grad_out, RATE_MAIN)
    return (layer[None], gradf[None]) + tuple(
        new[k] for k in range(3) for new in (new_in, new_bias, new_mid, new_out)
    )


def solution(mesh):
    nodes = P("grp", "tile", None)
    rows = P("grp", "tile")
    by_column = P(None, None, ("tile", "grp"))
    by_row = P(None, ("tile", "grp"), None)
    shards = (by_column, by_column, by_row, by_row)
    return jax.shard_map(
        functools.partial(per_device, mesh.shape["tile"], mesh.shape["grp"]),
        mesh=mesh,
        in_specs=(
            nodes, nodes, nodes, P("grp", None, None), P("grp", None, None), nodes, rows, rows, rows,
            P("grp", None), nodes, rows, nodes, rows,
        ) + shards * 3,
        out_specs=(nodes, nodes) + shards * 3,
        check_vma=False,
    )
```

time: 3480 us -> 318 us (0.09)
  local copies, waits for them, and re-layouts: 1210 us -> 27.7 us
  matrix products: 931 us -> 0 us
  waiting for transfers between devices: 546 us -> 0 us
  other arithmetic: 388 us -> 8.68 us
  blocking collectives: 333 us -> 0 us
  Pallas kernels: 0 us -> 277 us
    dot_general x312 -> x0, matrix products: 931 us -> none  [the longest x26 203 us: block_grad(): jnp.einsum('bkj,bkq->jq', act_two, grad_kernel, preferred_element_type=jn...]
    reshape x54 -> x14, local copies, waits for them, and re-layouts: 655 us -> 7.84 us  [the longest x3 2.59 us: edge_geom(): jnp.broadcast_to(rows[..., None], rows.shape + (lv.slots,))]
    convert_element_type x28 -> x3, local copies, waits for them, and re-layouts: 314 us -> 0.25 us  [edge_geom(): geom.astype(F32)]
    reduce_scatter x2 -> x0, waiting for transfers between devices: 293 us -> none  [the longest x1 269 us: per_device(): lax.psum_scatter(jnp.stack([sums_fine[3], sums_mid[3], sums_coarse[3]]),...]
    pallas_call x0 -> x1, Pallas kernels: none -> 277 us  [per_device(): pl.pallas_call(kernel, out_shape=(S((nf, C), BF), S((nf, C), BF), S((3, 2...]
    all_gather x6 -> x0, blocking collectives: 260 us -> none  [the longest x1 67.8 us: per_device(): lax.all_gather(kernel_mid.astype(jnp.bfloat16), ('tile', 'grp'), axis=1,...]
    psum x3 -> x0, waiting for transfers between devices: 250 us -> none  [the longest x2 178 us: coarse_back(): return (grad_output + lax.psum(partial_value, 'tile'), weight_sums)]
    convert_element_type x222 -> x5, other arithmetic: 224 us -> 3.14 us  [the longest x3 3.06 us: per_device(): s.astype(F32)]
  transfers between devices with their start and end apart: 12 -> 0, of which waited for: 6 -> 0; matrix products, arithmetic and copies ran while one was open for 4% -> 0% of each run, Pallas kernels for 0% -> 0%
where the time goes in v1:
time: 318 us; the launch traced here: 314 us
  Pallas kernels  277 us (87%)
  local copies, waits for them, and re-layouts  27.7 us (9%)
  other arithmetic  8.68 us (3%)
    pallas_call x1, Pallas kernels, per_device(): pl.pallas_call(kernel, out_shape=(S((nf, C), BF), S((nf, C), BF), S((3, 2...  277 us
    unnamed x73, local copies, waits for them, and re-layouts  12.3 us

profile of v1, /device:TPU:1, one launch (start us, length us, event | category | flops | bytes accessed | tf_op | source)
XLA Modules:
  0.0 314.4 jit_solution(13238844619815505242)
XLA Ops:
  0.7 0.7 copy-done.21
  2.8 0.9 reshape.245.zdm
  3.6 0.7 copy-done.22
  4.7 0.7 reshape.246.zdc
  5.9 1.2 fusion.12
  7.4 0.7 copy-done.10
  8.5 0.7 compare_select_fusion.lkf
  9.5 1.0 copy.158.zdf
  10.7 0.7 copy-done.20
  11.6 0.7 copy-done.7
  12.3 0.6 reshape.247
  13.7 0.7 concatenate.32.wsm
  14.4 1.2 fusion.14
  16.1 0.6 compare_select_fusion.1.lkm
  16.8 0.7 convert_bitcast_fusion
  20.4 1.0 copy.175
  21.9 0.8 maximum_maximum_fusion.tab
  22.8 0.8 copy.143
  23.6 0.6 pad.23.gm
  24.3 0.6 pad.24.gc
  24.9 277.0 %layer.1 = (bf16[512,64]{1,0:T(8,128)(2,1)}, bf16[512,64]{1,0:T(8,128)(2,1)}, f32[3,2,8,2048]{3,2,1,0:T(8,128)}, f32[3,8,384]{2,1,0:T(8,128)}) custom-call(bf16[512,128]{1,0:T(8,128)(2,1)} %maximum_maximum_fusion.tab, f32[512,64]{1,0:T(8,128)} %bitcast.67, s32[1,128]{1,0:T(1,128)} %send.1, s32[32,1,256]{2,1,0:T(1,128)} %compare_select_fusion.lkf, ...), custom_call_target="tpu_custom_call" | custom-call | tf_op jit(solution)/shard_map/layer/pallas_call | solution.py:919
  301.9 0.7 slice_bitcast_fusion
  304.3 0.6 copy-done.19
  305.1 0.7 copy.170
  305.8 0.7 copy.171
  306.5 0.7 copy.172
  307.2 0.6 reshape.251
  308.8 0.6 multiply_subtract_fusion.1
  310.8 0.7 copy-done.2
  311.6 1.2 multiply_subtract_fusion
  312.8 0.7 copy.168
  313.7 0.7 copy.169
  (128 shorter events, 12.9 us)
Async XLA Ops:
  0.6 0.7 copy-start.21
  0.7 1.6 copy-start.13
  3.6 0.7 copy-start.22
  4.7 1.2 copy-start.25
  4.7 1.2 copy-start.26
  7.3 0.8 copy-start.10
  8.5 0.7 copy-start.16
  9.5 1.0 copy-start.17
  10.7 0.7 copy-start.20
  11.5 0.7 copy-start.7
  13.1 1.3 copy-start.27
  13.1 2.8 copy-start.14
  13.7 5.8 %copy-start = (f32[3,8,4096]{2,1,0:T(8,128)S(1)}, f32[3,8,4096]{2,1,0:T(8,128)}, u32[]{:S(2)}) copy-start(f32[3,8,4096]{2,1,0:T(8,128)} %param.43) | copy-start | bytes 1179652
  16.1 0.7 copy-start.28
  17.5 0.7 copy-start.15
  20.4 1.0 copy-start.8
  21.9 0.9 copy-start.4
  302.6 1.6 copy-start.18
  302.8 0.7 copy-start.23
  302.8 0.7 copy-start.24
  304.2 0.7 copy-start.19
  305.1 2.1 copy-start.9
  307.8 0.8 copy-start.12
  308.0 0.7 copy-start.11
  308.0 1.4 copy-start.1
  310.5 1.0 copy-start.2
  310.5 1.1 copy-start.3
  311.6 1.2 copy-start.6
  312.8 0.9 copy-start.5

commit v2 on v1

v2 whole, which is shorter than its diff:
```python
import functools

import jax
import jax.numpy as jnp
from jax import lax
from jax.experimental import pallas as pl
from jax.experimental.pallas import tpu as pltpu
from jax.sharding import PartitionSpec as P

STEP = 5
B_ONE = 0.9
B_TWO = 0.95
EPSILON = 1e-08
WEIGHT_DECAY = 0.1
RATE_FIRST = 0.4
RATE_MAIN = 0.02

BF = jnp.bfloat16
F32 = jnp.float32
I32 = jnp.int32
MESH = pl.DeviceIdType.MESH
NN = ((1,), (0,))
NT = ((1,), (1,))
TN = ((0,), (0,))
LANES = 512
GROUP = 16


def dot(a, b, dims=NN):
    return lax.dot_general(a, b, (dims, ((), ())), preferred_element_type=F32)


def sig(v):
    return 0.5 + 0.5 * jnp.tanh(0.5 * v)


def split3(v):
    high = v.astype(BF)
    rest = v - high.astype(F32)
    mid = rest.astype(BF)
    low = (rest - mid.astype(F32)).astype(BF)
    return jnp.concatenate([high, mid, low], axis=0)


def join3(v):
    n = v.shape[0] // 3
    return v[:n] + v[n : 2 * n] + v[2 * n :]


def iota(shape, dim):
    return lax.broadcasted_iota(I32, shape, dim)


def log2(n):
    assert n & (n - 1) == 0
    return n.bit_length() - 1


def group_mask(width):
    return (iota((GROUP, width), 1) >> log2(width // GROUP) == iota((GROUP, width), 0)).astype(F32)


def one_hot(row, start, rows):
    return (iota((rows, row.shape[1]), 0) + start == row).astype(F32).astype(BF)


def spread(x, mask):
    return (x[:, None, :] * mask[None]).reshape(x.shape[0] * GROUP, mask.shape[1]).astype(BF)


def place(rows, columns, pairs):
    r, c = iota((rows, columns), 0), iota((rows, columns), 1)
    hit = jnp.zeros((rows, columns), F32)
    for row, column, count in pairs:
        hit = hit + jnp.where((r - row == c - column) & (r >= row) & (r < row + count), 1.0, 0.0)
    return hit.astype(BF)


def column_order(KW, NG, natural_rows):
    p = iota((KW, KW), 1 if natural_rows else 0)
    n = iota((KW, KW), 0 if natural_rows else 1)
    shift = log2(NG)
    inner, core, grp, chip = p & 7, (p >> 3) & 1, (p >> 4) & (NG - 1), p >> (4 + shift)
    return ((((((chip << 1) + core) << shift) + grp) << 3) + inner == n).astype(F32).astype(BF)


class Level:
    def __init__(self, index, nodes, slots, sources):
        self.index, self.nodes, self.slots, self.sources = index, nodes, slots, sources
        self.steps = nodes * slots // LANES
        self.width = GROUP * slots
        self.blocks = LANES // self.width
        self.chunk = sources if sources <= 1024 else 512


def make_kernel(T, NG, C, KW, fine, mid, coarse, halo, inside):
    H = T // 4
    NCH = T // 2 * NG
    A = KW // (32 * NG)
    NB = KW // 16
    R = T // 2
    HALF = C * C // 2
    QH = HALF // 2
    SMW = KW + 128
    levels = (fine, mid, coarse)
    NM, NC = mid.nodes, coarse.nodes

    def kernel(
        feat_h, cot_h, geof_h, geom_h, geoc_h, lkf_h, slf_h, send_h, parf_h, parm_h, lkm_h, slm_h, lkc_h, slc_h,
        kin_h, kb_h, kmid_h, kout_h,
        layer, gradf, gwc, gsmall,
        feat, cot, geof, geom, geoc, lkf, slf, send, parf, parm, lkm, slm, lkc, slc, kin, kb, kmid, ownw,
        geom_own, lkc_wide, slc_wide, pk0, pk1, pk2, gm, gc,
        extT, agbuf, gbuf, s0buf, smbuf, waT, wbT, wbr, bbc,
        mt0, mt1, mt2, qt1, qt2, as1, as2, xs0, xs1, xs2, zs0, zs1, zs2,
        ohp, tx_s, rx_s, tx_w, rx_w, tx_q, rx_q, tx_u, rx_u, tx_g, rx_g, tx_b, rx_b, tx_f, rx_f, tx_h, rx_h,
        x1T, x1b, x2T, x2b, acc0, acc1, acc2, acc1b, acc2b, rs1a, rs2a, rs1buf, rs2buf, v0s, gys,
        rsr0, rsr1, rsr2, rsr3, rsf, rsr4, gsb, rcA, rcB, sems,
    ):
        t = lax.axis_index("tile")
        g = lax.axis_index("grp")
        core = lax.rem(t, 2)
        r = t // 2
        lo = lax.rem(r, 2)
        hi = r // 2
        ch = r * NG + g
        ocore, olo, og = 1 - core, 1 - lo, 1 - g

        def tile_of(hi_, lo_, core_):
            return (hi_ * 2 + lo_) * 2 + core_

        partner = {"tile": tile_of(hi, lo, ocore), "grp": g}
        xn = {"tile": tile_of(hi, olo, core), "grp": g}
        yn = {"tile": t, "grp": og}

        counter = [0]
        open_recv, open_send = [], []

        def sem_block(n):
            base = counter[0]
            counter[0] += n
            return base

        def copy(src, dst, ssem, rsem, dev):
            return pltpu.make_async_remote_copy(
                src_ref=src, dst_ref=dst, send_sem=sems.at[ssem], recv_sem=sems.at[rsem],
                device_id=dev, device_id_type=MESH,
            )

        local = sem_block(1)

        def own_copy(src, dst):
            c = pltpu.make_async_copy(src, dst, sems.at[local])
            c.start()
            c.wait()

        class One:
            def __init__(self, src, dst, dev):
                self.s, self.r = sem_block(1), sem_block(1)
                self.d = None
                self.parts = (src, dst, self.s, self.r, dev)

            def start(self):
                self.d = copy(*self.parts)
                self.d.start()
                open_recv.append(self)
                open_send.append(self)

            def recv(self):
                open_recv.remove(self)
                self.d.wait_recv()

            def sent(self):
                open_send.remove(self)
                self.d.wait_send()

        class Ring:
            def __init__(self, n, src, dst, dev):
                self.n, self.src, self.dst, self.dev = n, src, dst, dev
                self.s, self.r = sem_block(n - 1), sem_block(n - 1)

            def each(self, f):
                def body(i, _):
                    d = i + 1
                    f(copy(self.src(d), self.dst(d), self.s + i, self.r + i, self.dev(d)))
                    return 0

                lax.fori_loop(0, self.n - 1, body, 0)

            def start(self):
                self.each(lambda c: c.start())
                open_recv.append(self)
                open_send.append(self)

            def recv(self):
                open_recv.remove(self)
                self.each(lambda c: c.wait_recv())

            def sent(self):
                open_send.remove(self)
                self.each(lambda c: c.wait_send())

        class Sides:
            def __init__(self, src_left, src_right, rx):
                self.ls, self.lr, self.rs, self.rr = (sem_block(1) for _ in range(4))
                self.rx = rx
                self.to_left = copy(src_left, rx.at[1], self.ls, self.lr, {"tile": t - 1, "grp": g})
                self.to_right = copy(src_right, rx.at[0], self.rs, self.rr, {"tile": t + 1, "grp": g})

            def start(self):
                open_recv.append(self)
                open_send.append(self)

                @pl.when(t > 0)
                def _():
                    self.to_left.start()

                @pl.when(t < T - 1)
                def _():
                    self.to_right.start()

                @pl.when(t == 0)
                def _():
                    self.rx[0] = jnp.zeros(self.rx.shape[1:], self.rx.dtype)

                @pl.when(t == T - 1)
                def _():
                    self.rx[1] = jnp.zeros(self.rx.shape[1:], self.rx.dtype)

            def recv(self):
                open_recv.remove(self)

                @pl.when(t < T - 1)
                def _():
                    self.to_left.wait_recv()

                @pl.when(t > 0)
                def _():
                    self.to_right.wait_recv()

            def sent(self):
                open_send.remove(self)

                @pl.when(t > 0)
                def _():
                    self.to_left.wait_send()

                @pl.when(t < T - 1)
                def _():
                    self.to_right.wait_send()

        def started(c):
            c.start()
            return c

        def finish():
            for c in tuple(open_recv):
                c.recv()
            for c in tuple(open_send):
                c.sent()

        barrier = pltpu.get_barrier_semaphore()
        total = T * NG
        me = t * NG + g

        def greet(i, _):
            other = lax.rem(me + i + 1, total)
            pl.semaphore_signal(
                barrier, inc=1, device_id={"tile": other // NG, "grp": lax.rem(other, NG)}, device_id_type=MESH
            )
            return 0

        lax.fori_loop(0, total - 1, greet, 0)

        loads = []

        def load(src, dst):
            c = pltpu.make_async_copy(src, dst, sems.at[sem_block(1)])
            c.start()
            loads.append(c)

        for src, dst in (
            (feat_h, feat), (geof_h, geof), (send_h, send), (kin_h, kin), (kb_h, kb), (kmid_h, kmid), (lkf_h, lkf),
            (slf_h, slf), (parf_h, parf), (geom_h, geom), (geoc_h, geoc), (parm_h, parm), (lkm_h, lkm), (slm_h, slm),
            (lkc_h, lkc), (slc_h, slc), (cot_h, cot),
        ):
            if inside or not any(dst is v for v in (kin, kb, kmid)):
                load(src, dst)
        own_lanes = pl.ds(pl.multiple_of(t * NM, NM), NM)
        load(geom_h.at[:, own_lanes], geom_own)
        if inside:
            for l in range(3):
                load(kout_h.at[l, core], ownw.at[l])
        for c in loads:
            c.wait()

        n0 = fine.nodes
        extT[:, 0:n0] = (
            dot(place(80, C, [(0, 0, C)]), feat[...]) + dot(place(80, 3, [(C + 5, 0, 3)]), geof[...])
        ).astype(BF)
        tx_s[0] = dot(extT[:, 0:n0], one_hot(send[...], 0, n0)).astype(BF)

        def window(index, start, n, at):
            off = index - start
            return jnp.where(off < 0, off + at + 8, jnp.where(off >= n, off - n + at + 8, off))

        ohp[...] = one_hot(window(parf[...], t * NM, NM, NM), 0, 2 * NM)
        if inside:
            order = column_order(KW, NG, True)
            for l in range(3):
                second = dot(kmid[l].astype(BF), order)
                first = dot(kin[l].astype(BF), place(6, 128, [(0, 0, 3), (3, 5, 3)]), TN)
                first = first + dot(kb[l].astype(BF), place(2, 128, [(0, 3, 1), (1, 8, 1)]), TN)
                smbuf[l, ch, core] = jnp.concatenate([second, first], axis=1)
        else:
            own_copy(kmid_h, smbuf)
            own_copy(kout_h, agbuf)
        pl.semaphore_wait(barrier, total - 1)

        def chip_dev(d):
            o = lax.rem(ch + d, NCH)
            return {"tile": (o // NG) * 2 + core, "grp": lax.rem(o, NG)}

        if inside:
            sm_a0 = started(Ring(NCH, lambda d: smbuf.at[0, ch, core], lambda d: smbuf.at[0, ch, core], chip_dev))
        halo_x = started(Sides(tx_s.at[0], tx_s.at[0], rx_s))
        if inside:
            s0c = [started(One(kout_h.at[l, ocore], s0buf.at[l], partner)) for l in range(3)]
            sm_a12 = started(Ring(NCH, lambda d: smbuf.at[1:3, ch, core], lambda d: smbuf.at[1:3, ch, core], chip_dev))

        ag = [[] for _ in range(3)]

        def ag_s1(l):
            if not inside:
                return
            s0c[l].recv()
            mine, theirs = ownw[l], s0buf[l]
            first = core == 0
            agbuf[l, core, hi, lo, g] = jnp.concatenate(
                [jnp.where(first, mine, theirs), jnp.where(first, theirs, mine)], axis=0
            ).astype(BF)
            c = Ring(
                H,
                lambda d: agbuf.at[l, core, hi, lo, g],
                lambda d: agbuf.at[l, core, hi, lo, g],
                lambda d: {"tile": tile_of(lax.rem(hi + d, H), lo, core), "grp": g},
            )
            c.start()
            ag[l].append([c])

        def ag_next(l, *copies):
            if not inside:
                return
            for c in ag[l][-1]:
                c.recv()
            for c in copies:
                c.start()
            ag[l].append(copies)

        def ag_s2(l):
            part = agbuf.at[l, core, :, lo, g]
            ag_next(l, One(part, part, xn), One(part, part, yn))

        def ag_s3(l):
            a = agbuf.at[l, core, :, olo, g, :, 0:QH]
            b = agbuf.at[l, core, :, lo, og, :, QH:HALF]
            ag_next(l, One(a, a, yn), One(b, b, xn))

        def ag_s4(l):
            part = agbuf.at[l, core]
            ag_next(l, One(part, part, partner))

        def ag_fin(l):
            if inside:
                for c in ag[l][-1]:
                    c.recv()
                for cs in ag[l]:
                    for c in cs:
                        c.sent()
        def unpack_small(l):
            block = smbuf[l].reshape(KW, SMW)
            second = block[:, 0:KW]
            wbr[l] = second.astype(BF)
            wbT[l] = second.T.astype(BF)
            waT[l] = block[:, KW : KW + 8].astype(BF)
            bbc[l] = jnp.broadcast_to(block[:, KW + 8 : KW + 9], (KW, 128))

        mts, qts = (mt0, mt1, mt2), (mt0, qt1, qt2)
        xss, zss, pks, a2s = (xs0, xs1, xs2), (zs0, zs1, zs2), (pk0, pk1, pk2), (None, as1, as2)

        def pack_nodes(lv, links, used, geometry):
            k, n = links.shape
            links = jnp.where(iota((k, n), 0) < used, links, -1).astype(F32)
            high = links.astype(BF).astype(F32)
            rows = dot(place(8, 3, [(0, 0, 3)]), geometry) + jnp.where(iota((8, n), 0) == 3, 1.0, 0.0)
            pad = jnp.zeros((128 - 2 * k - 8, n), F32)
            pks[lv.index][...] = jnp.concatenate([high, links - high, rows, pad], axis=0).T.astype(BF)

        def edge_columns(lv, i):
            k = lv.slots
            n = LANES // k
            at = pl.ds(pl.multiple_of(i * n, n), n)
            nodes = (iota((n, LANES), 1) >> log2(k) == iota((n, LANES), 0)).astype(F32).astype(BF)
            got = dot(pks[lv.index][at, :], nodes, TN)
            slot = iota((k, LANES), 1) & (k - 1) == iota((k, LANES), 0)
            links = jnp.sum(jnp.where(slot, got[0:k] + got[k : 2 * k], 0.0), axis=0, keepdims=True)
            return links, got[2 * k : 2 * k + 8]

        def take(table, row, lv):
            rows = lv.chunk
            if lv.sources == rows:
                return dot(table[...], one_hot(row, 0, rows))
            n = lv.sources // rows

            def body(k, acc):
                start = pl.multiple_of(k * rows, rows)
                return acc + dot(table[:, pl.ds(start, rows)], one_hot(row, start, rows))

            return lax.fori_loop(0, n, body, jnp.zeros((table.shape[0], LANES), F32))

        def put(acc, values, row, lv):
            rows = lv.chunk
            if lv.sources == rows:
                acc[...] += dot(values, one_hot(row, 0, rows), NT)
                return
            n = lv.sources // rows

            def body(k, _):
                start = pl.multiple_of(k * rows, rows)
                at = pl.ds(start, rows)
                acc[:, at] += dot(values, one_hot(row, start, rows), NT)
                return 0

            lax.fori_loop(0, n, body, 0)

        def edge_geometry(lv, x_table, g_table, first, last):
            l = lv.index

            def body(i, _):
                links, z = edge_columns(lv, i)
                row = links.astype(I32)
                if g_table is None:
                    got = take(x_table, row, lv)
                    xss[l][i] = got[0:C].astype(BF)
                    z = z + got[C : C + 8]
                else:
                    z = z + take(g_table, row, lv)[0:8]
                zss[l][i] = jnp.where(iota((8, LANES), 0) == 4, links, z)
                return 0

            lax.fori_loop(first, last, body, 0)

        def hidden(l, z):
            t1 = dot(waT[l], z.astype(BF))
            a1 = (t1 * sig(t1)).astype(BF)
            t2 = dot(wbT[l], a1) + bbc[l][:, 0:1]
            return (t2 * sig(t2)).astype(BF)

        def edge_hidden(lv):
            l = lv.index

            def body(i, _):
                a2s[l][i] = hidden(l, zss[l][i])
                return 0

            lax.fori_loop(0, lv.steps, body, 0)

        def edges_forward(lv, x_table, first, last):
            l = lv.index
            mask = group_mask(lv.width)

            def body(i, _):
                if x_table is None:
                    x = xss[l][i].astype(F32)
                    a2 = hidden(l, zss[l][i])
                else:
                    x = take(x_table, zss[l][i, 4:5, :].astype(I32), lv)
                    xss[l][i] = x.astype(BF)
                    a2 = a2s[l][i]
                for k in range(lv.blocks):
                    sl = slice(lv.width * k, lv.width * (k + 1))
                    m = dot(spread(x[:, sl], mask), a2[:, sl], NT)
                    at = pl.ds(pl.multiple_of((lv.blocks * i + k) * GROUP, GROUP), GROUP)
                    mts[l][:, at, :] = m.astype(BF).reshape(C, GROUP, KW)
                return 0

            lax.fori_loop(first, last, body, 0)

        def third(l, pair):
            per_half = C // 4
            half, k = pair // per_half, lax.rem(pair, per_half)
            return agbuf[l, half, :, :, :, :, pl.ds(pl.multiple_of(k * 128, 128), 128)].reshape(KW, 2 * C)

        def node_sums(lv):
            l = lv.index
            each = 4

            def body(i, accs):
                w = jnp.concatenate([third(l, each * i + u) for u in range(each)], axis=0)
                out = []
                for odd in range(2):
                    m = jnp.concatenate([mts[l][2 * (each * i + u) + odd] for u in range(each)], axis=1)
                    out.append(accs[odd] + dot(m, w))
                return tuple(out)

            zero = jnp.zeros((lv.nodes, 2 * C), F32)
            even, odd = lax.fori_loop(0, C // 2 // each, body, (zero, zero))
            return even.T[0:C] + odd.T[C:]

        stage = (gbuf, agbuf.at[1], agbuf.at[2])

        def third_grad(lv, gsT):
            l = lv.index
            n = C // 4
            each = 4

            def body(j, _):
                for u in range(each):
                    i = each * j + u
                    both = jnp.concatenate([dot(gsT, mts[l][2 * i]), dot(gsT, mts[l][2 * i + 1])], axis=0)
                    out = both.T.astype(BF).reshape(A, 2, NG, 16, 128)
                    stage[l][i // n, :, :, :, :, pl.ds(pl.multiple_of(lax.rem(i, n) * 128, 128), 128)] = out
                return 0

            lax.fori_loop(0, C // 2 // each, body, 0)

        def node_weights(lv, gsT):
            l = lv.index
            each = 4
            gsT = gsT.astype(F32)
            zero = jnp.zeros(gsT.shape, F32)
            low = jnp.concatenate([gsT, zero], axis=0).T[0 : lv.nodes].astype(BF)
            high = jnp.concatenate([zero, gsT], axis=0).T[0 : lv.nodes].astype(BF)

            def body(j, _):
                for u in range(each):
                    w = third(l, each * j + u)
                    c = 2 * (each * j + u)
                    qts[l][c] = dot(low, w, NT).astype(BF)
                    qts[l][c + 1] = dot(high, w, NT).astype(BF)
                return 0

            lax.fori_loop(0, C // 2 // each, body, 0)

        def edges_backward(lv, acc, first, last):
            l = lv.index
            mask = group_mask(lv.width)
            fold = (iota((C, C * GROUP), 1) >> log2(GROUP) == iota((C, C * GROUP), 0)).astype(F32).astype(BF)

            def body(i, _):
                zb = zss[l][i].astype(BF)
                t1 = dot(waT[l], zb)
                s1 = sig(t1)
                f1 = t1 * s1
                d1 = s1 + f1 * (1.0 - s1)
                a1 = f1.astype(BF)
                t2 = dot(wbT[l], a1) + bbc[l][:, 0:1]
                s2 = sig(t2)
                f2 = t2 * s2
                d2 = s2 + f2 * (1.0 - s2)
                a2 = f2.astype(BF)
                x = xss[l][i].astype(F32)
                g2s, gxs = [], []
                for k in range(lv.blocks):
                    sl = slice(lv.width * k, lv.width * (k + 1))
                    at = pl.ds(pl.multiple_of((lv.blocks * i + k) * GROUP, GROUP), GROUP)
                    q = qts[l][:, at, :].reshape(C * GROUP, KW)
                    g2s.append((dot(q, spread(x[:, sl], mask), TN) * d2[:, sl]).astype(BF))
                    every = dot(q, a2[:, sl])
                    own = (every.reshape(C, GROUP, lv.width) * mask[None]).reshape(C * GROUP, lv.width).astype(BF)
                    gxs.append(dot(fold, own).astype(BF))
                g2 = jnp.concatenate(g2s, axis=1)
                gx = jnp.concatenate(gxs, axis=1)
                g1 = (dot(wbr[l], g2) * d1).astype(BF)
                sm2 = dot(a1, g2, NT)
                p1 = dot(g1, zb, NT)
                p2 = dot(g2, zb, NT)
                gsb[l, :, :, :, 0:KW] += sm2.reshape(NB, 2, 8, KW)
                gsb[l, :, :, :, KW : KW + 8] += p1.reshape(NB, 2, 8, 8)
                gsb[l, :, :, :, KW + 8 : KW + 16] += p2.reshape(NB, 2, 8, 8)
                put(acc, gx, zss[l][i, 4:5, :].astype(I32), lv)
                return 0

            lax.fori_loop(first, last, body, 0)

        def roll_pick(left, right, n_left, left_lane, right_lane):
            lane = iota((1, 128), 1)
            a = pltpu.roll(left, (left_lane - (n_left - 8)) % 128, 1)
            b = pltpu.roll(right, right_lane % 128, 1)
            return jnp.where((lane >= left_lane) & (lane < left_lane + 8), a, 0.0) + jnp.where(
                (lane >= right_lane) & (lane < right_lane + 8), b, 0.0
            )

        def margin_pick(from_left, from_right, n_own, left_at, right_at):
            lane = iota((1, 128), 1)
            a = pltpu.roll(from_left, (0 - right_at) % 128, 1)
            b = pltpu.roll(from_right, (n_own - 8 - left_at) % 128, 1)
            return jnp.where(lane < 8, a, 0.0) + jnp.where((lane >= n_own - 8) & (lane < n_own), b, 0.0)

        ag_s1(0)
        halo_x.recv()
        near, far = (pltpu.roll(rx_s[k].astype(F32), halo, 1) for k in (0, 1))
        extT[:, n0:] = jnp.where(iota((1, 128), 1) < halo, near, far).astype(BF)
        pack_nodes(fine, lkf[...], slf[...], geof[...])
        pack_nodes(mid, lkm[...], slm[...], geom_own[...])
        lkc_wide[...] = jnp.zeros(lkc_wide.shape, F32)
        lkc_wide[0:NC] = lkc[...].astype(F32)
        slc_wide[...] = jnp.ones(slc_wide.shape, I32)
        slc_wide[:, 0:NC] = slc[...]
        eye = place(coarse.slots, coarse.slots, [(0, 0, coarse.slots)])
        high = lkc_wide[...].astype(BF)
        low = (lkc_wide[...] - high.astype(F32)).astype(BF)
        turned = (dot(eye, high, NT) + dot(eye, low, NT)).astype(I32)
        lanes = iota((1, 128), 1)
        own_c = jnp.where(lanes < NC, t * NC + lanes, -1)
        geo = dot(geoc[...], one_hot(own_c, 0, coarse.sources)).astype(BF)
        pack_nodes(coarse, turned, jnp.where(lanes < NC, slc_wide[...], 0), geo)
        to_rows = place(16, 3, [(5, 0, 3)])
        gm[...] = dot(to_rows, geom[...]).astype(BF)
        gc[...] = dot(to_rows, geoc[...]).astype(BF)
        nf, nm, nc = (v[...].astype(F32) for v in (slf, slm, slc_wide))
        blocks = [parm[:, pl.ds(pl.multiple_of(b * NM, NM), NM)].astype(F32)
                  for b in (jnp.maximum(t - 1, 0), t, jnp.minimum(t + 1, T - 1))]
        before, after = (pltpu.roll(jnp.broadcast_to(v, (8, NM)), 8, 1)[0:1] for v in (blocks[0], blocks[2]))
        sides = jnp.where((lanes < 8) & (t > 0), before, jnp.where((lanes >= 8) & (lanes < 16) & (t < T - 1), after, -1.0))
        around = jnp.concatenate([blocks[1], sides], axis=1).astype(I32)
        pw = jnp.where(around < 0, -1, window(around, t * NC, NC, NC))
        edge_geometry(fine, extT, None, 0, fine.steps)
        edge_geometry(mid, None, gm, 0, mid.steps)
        edge_geometry(coarse, None, gc, 0, coarse.steps)
        if inside:
            sm_a0.recv()
            sm_b0 = started(One(smbuf.at[0, :, core], smbuf.at[0, :, core], partner))
            ag_s2(0)
            sm_a12.recv()
            sm_b12 = started(One(smbuf.at[1:3, :, core], smbuf.at[1:3, :, core], partner))
            sm_b0.recv()
        unpack_small(0)
        n = fine.steps
        quarter = n // 4
        cuts = (0, n // 4, n // 2, 3 * n // 4, n)
        edges_forward(fine, None, cuts[0], cuts[1])
        ag_s1(1)
        edges_forward(fine, None, cuts[1], cuts[2])
        ag_s3(0)
        ag_s2(1)
        ag_s1(2)
        edges_forward(fine, None, cuts[2], cuts[3])
        ag_s4(0)
        edges_forward(fine, None, cuts[3], cuts[4])
        ag_s3(1)
        ag_s2(2)
        ag_fin(0)
        v0 = extT[0:C, 0 : fine.nodes].astype(F32) + node_sums(fine) / nf
        v0s[...] = v0

        ones8 = jnp.ones((8, fine.nodes), BF)
        part = dot(jnp.concatenate([split3(v0), ones8], axis=0), ohp[...], NT)
        sums = jnp.concatenate([join3(part[0 : 3 * C]), part[3 * C :]], axis=0)
        tx_w[0] = sums[:, NM:]
        ex_w = started(Sides(tx_w.at[0], tx_w.at[0], rx_w))
        if inside:
            sm_b12.recv()
        unpack_small(1)
        ag_s4(1)
        ex_w.recv()
        own = sums[:, 0:NM] + margin_pick(rx_w[0], rx_w[1], NM, 0, 8)
        inv1 = 1.0 / jnp.maximum(own[C : C + 1], 1.0)
        v1 = own[0:C] / jnp.maximum(own[C : C + 1], 1.0)
        x1b[r, core] = v1.astype(BF)

        def chip_ring(src, dst):
            return Ring(R, src, dst, lambda d: {"tile": lax.rem(r + d, R) * 2 + core, "grp": g})

        ag1 = started(chip_ring(lambda d: x1b.at[r, core], lambda d: x1b.at[r, core]))
        edge_hidden(mid)
        ag_s3(2)
        ag1.recv()
        ag1p = started(One(x1b.at[:, core], x1b.at[:, core], partner))
        unpack_small(2)
        ag1p.recv()
        for k in range(T):
            x1T[:, NM * k : NM * (k + 1)] = x1b[k // 2, k % 2]

        edges_forward(mid, x1T, 0, mid.steps)
        ag_fin(1)
        w1 = v1 + node_sums(mid) / nm
        tx_q[0, 0:C] = w1
        ohq = one_hot(pw, 0, 128)
        part = dot(jnp.concatenate([split3(w1), jnp.ones((8, NM), BF)], axis=0), ohq[:, 0:NM], NT)
        tx_q[0, C : 2 * C + 8] = jnp.concatenate([join3(part[0 : 3 * C]), part[3 * C :]], axis=0)
        ex_q = started(Sides(tx_q.at[0], tx_q.at[0], rx_q))
        edge_hidden(coarse)
        ag_s4(2)
        ex_q.recv()
        own = tx_q[0, C : 2 * C + 8] + margin_pick(rx_q[0, C : 2 * C + 8], rx_q[1, C : 2 * C + 8], NC, NC, NC + 8)
        w1m = roll_pick(rx_q[0, 0:C], rx_q[1, 0:C], NM, 0, 8)
        w1win = jnp.concatenate([w1, w1m], axis=1)
        lane = iota((1, 128), 1)
        mine = lane < NC
        cnt2 = jnp.maximum(own[C : C + 1], 1.0)
        v2 = jnp.where(mine, own[0:C] / cnt2, 0.0)

        x2b[r, core] = v2.astype(BF)
        ag2 = started(chip_ring(lambda d: x2b.at[r, core], lambda d: x2b.at[r, core]))
        ag2.recv()
        ag2p = started(One(x2b.at[:, core], x2b.at[:, core], partner))
        ag2p.recv()
        per = 128 // NC
        cols = []
        for k in range(coarse.sources // 128):
            block = x2b[per * k // 2, 0].astype(F32)
            for u in range(1, per):
                block = block + pltpu.roll(x2b[(per * k + u) // 2, (per * k + u) % 2].astype(F32), NC * u, 1)
            cols.append(block.astype(BF))
        for k, block in enumerate(cols):
            x2T[:, 128 * k : 128 * k + 128] = block
        edges_forward(coarse, x2T, 0, coarse.steps)
        ag_fin(2)
        sc = node_sums(coarse)
        sc = jnp.concatenate([sc, jnp.zeros((C, 128 - NC), F32)], axis=1)
        w2 = v2 + jnp.where(mine, sc / nc, 0.0)
        tx_u[0] = w2
        ex_u = started(Sides(tx_u.at[0], tx_u.at[0], rx_u))
        ex_u.recv()
        w2win = w2 + roll_pick(rx_u[0], rx_u[1], NC, NC, NC + 8)

        y1win = w1win + join3(dot(split3(w2win), ohq))
        y0 = v0s[...] + join3(dot(split3(y1win), ohp[...]))
        s0 = sig(y0)
        f0 = y0 * s0
        layer[...] = f0.astype(BF)
        gy0 = cot[...] * (s0 + f0 * (1.0 - s0))
        gys[...] = gy0
        gy1p = join3(dot(split3(gy0), ohp[...], NT))
        gw2p = join3(dot(split3(gy1p), ohq, NT))
        tx_g[0, 0:C] = gy1p[:, NM:]
        tx_g[0, C : 2 * C] = gw2p
        ex_g = started(Sides(tx_g.at[0], tx_g.at[0], rx_g))
        ex_g.recv()
        gy1 = gy1p[:, 0:NM] + margin_pick(rx_g[0, 0:C], rx_g[1, 0:C], NM, 0, 8)
        gw2 = jnp.where(mine, gw2p + margin_pick(rx_g[0, C:], rx_g[1, C:], NC, NC, NC + 8), 0.0)

        rs = [[] for _ in range(3)]

        def rs_step(l, fix, *copies):
            if not inside:
                return
            if rs[l]:
                for c in rs[l][-1]:
                    c.recv()
            fix()
            for c in copies:
                c.start()
            rs[l].append(copies)

        def rs_s0(l):
            rs_step(l, lambda: None, One(stage[l].at[ocore], rsr0.at[l], partner))

        def rs_s1(l):
            def fix():
                def body(i, _):
                    both = stage[l][core, i].astype(F32) + rsr0[l, i].astype(F32)
                    stage[l][core, i] = both.astype(BF)
                    return 0

                lax.fori_loop(0, H, body, 0)

            rs_step(
                l, fix,
                One(stage[l].at[core, :, olo, og, :, 0:QH], rsr1.at[l, 0], xn),
                One(stage[l].at[core, :, olo, og, :, QH:HALF], rsr1.at[l, 1], yn),
            )

        def rs_s2(l):
            def fix():
                def body(i, _):
                    a = stage[l][core, i, lo, og, :, 0:QH].astype(F32) + rsr1[l, 0, i].astype(F32)
                    stage[l][core, i, lo, og, :, 0:QH] = a.astype(BF)
                    b = stage[l][core, i, olo, g, :, QH:HALF].astype(F32) + rsr1[l, 1, i].astype(F32)
                    stage[l][core, i, olo, g, :, QH:HALF] = b.astype(BF)
                    return 0

                lax.fori_loop(0, H, body, 0)

            rs_step(
                l, fix,
                One(stage[l].at[core, :, lo, og], rsr2.at[l, 0], yn),
                One(stage[l].at[core, :, olo, g], rsr2.at[l, 1], xn),
            )

        def rs_s3(l):
            def fix():
                def body(i, _):
                    a = stage[l][core, i, lo, g].astype(F32) + rsr2[l, 0, i].astype(F32) + rsr2[l, 1, i].astype(F32)
                    stage[l][core, i, lo, g] = a.astype(BF)
                    return 0

                lax.fori_loop(0, H, body, 0)

            rs_step(
                l, fix,
                Ring(
                    H,
                    lambda d: stage[l].at[core, lax.rem(hi + d, H), lo, g],
                    lambda d: rsr3.at[l, d - 1],
                    lambda d: {"tile": tile_of(lax.rem(hi + d, H), lo, core), "grp": g},
                ),
            )

        def rs_s4(l):
            def fix():
                tot = stage[l][core, hi, lo, g].astype(F32)
                for k in range(H - 1):
                    tot = tot + rsr3[l, k].astype(F32)
                rsf[l, 0] = tot[0:8]
                rsf[l, 1] = tot[8:16]

            rs_step(l, fix, One(rsf.at[l, ocore], rsr4.at[l], partner))

        def rs_s5(l):
            if not inside:
                own_copy(stage[l], gwc.at[l])
                return
            for c in rs[l][-1]:
                c.recv()
            gwc[l, core] = rsf[l, core]
            gwc[l, ocore] = rsr4[l]

        gsb[...] = jnp.zeros(gsb.shape, F32)
        gs_copies = {}

        def gs_start(a, b):
            if inside:
                gs_copies[a] = started(One(gsb.at[a:b, :, ocore], rcA.at[a:b], partner))

        def gs_ring(a, b):
            if inside:
                gs_copies[a].recv()
                for l in range(a, b):
                    gsb[l, :, core] += rcA[l]
                gs_copies[a] = started(
                    Ring(
                        NCH,
                        lambda d: gsb.at[a:b, lax.rem(ch + d, NCH), core],
                        lambda d: rcB.at[d - 1, a:b],
                        chip_dev,
                    )
                )

        def gs_end(a, b):
            if not inside:
                gsmall[a:b] = gsb[a:b]
                return
            gs_copies[a].recv()

            def add3(k, acc):
                return acc + rcB[k, a:b]

            gsmall[a:b] = lax.fori_loop(0, NCH - 1, add3, gsb[a:b, ch, core])


        gs2T = jnp.where(mine, gw2 / nc, 0.0).astype(BF)
        node_weights(coarse, gs2T)
        acc2[...] = jnp.zeros(acc2.shape, F32)
        edges_backward(coarse, acc2, 0, coarse.steps)
        a2rows = jnp.concatenate([acc2[...], jnp.zeros(acc2.shape, F32)], axis=0)
        acc2b[...] = a2rows.T.astype(BF).reshape(R, 2, NC, 128)
        r2p = started(One(acc2b.at[:, ocore], rs2a, partner))
        third_grad(coarse, gs2T[:, 0:NC])
        r2p.recv()
        acc2b[:, core] = (acc2b[:, core].astype(F32) + rs2a[...].astype(F32)).astype(BF)
        r2 = started(chip_ring(lambda d: acc2b.at[lax.rem(r + d, R), core], lambda d: rs2buf.at[d - 1]))
        rs_s0(2)
        r2.recv()

        def add2(k, acc):
            return acc + rs2buf[k].astype(F32)

        own2 = lax.fori_loop(0, R - 1, add2, acc2b[r, core].astype(F32))
        own2 = jnp.concatenate([own2, jnp.zeros((128 - NC, 128), F32)], axis=0).T[0:C]
        gv2 = jnp.where(mine, (gw2 + own2) / cnt2, 0.0)
        tx_b[0] = gv2
        ex_b = started(Sides(tx_b.at[0], tx_b.at[0], rx_b))
        rs_s1(2)
        ex_b.recv()
        gv2win = gv2 + roll_pick(rx_b[0], rx_b[1], NC, NC, NC + 8)
        gw1 = gy1 + join3(dot(split3(gv2win), ohq[:, 0:NM]))

        gs1T = (gw1 / nm).astype(BF)
        node_weights(mid, gs1T)
        acc1[...] = jnp.zeros(acc1.shape, F32)
        edges_backward(mid, acc1, 0, mid.steps)
        for k in range(T):
            acc1b[k // 2, k % 2] = acc1[:, NM * k : NM * (k + 1)].astype(BF)
        r1p = started(One(acc1b.at[:, ocore], rs1a, partner))
        rs_s2(2)
        r1p.recv()
        acc1b[:, core] = (acc1b[:, core].astype(F32) + rs1a[...].astype(F32)).astype(BF)
        r1 = started(chip_ring(lambda d: acc1b.at[lax.rem(r + d, R), core], lambda d: rs1buf.at[d - 1]))
        third_grad(mid, gs1T)
        rs_s0(1)
        r1.recv()

        def add1(k, acc):
            return acc + rs1buf[k].astype(F32)

        own1 = lax.fori_loop(0, R - 1, add1, acc1b[r, core].astype(F32))
        gv1 = (gw1 + own1) * inv1
        tx_f[0] = gv1
        ex_f = started(Sides(tx_f.at[0], tx_f.at[0], rx_f))
        gs_start(1, 3)
        rs_s1(1)
        ex_f.recv()
        gv1win = jnp.concatenate([gv1, roll_pick(rx_f[0], rx_f[1], NM, 0, 8)], axis=1)
        gv0 = gys[...] + join3(dot(split3(gv1win), ohp[...]))
        gys[...] = gv0

        gs0 = gv0 / nf
        gs0T = gs0.astype(BF)
        third_grad(fine, gs0T)
        rs_s0(0)
        rs_s3(2)
        rs_s2(1)
        node_weights(fine, gs0T)
        acc0[...] = jnp.zeros(acc0.shape, F32)
        rs_s1(0)
        gs_ring(1, 3)
        edges_backward(fine, acc0, cuts[0], cuts[1])
        rs_s2(0)
        rs_s3(1)
        rs_s4(2)
        edges_backward(fine, acc0, cuts[1], cuts[2])
        rs_s3(0)
        rs_s4(1)
        rs_s5(2)
        edges_backward(fine, acc0, cuts[2], cuts[3])
        rs_s4(0)
        rs_s5(1)
        gs_end(1, 3)
        edges_backward(fine, acc0, cuts[3], cuts[4])
        tx_h[0] = acc0[:, fine.nodes : fine.nodes + 2 * halo]
        ex_h = started(Sides(tx_h.at[0], tx_h.at[0], rx_h))

        gs_start(0, 1)
        rs_s5(0)
        ex_h.recv()
        lane1 = iota((1, 128), 1)
        back = jnp.where(lane1 < halo, pltpu.roll(rx_h[0], halo, 1), pltpu.roll(rx_h[1], halo, 1))
        ohs2 = one_hot(send[...], 0, n0)
        gf = gys[...] + acc0[:, 0 : fine.nodes] + join3(dot(split3(back), ohs2, NT))
        gradf[...] = gf.astype(BF)
        gs_ring(0, 1)
        gs_end(0, 1)

        finish()

    n_sems = (
        2 * (2 * (NCH - 1)) + 4 + 2 * 3 + 3 * (2 * (H - 1) + 4 + 4 + 2) + 4
        + 4 * 7 + 4 * (2 * (T - 1)) + 4 * NCH + 3 * (2 + 4 + 4 + 2 * (H - 1) + 2) + 2 + 2 * (NCH - 1) + 32
    )
    V = pltpu.VMEM
    ls = 3 if inside else 1
    nf, nm_, nc_ = fine.nodes, NM, NC
    scratch = [
        V((C, nf), BF), V((C, nf), F32), V((3, nf), BF), V((3, mid.sources), BF), V((3, coarse.sources), BF),
        V((fine.slots, nf), I32), V((1, nf), I32), V((1, 2 * halo), I32), V((1, nf), I32), V((1, mid.sources), I32),
        V((mid.slots, nm_), I32), V((1, nm_), I32), V((nc_, coarse.slots), I32), V((1, nc_), I32),
        V((3, 6, 8), F32), V((3, 2, 8), F32), V((3, 8, KW), F32), V((ls, 8, HALF), F32),
        V((3, nm_), BF), V((128, coarse.slots), F32), V((1, 128), I32),
        V((nf, 128), BF), V((nm_, 128), BF), V((128, 128), BF), V((16, mid.sources), BF), V((16, coarse.sources), BF),
        V((80, nf + 2 * halo), BF),
        V((3, 2, A, 2, NG, 16, HALF), BF), V((2, A, 2, NG, 16, HALF), BF), V((ls, 8, HALF), F32),
        V((3, NB, 2, 8, SMW), F32), V((3, KW, 8), BF), V((3, KW, KW), BF), V((3, KW, KW), BF), V((3, KW, 128), F32),
        V((C, nf, KW), BF), V((C, nm_, KW), BF), V((C, nc_, KW), BF), V((C, nm_, KW), BF), V((C, nc_, KW), BF),
        V((mid.steps, KW, LANES), BF), V((coarse.steps, KW, LANES), BF),
        V((fine.steps, C, LANES), BF), V((mid.steps, C, LANES), BF), V((coarse.steps, C, LANES), BF),
        V((fine.steps, 8, LANES), F32), V((mid.steps, 8, LANES), F32), V((coarse.steps, 8, LANES), F32),
        V((2 * NM, nf), BF),
        V((1, 80, 128), BF), V((2, 80, 128), BF),
        V((1, C + 8, 128), F32), V((2, C + 8, 128), F32),
        V((1, 2 * C + 8, 128), F32), V((2, 2 * C + 8, 128), F32),
        V((1, C, 128), F32), V((2, C, 128), F32),
        V((1, 2 * C, 128), F32), V((2, 2 * C, 128), F32),
        V((1, C, 128), F32), V((2, C, 128), F32),
        V((1, C, 128), F32), V((2, C, 128), F32),
        V((1, C, 128), F32), V((2, C, 128), F32),
        V((C, mid.sources), BF), V((R, 2, C, 128), BF), V((C, coarse.sources), BF), V((R, 2, C, 128), BF),
        V((C, nf + 2 * halo), F32), V((C, mid.sources), F32), V((C, coarse.sources), F32),
        V((R, 2, C, 128), BF), V((R, 2, NC, 128), BF), V((R, C, 128), BF), V((R, NC, 128), BF),
        V((R - 1, C, 128), BF), V((R - 1, NC, 128), BF), V((C, nf), F32), V((C, nf), F32),
        V((ls, A, 2, NG, 16, HALF), BF), V((ls, 2, A, 16, QH), BF), V((ls, 2, A, 16, HALF), BF),
        V((ls, A - 1, 16, HALF), BF), V((ls, 2, 8, HALF), F32), V((ls, 8, HALF), F32),
        V((3, NB, 2, 8, SMW), F32), V((ls, NB, 8, SMW), F32), V((NB - 1, 3, 8, SMW), F32),
        pltpu.SemaphoreType.DMA((n_sems,)),
    ]
    return kernel, scratch


def adamw(master, moment, square, grad, learn_rate):
    moment_new = B_ONE * moment + (1.0 - B_ONE) * grad
    square_new = B_TWO * square + (1.0 - B_TWO) * grad * grad
    fix_one = 1.0 - B_ONE**STEP
    fix_two = 1.0 - B_TWO**STEP
    master_new = master - learn_rate * (
        moment_new / fix_one / (jnp.sqrt(square_new / fix_two) + EPSILON) + WEIGHT_DECAY * master
    )
    return (master_new, moment_new, square_new)


def make_update(KW, NG, per, inside):
    rates = (RATE_FIRST, RATE_MAIN, RATE_MAIN, RATE_MAIN)

    def kernel(*refs):
        far_in, far_out, near_in, near_out, sems = refs[0:14], refs[14:26], refs[26:40], refs[40:52], refs[52]
        copies = [pltpu.make_async_copy(a, b, sems.at[k]) for k, (a, b) in enumerate(zip(far_in, near_in))]
        for c in copies:
            c.start()
        for c in copies:
            c.wait()
        gwc, gsmall = near_in[0:2]
        order = column_order(KW, NG, False)
        out = []

        def update(k, index, grad):
            new = adamw(*(near_in[2 + 4 * m + k][index] for m in range(3)), grad, rates[k])
            for m in range(3):
                near_out[4 * m + k][index] = new[m]

        def done(k):
            for m in range(3):
                c = pltpu.make_async_copy(near_out[4 * m + k], far_out[4 * m + k], sems.at[14 + 4 * m + k])
                c.start()
                out.append(c)

        for l in range(3):
            update(3, l, gwc[l])
        done(3)
        for l in range(3):
            grad = gsmall[l, :, 0:KW]
            update(2, l, join3(dot(split3(grad), order)) if inside else grad)
        done(2)
        for l in range(3):
            parts = split3(gsmall[l, :, KW:])
            parts = [parts[per * k : per * (k + 1)] for k in range(3)]
            for k, picks, rows in ((0, [(0, 0, 3), (3, 5, 3)], 6), (1, [(0, 3, 1), (1, 11, 1)], 2)):
                pick = place(rows, 128, picks)
                update(k, l, sum(dot(pick, part, NT) for part in parts))
        done(0)
        done(1)
        for c in out:
            c.wait()

    return kernel


def per_device(
    T, NG,
    features, cotangent, geom_fine, geom_mid, geom_coarse, links_fine, slots_fine, send_lists, parent_fine,
    parent_mid, links_mid, slots_mid, links_coarse, slots_coarse, kernel_in, kernel_bias, kernel_mid, kernel_out,
    *moments,
):
    C = features.shape[2]
    KW = kernel_mid.shape[2]
    NM, NC = links_mid.shape[1], links_coarse.shape[1]
    halo = send_lists.shape[1] // 2
    nf = features.shape[1]
    fine = Level(0, nf, links_fine.shape[2], nf + 2 * halo)
    mid = Level(1, NM, links_mid.shape[2], geom_mid.shape[1])
    coarse = Level(2, NC, links_coarse.shape[2], geom_coarse.shape[1])
    per = kernel_mid.shape[1]
    inside = per == 8
    everyone = ("tile", "grp")
    half = C * C // 2
    grid = (3, 2, KW // (32 * NG), 2, NG, 16, half)
    small = kernel_mid
    large = kernel_out.reshape(3, per, C, C).transpose(0, 3, 2, 1).reshape(3, 2, half, per).swapaxes(2, 3)
    if not inside:
        zero = jnp.zeros((3, per, 1), F32)
        first = kernel_in.swapaxes(1, 2)
        bias = kernel_bias.swapaxes(1, 2)
        small = jnp.concatenate(
            [kernel_mid, first[..., 0:3], bias[..., 0:1], zero, first[..., 3:6], bias[..., 1:2],
             jnp.zeros((3, per, 119), F32)], axis=2
        )
        small = lax.all_gather(small, everyone, axis=1, tiled=True).reshape(3, KW // 16, 2, 8, KW + 128)
        large = lax.all_gather(large.astype(BF), everyone, axis=2, tiled=True).reshape(grid)

    kernel, scratch = make_kernel(T, NG, C, KW, fine, mid, coarse, halo, inside)
    S = jax.ShapeDtypeStruct
    vm = pl.BlockSpec(memory_space=pltpu.VMEM)
    far = pl.BlockSpec(memory_space=pl.ANY)
    turn = lambda v: v[0].swapaxes(0, 1)
    operands = (
        turn(features), turn(cotangent), turn(geom_fine), turn(geom_mid), turn(geom_coarse),
        turn(links_fine), slots_fine, send_lists, parent_fine, parent_mid, turn(links_mid), slots_mid,
        links_coarse[0], slots_coarse, kernel_in, kernel_bias, small, large,
    )
    layer, gradf, gwc, gsmall = pl.pallas_call(
        kernel,
        out_shape=(S((C, nf), BF), S((C, nf), BF), S((3, 2, 8, half), F32) if inside else S(grid, BF),
                   S((3, 8, KW + 128) if inside else (3, KW // 16, 2, 8, KW + 128), F32)),
        in_specs=[far] * len(operands),
        out_specs=(vm, vm, vm if inside else far, vm),
        scratch_shapes=scratch,
        compiler_params=pltpu.CompilerParams(
            collective_id=0, has_side_effects=True, vmem_limit_bytes=63 << 20
        ),
        name="layer",
    )(*operands)
    if not inside:
        gwc = gwc.astype(F32).reshape(3, 2, KW, half)
        gwc = lax.psum_scatter(gwc, everyone, scatter_dimension=2, tiled=True)
        gsmall = lax.psum_scatter(gsmall.reshape(3, KW, KW + 128), everyone, scatter_dimension=1, tiled=True)
    gwc = gwc.swapaxes(1, 2).reshape(3, per, C, C).swapaxes(2, 3).reshape(3, per, C * C)
    state = (kernel_in, kernel_bias, kernel_mid, kernel_out) + moments
    new = pl.pallas_call(
        make_update(KW, NG, per, inside),
        out_shape=tuple(S(v.shape, F32) for v in state),
        in_specs=[far] * 14,
        out_specs=(far,) * 12,
        scratch_shapes=[pltpu.VMEM(v.shape, F32) for v in (gwc, gsmall) + state]
        + [pltpu.VMEM(v.shape, F32) for v in state] + [pltpu.SemaphoreType.DMA((26,))],
        compiler_params=pltpu.CompilerParams(vmem_limit_bytes=63 << 20),
        name="update",
    )(gwc, gsmall, *state)
    return (layer.swapaxes(0, 1)[None], gradf.swapaxes(0, 1)[None]) + tuple(new)


def solution(mesh):
    nodes = P("grp", "tile", None)
    rows = P("grp", "tile")
    by_column = P(None, None, ("tile", "grp"))
    by_row = P(None, ("tile", "grp"), None)
    shards = (by_column, by_column, by_row, by_row)
    return jax.shard_map(
        functools.partial(per_device, mesh.shape["tile"], mesh.shape["grp"]),
        mesh=mesh,
        in_specs=(
            nodes, nodes, nodes, P("grp", None, None), P("grp", None, None), nodes, rows, rows, rows,
            P("grp", None), nodes, rows, nodes, rows,
        ) + shards * 3,
        out_specs=(nodes, nodes) + shards * 3,
        check_vma=False,
    )
```

time: 318 us -> 221 us (0.69)
  Pallas kernels: 277 us -> 211 us
  local copies, waits for them, and re-layouts: 27.7 us -> 7.51 us
  other arithmetic: 8.68 us -> 0 us
    pallas_call x1 -> x2, Pallas kernels: 277 us -> 211 us  [the longest x1 208 us: per_device(): pl.pallas_call(kernel, out_shape=(S((C, nf), BF), S((C, nf), BF), S((3, 2...]
    unnamed x73 -> x6, local copies, waits for them, and re-layouts: 12.3 us -> 1.46 us
    reshape x8 -> x0, local copies, waits for them, and re-layouts: 5.12 us -> none  [the longest x3 2.59 us: edge_geom(): jnp.broadcast_to(rows[..., None], rows.shape + (lv.slots,))]
where the time goes in v2:
time: 221 us; the launch traced here: 219 us
  Pallas kernels  211 us (95%)
  local copies, waits for them, and re-layouts  7.51 us (3%)
    pallas_call x1, Pallas kernels, per_device(): pl.pallas_call(kernel, out_shape=(S((C, nf), BF), S((C, nf), BF), S((3, 2...  208 us

profile of v2, /device:TPU:1, one launch (start us, length us, event | category | flops | bytes accessed | tf_op | source)
XLA Modules:
  0.0 219.2 jit_solution(4671161226149784174)
XLA Ops:
  0.6 1.3 reshape.40
  2.0 0.3 copy.40
  2.2 0.4 reshape.41
  2.6 1.0 copy.45
  3.6 207.5 %layer.1 = (bf16[64,512]{1,0:T(8,128)(2,1)}, bf16[64,512]{1,0:T(8,128)(2,1)}, f32[3,2,8,2048]{3,2,1,0:T(8,128)}, f32[3,8,384]{2,1,0:T(8,128)}) custom-call(bf16[64,512]{1,0:T(8,128)(2,1)} %bitcast.45, f32[64,512]{1,0:T(8,128)} %bitcast.44, bf16[3,512]{1,0:T(4,128)(2,1)} %bitcast.52, bf16[3,2048]{1,0:T(4,128)(2,1)} %bitcast.49, bf16[3,512]{1,0:T(4,128)(2,1)} %bitcast.53, ...), custom_call_target="tpu_custom_call" | custom-call | tf_op jit(solution)/shard_map/layer/pallas_call | solution.py:1099
  211.1 1.3 copy.42
  212.4 0.5 reshape.42
  212.9 0.3 copy.43
  213.2 1.0 reshape.43.refs_0_
  214.2 0.0 copy-start.1
  214.2 3.5 %update.1 = (f32[3,6,8]{2,1,0:T(8,128)}, f32[3,2,8]{2,1,0:T(2,128)}, f32[3,8,256]{2,1,0:T(8,128)}, f32[3,8,4096]{2,1,0:T(8,128)}, f32[3,6,8]{2,1,0:T(8,128)}, /*...) custom-call(f32[3,8,4096]{2,1,0:T(8,128)} %reshape.43.refs_0_, ...), custom_call_target="tpu_custom_call" | custom-call | tf_op jit(solution)/shard_map/update/pallas_call | solution.py:1117
  217.7 0.0 copy-done.1
  217.7 0.0 copy-start
  217.8 0.6 copy.48
  218.4 0.2 copy-done
  218.6 0.6 copy.49
Async XLA Ops:
  214.2 3.5 %copy-start.1 = (bf16[64,512]{1,0:T(8,128)(2,1)S(1)}, bf16[64,512]{1,0:T(8,128)(2,1)}, u32[]{:S(2)}) copy-start(bf16[64,512]{1,0:T(8,128)(2,1)} %get-tuple-element.30) | copy-start | bytes 196612
  217.7 0.8 copy-start

commit v3 on v2

--- a/solution.py
+++ b/solution.py
@@ -23,7 +23,7 @@
 NT = ((1,), (1,))
 TN = ((0,), (0,))
 LANES = 512
-GROUP = 16
+GROUP = 8
 
 
 def dot(a, b, dims=NN):
@@ -90,7 +90,7 @@
         self.steps = nodes * slots // LANES
         self.width = GROUP * slots
         self.blocks = LANES // self.width
-        self.chunk = sources if sources <= 1024 else 512
+        self.parts = sources // 128
 
 
 def make_kernel(T, NG, C, KW, fine, mid, coarse, halo, inside):
@@ -102,6 +102,7 @@
     HALF = C * C // 2
     QH = HALF // 2
     SMW = KW + 128
+    BW = HALF + KW
     levels = (fine, mid, coarse)
     NM, NC = mid.nodes, coarse.nodes
 
@@ -111,10 +112,10 @@
         layer, gradf, gwc, gsmall,
         feat, cot, geof, geom, geoc, lkf, slf, send, parf, parm, lkm, slm, lkc, slc, kin, kb, kmid, ownw,
         geom_own, lkc_wide, slc_wide, pk0, pk1, pk2, gm, gc,
-        extT, agbuf, gbuf, s0buf, smbuf, waT, wbT, wbr, bbc,
-        mt0, mt1, mt2, qt1, qt2, as1, as2, xs0, xs1, xs2, zs0, zs1, zs2,
+        extT, agbuf, gbuf, s0buf, s0x, smx, smbuf, smfull, waT, wbT, wbr, bbc,
+        mt0, mt1, mt2, qt1, qt2, as0, as1, as2, xs0, xs1, xs2, zs0, zs1, zs2,
         ohp, tx_s, rx_s, tx_w, rx_w, tx_q, rx_q, tx_u, rx_u, tx_g, rx_g, tx_b, rx_b, tx_f, rx_f, tx_h, rx_h,
-        x1T, x1b, x2T, x2b, acc0, acc1, acc2, acc1b, acc2b, rs1a, rs2a, rs1buf, rs2buf, v0s, gys,
+        x1b, x2T, x2b, acc0, acc1, acc2, acc1b, acc2b, rs1a, rs2a, rs1buf, rs2buf, v0s, gys,
         rsr0, rsr1, rsr2, rsr3, rsf, rsr4, gsb, rcA, rcB, sems,
     ):
         t = lax.axis_index("tile")
@@ -133,6 +134,13 @@
         xn = {"tile": tile_of(hi, olo, core), "grp": g}
         yn = {"tile": t, "grp": og}
 
+        nil = t - t
+
+        levels_at = [nil + k for k in range(3)]
+
+        def ix(k):
+            return levels_at[k]
+
         counter = [0]
         open_recv, open_send = [], []
 
@@ -143,7 +151,7 @@
 
         def copy(src, dst, ssem, rsem, dev):
             return pltpu.make_async_remote_copy(
-                src_ref=src, dst_ref=dst, send_sem=sems.at[ssem], recv_sem=sems.at[rsem],
+                src_ref=src, dst_ref=dst, send_sem=sems.at[nil + ssem], recv_sem=sems.at[nil + rsem],
                 device_id=dev, device_id_type=MESH,
             )
 
@@ -157,22 +165,20 @@
         class One:
             def __init__(self, src, dst, dev):
                 self.s, self.r = sem_block(1), sem_block(1)
-                self.d = None
                 self.parts = (src, dst, self.s, self.r, dev)
 
             def start(self):
-                self.d = copy(*self.parts)
-                self.d.start()
+                copy(*self.parts).start()
                 open_recv.append(self)
                 open_send.append(self)
 
             def recv(self):
                 open_recv.remove(self)
-                self.d.wait_recv()
+                copy(*self.parts).wait_recv()
 
             def sent(self):
                 open_send.remove(self)
-                self.d.wait_send()
+                copy(*self.parts).wait_send()
 
         class Ring:
             def __init__(self, n, src, dst, dev):
@@ -204,8 +210,15 @@
             def __init__(self, src_left, src_right, rx):
                 self.ls, self.lr, self.rs, self.rr = (sem_block(1) for _ in range(4))
                 self.rx = rx
-                self.to_left = copy(src_left, rx.at[1], self.ls, self.lr, {"tile": t - 1, "grp": g})
-                self.to_right = copy(src_right, rx.at[0], self.rs, self.rr, {"tile": t + 1, "grp": g})
+                self.src_left, self.src_right = src_left, src_right
+
+            @property
+            def to_left(self):
+                return copy(self.src_left, self.rx.at[1], self.ls, self.lr, {"tile": t - 1, "grp": g})
+
+            @property
+            def to_right(self):
+                return copy(self.src_right, self.rx.at[0], self.rs, self.rr, {"tile": t + 1, "grp": g})
 
             def start(self):
                 open_recv.append(self)
@@ -260,91 +273,111 @@
                 c.sent()
 
         barrier = pltpu.get_barrier_semaphore()
-        total = T * NG
-        me = t * NG + g
-
-        def greet(i, _):
-            other = lax.rem(me + i + 1, total)
-            pl.semaphore_signal(
-                barrier, inc=1, device_id={"tile": other // NG, "grp": lax.rem(other, NG)}, device_id_type=MESH
-            )
+
+        def chip_dev(d):
+            o = lax.rem(ch + d, NCH)
+            return {"tile": (o // NG) * 2 + core, "grp": lax.rem(o, NG)}
+
+        def greet(dev):
+            pl.semaphore_signal(barrier, inc=1, device_id=dev, device_id_type=MESH)
+
+        def greet_chip(i, _):
+            greet(chip_dev(i + 1))
             return 0
 
-        lax.fori_loop(0, total - 1, greet, 0)
-
-        loads = []
-
-        def load(src, dst):
+        lax.fori_loop(0, NCH - 1, greet_chip, 0)
+        greet(partner)
+        beside = t - 1 + 2 * core
+        has_beside = (beside >= 0) & (beside < T)
+
+        @pl.when(has_beside)
+        def _():
+            greet({"tile": beside, "grp": g})
+
+        loads = {}
+
+        def load(name, src, dst):
             c = pltpu.make_async_copy(src, dst, sems.at[sem_block(1)])
             c.start()
-            loads.append(c)
-
-        for src, dst in (
-            (feat_h, feat), (geof_h, geof), (send_h, send), (kin_h, kin), (kb_h, kb), (kmid_h, kmid), (lkf_h, lkf),
-            (slf_h, slf), (parf_h, parf), (geom_h, geom), (geoc_h, geoc), (parm_h, parm), (lkm_h, lkm), (slm_h, slm),
-            (lkc_h, lkc), (slc_h, slc), (cot_h, cot),
-        ):
-            if inside or not any(dst is v for v in (kin, kb, kmid)):
-                load(src, dst)
-        own_lanes = pl.ds(pl.multiple_of(t * NM, NM), NM)
-        load(geom_h.at[:, own_lanes], geom_own)
+            loads[name] = c
+
+        def loaded(*names):
+            for name in names:
+                loads.pop(name).wait()
+
+        if inside:
+            load("kmid", kmid_h, kmid)
+            load("kin", kin_h, kin)
+            load("kb", kb_h, kb)
+        load("feat", feat_h, feat)
+        load("geof", geof_h, geof)
+        load("send", send_h, send)
         if inside:
             for l in range(3):
-                load(kout_h.at[l, core], ownw.at[l])
-        for c in loads:
-            c.wait()
-
+                load(l, kout_h.at[l, core], ownw.at[l])
+        own_lanes = pl.ds(pl.multiple_of(t * NM, NM), NM)
+        for name, src, dst in (
+            ("lkf", lkf_h, lkf), ("slf", slf_h, slf), ("lkm", lkm_h, lkm), ("slm", slm_h, slm),
+            ("own", geom_h.at[:, own_lanes], geom_own), ("lkc", lkc_h, lkc), ("slc", slc_h, slc), ("geom", geom_h, geom),
+            ("geoc", geoc_h, geoc), ("parf", parf_h, parf), ("parm", parm_h, parm), ("cot", cot_h, cot),
+        ):
+            load(name, src, dst)
+
+        if inside:
+            loaded("kmid", "kin", "kb")
+            order = column_order(KW, NG, True)
+            for l in range(3):
+                second = dot(kmid[l].astype(BF), order)
+                first = dot(kin[l].astype(BF), place(6, 128, [(0, 0, 3), (3, 5, 3)]), TN)
+                first = first + dot(kb[l].astype(BF), place(2, 128, [(0, 3, 1), (1, 8, 1)]), TN)
+                if l == 0:
+                    smbuf[ch, core] = jnp.concatenate([second, first], axis=1)
+                else:
+                    smx[l - 1, 0] = second
+                    smx[l - 1, 1] = jnp.concatenate([first, jnp.zeros((8, KW - 128), F32)], axis=1)
+        pl.semaphore_wait(barrier, NCH + has_beside.astype(I32))
+        if inside:
+            sm_a0 = started(Ring(NCH, lambda d: smbuf.at[ch, core], lambda d: smbuf.at[ch, core], chip_dev))
+            s0c = [[started(One(kout_h.at[l, ocore], s0buf.at[l], partner))] for l in range(3)]
+            for l in range(2):
+                s0c[l].append(started(One(smx.at[l, ocore], s0x.at[l], partner)))
+        loaded("feat", "geof", "send")
         n0 = fine.nodes
         extT[:, 0:n0] = (
             dot(place(80, C, [(0, 0, C)]), feat[...]) + dot(place(80, 3, [(C + 5, 0, 3)]), geof[...])
         ).astype(BF)
         tx_s[0] = dot(extT[:, 0:n0], one_hot(send[...], 0, n0)).astype(BF)
+        halo_x = started(Sides(tx_s.at[0], tx_s.at[0], rx_s))
 
         def window(index, start, n, at):
             off = index - start
             return jnp.where(off < 0, off + at + 8, jnp.where(off >= n, off - n + at + 8, off))
 
-        ohp[...] = one_hot(window(parf[...], t * NM, NM, NM), 0, 2 * NM)
-        if inside:
-            order = column_order(KW, NG, True)
-            for l in range(3):
-                second = dot(kmid[l].astype(BF), order)
-                first = dot(kin[l].astype(BF), place(6, 128, [(0, 0, 3), (3, 5, 3)]), TN)
-                first = first + dot(kb[l].astype(BF), place(2, 128, [(0, 3, 1), (1, 8, 1)]), TN)
-                smbuf[l, ch, core] = jnp.concatenate([second, first], axis=1)
-        else:
-            own_copy(kmid_h, smbuf)
+        if not inside:
+            own_copy(kmid_h, smfull)
             own_copy(kout_h, agbuf)
-        pl.semaphore_wait(barrier, total - 1)
-
-        def chip_dev(d):
-            o = lax.rem(ch + d, NCH)
-            return {"tile": (o // NG) * 2 + core, "grp": lax.rem(o, NG)}
-
-        if inside:
-            sm_a0 = started(Ring(NCH, lambda d: smbuf.at[0, ch, core], lambda d: smbuf.at[0, ch, core], chip_dev))
-        halo_x = started(Sides(tx_s.at[0], tx_s.at[0], rx_s))
-        if inside:
-            s0c = [started(One(kout_h.at[l, ocore], s0buf.at[l], partner)) for l in range(3)]
-            sm_a12 = started(Ring(NCH, lambda d: smbuf.at[1:3, ch, core], lambda d: smbuf.at[1:3, ch, core], chip_dev))
 
         ag = [[] for _ in range(3)]
+        wide = (BW, BW, HALF)
 
         def ag_s1(l):
             if not inside:
                 return
-            s0c[l].recv()
+            for c in s0c[l]:
+                c.recv()
             mine, theirs = ownw[l], s0buf[l]
+            if l < 2:
+                mine = jnp.concatenate([mine, smx[l, core]], axis=1)
+                theirs = jnp.concatenate([theirs, s0x[l]], axis=1)
             first = core == 0
-            agbuf[l, core, hi, lo, g] = jnp.concatenate(
+            agbuf[l, core, hi, lo, g, :, 0 : wide[l]] = jnp.concatenate(
                 [jnp.where(first, mine, theirs), jnp.where(first, theirs, mine)], axis=0
             ).astype(BF)
-            c = Ring(
-                H,
-                lambda d: agbuf.at[l, core, hi, lo, g],
-                lambda d: agbuf.at[l, core, hi, lo, g],
-                lambda d: {"tile": tile_of(lax.rem(hi + d, H), lo, core), "grp": g},
-            )
+
+            def part(d):
+                return agbuf.at[ix(l), core, hi, lo, g, :, 0 : wide[l]]
+
+            c = Ring(H, part, part, lambda d: {"tile": tile_of(lax.rem(hi + d, H), lo, core), "grp": g})
             c.start()
             ag[l].append([c])
 
@@ -358,16 +391,16 @@
             ag[l].append(copies)
 
         def ag_s2(l):
-            part = agbuf.at[l, core, :, lo, g]
+            part = agbuf.at[ix(l), core, :, lo, g, :, 0 : wide[l]]
             ag_next(l, One(part, part, xn), One(part, part, yn))
 
         def ag_s3(l):
-            a = agbuf.at[l, core, :, olo, g, :, 0:QH]
-            b = agbuf.at[l, core, :, lo, og, :, QH:HALF]
+            a = agbuf.at[ix(l), core, :, olo, g, :, 0:QH]
+            b = agbuf.at[ix(l), core, :, lo, og, :, QH : wide[l]]
             ag_next(l, One(a, a, yn), One(b, b, xn))
 
         def ag_s4(l):
-            part = agbuf.at[l, core]
+            part = agbuf.at[ix(l), core, :, :, :, :, 0 : wide[l]]
             ag_next(l, One(part, part, partner))
 
         def ag_fin(l):
@@ -378,15 +411,22 @@
                     for c in cs:
                         c.sent()
         def unpack_small(l):
-            block = smbuf[l].reshape(KW, SMW)
-            second = block[:, 0:KW]
+            if not inside:
+                block = smfull[l].reshape(KW, SMW)
+                second, first = block[:, 0:KW], block[:, KW:]
+            elif l == 0:
+                block = smbuf[...].reshape(KW, SMW)
+                second, first = block[:, 0:KW], block[:, KW:]
+            else:
+                second = agbuf[l - 1, 0, :, :, :, :, HALF:BW].reshape(KW, KW).astype(F32)
+                first = agbuf[l - 1, 1, :, :, :, :, HALF : HALF + 128].reshape(KW, 128).astype(F32)
             wbr[l] = second.astype(BF)
             wbT[l] = second.T.astype(BF)
-            waT[l] = block[:, KW : KW + 8].astype(BF)
-            bbc[l] = jnp.broadcast_to(block[:, KW + 8 : KW + 9], (KW, 128))
+            waT[l] = first[:, 0:8].astype(BF)
+            bbc[l] = jnp.broadcast_to(first[:, 8:9], (KW, 128))
 
         mts, qts = (mt0, mt1, mt2), (mt0, qt1, qt2)
-        xss, zss, pks, a2s = (xs0, xs1, xs2), (zs0, zs1, zs2), (pk0, pk1, pk2), (None, as1, as2)
+        xss, zss, pks, a2s = (xs0, xs1, xs2), (zs0, zs1, zs2), (pk0, pk1, pk2), (as0, as1, as2)
 
         def pack_nodes(lv, links, used, geometry):
             k, n = links.shape
@@ -406,32 +446,38 @@
             links = jnp.sum(jnp.where(slot, got[0:k] + got[k : 2 * k], 0.0), axis=0, keepdims=True)
             return links, got[2 * k : 2 * k + 8]
 
-        def take(table, row, lv):
-            rows = lv.chunk
-            if lv.sources == rows:
-                return dot(table[...], one_hot(row, 0, rows))
-            n = lv.sources // rows
-
-            def body(k, acc):
-                start = pl.multiple_of(k * rows, rows)
-                return acc + dot(table[:, pl.ds(start, rows)], one_hot(row, start, rows))
-
-            return lax.fori_loop(0, n, body, jnp.zeros((table.shape[0], LANES), F32))
+        def take(table, row, lv, rows):
+            top, hot = row >> 7, one_hot(row & 127, 0, 128)
+            n = min(lv.parts, 16)
+
+            def some(first):
+                got = dot(table(first, n), hot)
+                acc = jnp.zeros((rows, LANES), F32)
+                for h in range(n):
+                    acc = acc + jnp.where(top == first + h, got[rows * h : rows * (h + 1)], 0.0)
+                return acc
+
+            if n == lv.parts:
+                return some(0)
+            return lax.fori_loop(0, lv.parts // n, lambda k, acc: acc + some(k * n), jnp.zeros((rows, LANES), F32))
 
         def put(acc, values, row, lv):
-            rows = lv.chunk
-            if lv.sources == rows:
-                acc[...] += dot(values, one_hot(row, 0, rows), NT)
+            top, hot = row >> 7, one_hot(row & 127, 0, 128)
+            n = min(lv.parts, 16)
+
+            def some(first):
+                each = [values * jnp.where(top == first + h, 1.0, 0.0).astype(BF) for h in range(n)]
+                acc[pl.ds(first, n)] += dot(jnp.concatenate(each, axis=0), hot, NT).reshape(n, C, 128)
+
+            if n == lv.parts:
+                some(0)
                 return
-            n = lv.sources // rows
 
             def body(k, _):
-                start = pl.multiple_of(k * rows, rows)
-                at = pl.ds(start, rows)
-                acc[:, at] += dot(values, one_hot(row, start, rows), NT)
+                some(k * n)
                 return 0
 
-            lax.fori_loop(0, n, body, 0)
+            lax.fori_loop(0, lv.parts // n, body, 0)
 
         def edge_geometry(lv, x_table, g_table, first, last):
             l = lv.index
@@ -440,11 +486,11 @@
                 links, z = edge_columns(lv, i)
                 row = links.astype(I32)
                 if g_table is None:
-                    got = take(x_table, row, lv)
+                    got = dot(x_table[...], one_hot(row, 0, lv.sources))
                     xss[l][i] = got[0:C].astype(BF)
                     z = z + got[C : C + 8]
                 else:
-                    z = z + take(g_table, row, lv)[0:8]
+                    z = z + take(g_table, row, lv, 8)
                 zss[l][i] = jnp.where(iota((8, LANES), 0) == 4, links, z)
                 return 0
 
@@ -465,26 +511,34 @@
 
             lax.fori_loop(0, lv.steps, body, 0)
 
-        def edges_forward(lv, x_table, first, last):
+        def at_step(i, events):
+            for when, call in events:
+
+                @pl.when(i == when)
+                def _():
+                    call()
+
+        def edges_forward(lv, x_table, events=()):
             l = lv.index
             mask = group_mask(lv.width)
 
             def body(i, _):
+                at_step(i, events)
                 if x_table is None:
                     x = xss[l][i].astype(F32)
                     a2 = hidden(l, zss[l][i])
+                    a2s[l][i] = a2
                 else:
-                    x = take(x_table, zss[l][i, 4:5, :].astype(I32), lv)
+                    x = take(x_table, zss[l][i, 4:5, :].astype(I32), lv, C)
                     xss[l][i] = x.astype(BF)
                     a2 = a2s[l][i]
                 for k in range(lv.blocks):
                     sl = slice(lv.width * k, lv.width * (k + 1))
                     m = dot(spread(x[:, sl], mask), a2[:, sl], NT)
-                    at = pl.ds(pl.multiple_of((lv.blocks * i + k) * GROUP, GROUP), GROUP)
-                    mts[l][:, at, :] = m.astype(BF).reshape(C, GROUP, KW)
+                    mts[l][:, lv.blocks * i + k] = m.astype(BF).reshape(C // 2, 2 * GROUP, KW)
                 return 0
 
-            lax.fori_loop(first, last, body, 0)
+            lax.fori_loop(0, lv.steps, body, 0)
 
         def third(l, pair):
             per_half = C // 4
@@ -492,62 +546,86 @@
             return agbuf[l, half, :, :, :, :, pl.ds(pl.multiple_of(k * 128, 128), 128)].reshape(KW, 2 * C)
 
         def node_sums(lv):
-            l = lv.index
+            l, n = lv.index, lv.nodes
             each = 4
 
-            def body(i, accs):
+            def body(i, acc):
                 w = jnp.concatenate([third(l, each * i + u) for u in range(each)], axis=0)
-                out = []
-                for odd in range(2):
-                    m = jnp.concatenate([mts[l][2 * (each * i + u) + odd] for u in range(each)], axis=1)
-                    out.append(accs[odd] + dot(m, w))
-                return tuple(out)
-
-            zero = jnp.zeros((lv.nodes, 2 * C), F32)
-            even, odd = lax.fori_loop(0, C // 2 // each, body, (zero, zero))
-            return even.T[0:C] + odd.T[C:]
-
-        stage = (gbuf, agbuf.at[1], agbuf.at[2])
-
-        def third_grad(lv, gsT):
+                m = jnp.concatenate([mts[l][each * i + u].reshape(2 * n, KW) for u in range(each)], axis=1)
+                return acc + dot(m, w)
+
+            acc = lax.fori_loop(0, C // 2 // each, body, jnp.zeros((2 * n, 2 * C), F32))
+            acc = acc.reshape(n // GROUP, 2, GROUP, 2 * C)
+            both = acc[:, 0].reshape(n, 2 * C) + pltpu.roll(acc[:, 1].reshape(n, 2 * C), C, 1)
+            return both.T[0:C]
+
+        def by_parity(lv, gsT):
+            n = lv.nodes
+            gsT = gsT.astype(F32)
+            even = jnp.concatenate([gsT, jnp.zeros(gsT.shape, F32)], axis=0).T[0:n]
+            odd = pltpu.roll(even, C, 1)
+            shape = (n // GROUP, 1, GROUP, 2 * C)
+            return jnp.concatenate([even.reshape(shape), odd.reshape(shape)], axis=1).reshape(2 * n, 2 * C)
+
+        def stage(l):
+            return agbuf.at[ix(l), :, :, :, :, :, 0:HALF] if l else gbuf
+
+        def third_grad(lv, gs):
             l = lv.index
             n = C // 4
             each = 4
+            turned = gs.T.astype(BF)
 
             def body(j, _):
                 for u in range(each):
                     i = each * j + u
-                    both = jnp.concatenate([dot(gsT, mts[l][2 * i]), dot(gsT, mts[l][2 * i + 1])], axis=0)
+                    both = dot(turned, mts[l][i].reshape(2 * lv.nodes, KW))
                     out = both.T.astype(BF).reshape(A, 2, NG, 16, 128)
-                    stage[l][i // n, :, :, :, :, pl.ds(pl.multiple_of(lax.rem(i, n) * 128, 128), 128)] = out
+                    stage(l)[i // n, :, :, :, :, pl.ds(pl.multiple_of(lax.rem(i, n) * 128, 128), 128)] = out
                 return 0
 
             lax.fori_loop(0, C // 2 // each, body, 0)
 
-        def node_weights(lv, gsT):
+        def node_weights(lv, gs):
             l = lv.index
             each = 4
-            gsT = gsT.astype(F32)
-            zero = jnp.zeros(gsT.shape, F32)
-            low = jnp.concatenate([gsT, zero], axis=0).T[0 : lv.nodes].astype(BF)
-            high = jnp.concatenate([zero, gsT], axis=0).T[0 : lv.nodes].astype(BF)
+            gs = gs.astype(BF)
 
             def body(j, _):
                 for u in range(each):
-                    w = third(l, each * j + u)
-                    c = 2 * (each * j + u)
-                    qts[l][c] = dot(low, w, NT).astype(BF)
-                    qts[l][c + 1] = dot(high, w, NT).astype(BF)
+                    i = each * j + u
+                    q = dot(gs, third(l, i), NT)
+                    qts[l][i] = q.astype(BF).reshape(lv.nodes // GROUP, 2 * GROUP, KW)
                 return 0
 
             lax.fori_loop(0, C // 2 // each, body, 0)
 
-        def edges_backward(lv, acc, first, last):
+        def source_grads(lv, acc, events=()):
             l = lv.index
             mask = group_mask(lv.width)
             fold = (iota((C, C * GROUP), 1) >> log2(GROUP) == iota((C, C * GROUP), 0)).astype(F32).astype(BF)
 
             def body(i, _):
+                at_step(i, events)
+                gxs = []
+                for k in range(lv.blocks):
+                    sl = slice(lv.width * k, lv.width * (k + 1))
+                    q = qts[l][:, lv.blocks * i + k].reshape(C * GROUP, KW)
+                    every = dot(q, a2s[l][i, :, sl])
+                    own = (every.reshape(C, GROUP, lv.width) * mask[None]).reshape(C * GROUP, lv.width).astype(BF)
+                    gxs.append(own)
+                gx = dot(fold, jnp.concatenate(gxs, axis=1)).astype(BF)
+                put(acc, gx, zss[l][i, 4:5, :].astype(I32), lv)
+                return 0
+
+            lax.fori_loop(0, lv.steps, body, 0)
+
+        def weight_grads(lv, first, last, events=()):
+            l = lv.index
+            mask = group_mask(lv.width)
+
+            def body(i, _):
+                at_step(i, events)
                 zb = zss[l][i].astype(BF)
                 t1 = dot(waT[l], zb)
                 s1 = sig(t1)
@@ -556,21 +634,14 @@
                 a1 = f1.astype(BF)
                 t2 = dot(wbT[l], a1) + bbc[l][:, 0:1]
                 s2 = sig(t2)
-                f2 = t2 * s2
-                d2 = s2 + f2 * (1.0 - s2)
-                a2 = f2.astype(BF)
+                d2 = s2 + t2 * s2 * (1.0 - s2)
                 x = xss[l][i].astype(F32)
-                g2s, gxs = [], []
+                g2s = []
                 for k in range(lv.blocks):
                     sl = slice(lv.width * k, lv.width * (k + 1))
-                    at = pl.ds(pl.multiple_of((lv.blocks * i + k) * GROUP, GROUP), GROUP)
-                    q = qts[l][:, at, :].reshape(C * GROUP, KW)
+                    q = qts[l][:, lv.blocks * i + k].reshape(C * GROUP, KW)
                     g2s.append((dot(q, spread(x[:, sl], mask), TN) * d2[:, sl]).astype(BF))
-                    every = dot(q, a2[:, sl])
-                    own = (every.reshape(C, GROUP, lv.width) * mask[None]).reshape(C * GROUP, lv.width).astype(BF)
-                    gxs.append(dot(fold, own).astype(BF))
                 g2 = jnp.concatenate(g2s, axis=1)
-                gx = jnp.concatenate(gxs, axis=1)
                 g1 = (dot(wbr[l], g2) * d1).astype(BF)
                 sm2 = dot(a1, g2, NT)
                 p1 = dot(g1, zb, NT)
@@ -578,7 +649,6 @@
                 gsb[l, :, :, :, 0:KW] += sm2.reshape(NB, 2, 8, KW)
                 gsb[l, :, :, :, KW : KW + 8] += p1.reshape(NB, 2, 8, 8)
                 gsb[l, :, :, :, KW + 8 : KW + 16] += p2.reshape(NB, 2, 8, 8)
-                put(acc, gx, zss[l][i, 4:5, :].astype(I32), lv)
                 return 0
 
             lax.fori_loop(first, last, body, 0)
@@ -597,11 +667,22 @@
             b = pltpu.roll(from_right, (n_own - 8 - left_at) % 128, 1)
             return jnp.where(lane < 8, a, 0.0) + jnp.where((lane >= n_own - 8) & (lane < n_own), b, 0.0)
 
+        if inside:
+            loaded(0, 1, 2)
         ag_s1(0)
+        loaded("lkf", "slf", "parf")
+        pack_nodes(fine, lkf[...], slf[...], geof[...])
+        ohp[...] = one_hot(window(parf[...], t * NM, NM, NM), 0, 2 * NM)
         halo_x.recv()
         near, far = (pltpu.roll(rx_s[k].astype(F32), halo, 1) for k in (0, 1))
         extT[:, n0:] = jnp.where(iota((1, 128), 1) < halo, near, far).astype(BF)
-        pack_nodes(fine, lkf[...], slf[...], geof[...])
+        edge_geometry(fine, extT, None, 0, fine.steps)
+        if inside:
+            sm_a0.recv()
+            sm_b0 = started(One(smbuf.at[:, core], smbuf.at[:, core], partner))
+        ag_s2(0)
+        ag_s1(1)
+        loaded("lkm", "slm", "own", "lkc", "slc", "geom", "geoc", "parm", "cot")
         pack_nodes(mid, lkm[...], slm[...], geom_own[...])
         lkc_wide[...] = jnp.zeros(lkc_wide.shape, F32)
         lkc_wide[0:NC] = lkc[...].astype(F32)
@@ -615,9 +696,11 @@
         own_c = jnp.where(lanes < NC, t * NC + lanes, -1)
         geo = dot(geoc[...], one_hot(own_c, 0, coarse.sources)).astype(BF)
         pack_nodes(coarse, turned, jnp.where(lanes < NC, slc_wide[...], 0), geo)
-        to_rows = place(16, 3, [(5, 0, 3)])
-        gm[...] = dot(to_rows, geom[...]).astype(BF)
-        gc[...] = dot(to_rows, geoc[...]).astype(BF)
+        to_rows = place(8, 3, [(5, 0, 3)])
+        for table, source, lv in ((gm, geom, mid), (gc, geoc, coarse)):
+            rows = dot(to_rows, source[...])
+            for k in range(lv.parts):
+                table[k] = rows[:, 128 * k : 128 * (k + 1)]
         nf, nm, nc = (v[...].astype(F32) for v in (slf, slm, slc_wide))
         blocks = [parm[:, pl.ds(pl.multiple_of(b * NM, NM), NM)].astype(F32)
                   for b in (jnp.maximum(t - 1, 0), t, jnp.minimum(t + 1, T - 1))]
@@ -625,31 +708,16 @@
         sides = jnp.where((lanes < 8) & (t > 0), before, jnp.where((lanes >= 8) & (lanes < 16) & (t < T - 1), after, -1.0))
         around = jnp.concatenate([blocks[1], sides], axis=1).astype(I32)
         pw = jnp.where(around < 0, -1, window(around, t * NC, NC, NC))
-        edge_geometry(fine, extT, None, 0, fine.steps)
-        edge_geometry(mid, None, gm, 0, mid.steps)
-        edge_geometry(coarse, None, gc, 0, coarse.steps)
         if inside:
-            sm_a0.recv()
-            sm_b0 = started(One(smbuf.at[0, :, core], smbuf.at[0, :, core], partner))
-            ag_s2(0)
-            sm_a12.recv()
-            sm_b12 = started(One(smbuf.at[1:3, :, core], smbuf.at[1:3, :, core], partner))
             sm_b0.recv()
         unpack_small(0)
-        n = fine.steps
-        quarter = n // 4
-        cuts = (0, n // 4, n // 2, 3 * n // 4, n)
-        edges_forward(fine, None, cuts[0], cuts[1])
-        ag_s1(1)
-        edges_forward(fine, None, cuts[1], cuts[2])
-        ag_s3(0)
-        ag_s2(1)
-        ag_s1(2)
-        edges_forward(fine, None, cuts[2], cuts[3])
-        ag_s4(0)
-        edges_forward(fine, None, cuts[3], cuts[4])
-        ag_s3(1)
-        ag_s2(2)
+        edges_forward(
+            fine, None,
+            [(8, lambda: ag_s3(0)), (8, lambda: ag_s1(2)), (12, lambda: ag_s4(0)), (12, lambda: ag_s2(1))],
+        )
+        g_rows = lambda table: lambda first, n: table[pl.ds(first, n)].reshape(n * 8, 128).astype(BF)
+        edge_geometry(mid, None, g_rows(gm), 0, mid.steps)
+        edge_geometry(coarse, None, g_rows(gc), 0, coarse.steps)
         ag_fin(0)
         v0 = extT[0:C, 0 : fine.nodes].astype(F32) + node_sums(fine) / nf
         v0s[...] = v0
@@ -659,10 +727,8 @@
         sums = jnp.concatenate([join3(part[0 : 3 * C]), part[3 * C :]], axis=0)
         tx_w[0] = sums[:, NM:]
         ex_w = started(Sides(tx_w.at[0], tx_w.at[0], rx_w))
-        if inside:
-            sm_b12.recv()
         unpack_small(1)
-        ag_s4(1)
+        ag_s3(1)
         ex_w.recv()
         own = sums[:, 0:NM] + margin_pick(rx_w[0], rx_w[1], NM, 0, 8)
         inv1 = 1.0 / jnp.maximum(own[C : C + 1], 1.0)
@@ -673,17 +739,19 @@
             return Ring(R, src, dst, lambda d: {"tile": lax.rem(r + d, R) * 2 + core, "grp": g})
 
         ag1 = started(chip_ring(lambda d: x1b.at[r, core], lambda d: x1b.at[r, core]))
+        ag_s2(2)
         edge_hidden(mid)
-        ag_s3(2)
+        ag_s4(1)
         ag1.recv()
         ag1p = started(One(x1b.at[:, core], x1b.at[:, core], partner))
+        ag1p.recv()
+
+        def x1_rows(first, n):
+            return x1b[pl.ds(first // 2, n // 2)].reshape(n * C, 128)
+
+        edges_forward(mid, x1_rows, [(4, lambda: ag_s3(2))])
+        ag_fin(1)
         unpack_small(2)
-        ag1p.recv()
-        for k in range(T):
-            x1T[:, NM * k : NM * (k + 1)] = x1b[k // 2, k % 2]
-
-        edges_forward(mid, x1T, 0, mid.steps)
-        ag_fin(1)
         w1 = v1 + node_sums(mid) / nm
         tx_q[0, 0:C] = w1
         ohq = one_hot(pw, 0, 128)
@@ -714,8 +782,8 @@
                 block = block + pltpu.roll(x2b[(per * k + u) // 2, (per * k + u) % 2].astype(F32), NC * u, 1)
             cols.append(block.astype(BF))
         for k, block in enumerate(cols):
-            x2T[:, 128 * k : 128 * k + 128] = block
-        edges_forward(coarse, x2T, 0, coarse.steps)
+            x2T[k] = block
+        edges_forward(coarse, lambda first, n: x2T[pl.ds(first, n)].reshape(n * C, 128))
         ag_fin(2)
         sc = node_sums(coarse)
         sc = jnp.concatenate([sc, jnp.zeros((C, 128 - NC), F32)], axis=1)
@@ -755,45 +823,45 @@
             rs[l].append(copies)
 
         def rs_s0(l):
-            rs_step(l, lambda: None, One(stage[l].at[ocore], rsr0.at[l], partner))
+            rs_step(l, lambda: None, One(stage(l).at[ocore], rsr0.at[ix(l % 2)], partner))
 
         def rs_s1(l):
             def fix():
                 def body(i, _):
-                    both = stage[l][core, i].astype(F32) + rsr0[l, i].astype(F32)
-                    stage[l][core, i] = both.astype(BF)
+                    both = stage(l)[core, i].astype(F32) + rsr0[l % 2, i].astype(F32)
+                    stage(l)[core, i] = both.astype(BF)
                     return 0
 
                 lax.fori_loop(0, H, body, 0)
 
             rs_step(
                 l, fix,
-                One(stage[l].at[core, :, olo, og, :, 0:QH], rsr1.at[l, 0], xn),
-                One(stage[l].at[core, :, olo, og, :, QH:HALF], rsr1.at[l, 1], yn),
+                One(stage(l).at[core, :, olo, og, :, 0:QH], rsr1.at[ix(l), ix(0)], xn),
+                One(stage(l).at[core, :, olo, og, :, QH:HALF], rsr1.at[ix(l), ix(1)], yn),
             )
 
         def rs_s2(l):
             def fix():
                 def body(i, _):
-                    a = stage[l][core, i, lo, og, :, 0:QH].astype(F32) + rsr1[l, 0, i].astype(F32)
-                    stage[l][core, i, lo, og, :, 0:QH] = a.astype(BF)
-                    b = stage[l][core, i, olo, g, :, QH:HALF].astype(F32) + rsr1[l, 1, i].astype(F32)
-                    stage[l][core, i, olo, g, :, QH:HALF] = b.astype(BF)
+                    a = stage(l)[core, i, lo, og, :, 0:QH].astype(F32) + rsr1[l, 0, i].astype(F32)
+                    stage(l)[core, i, lo, og, :, 0:QH] = a.astype(BF)
+                    b = stage(l)[core, i, olo, g, :, QH:HALF].astype(F32) + rsr1[l, 1, i].astype(F32)
+                    stage(l)[core, i, olo, g, :, QH:HALF] = b.astype(BF)
                     return 0
 
                 lax.fori_loop(0, H, body, 0)
 
             rs_step(
                 l, fix,
-                One(stage[l].at[core, :, lo, og], rsr2.at[l, 0], yn),
-                One(stage[l].at[core, :, olo, g], rsr2.at[l, 1], xn),
+                One(stage(l).at[core, :, lo, og], rsr2.at[ix(l), ix(0)], yn),
+                One(stage(l).at[core, :, olo, g], rsr2.at[ix(l), ix(1)], xn),
             )
 
         def rs_s3(l):
             def fix():
                 def body(i, _):
-                    a = stage[l][core, i, lo, g].astype(F32) + rsr2[l, 0, i].astype(F32) + rsr2[l, 1, i].astype(F32)
-                    stage[l][core, i, lo, g] = a.astype(BF)
+                    a = stage(l)[core, i, lo, g].astype(F32) + rsr2[l, 0, i].astype(F32) + rsr2[l, 1, i].astype(F32)
+                    stage(l)[core, i, lo, g] = a.astype(BF)
                     return 0
 
                 lax.fori_loop(0, H, body, 0)
@@ -802,25 +870,25 @@
                 l, fix,
                 Ring(
                     H,
-                    lambda d: stage[l].at[core, lax.rem(hi + d, H), lo, g],
-                    lambda d: rsr3.at[l, d - 1],
+                    lambda d: stage(l).at[core, lax.rem(hi + d, H), lo, g],
+                    lambda d: rsr3.at[ix(l), d - 1],
                     lambda d: {"tile": tile_of(lax.rem(hi + d, H), lo, core), "grp": g},
                 ),
             )
 
         def rs_s4(l):
             def fix():
-                tot = stage[l][core, hi, lo, g].astype(F32)
+                tot = stage(l)[core, hi, lo, g].astype(F32)
                 for k in range(H - 1):
                     tot = tot + rsr3[l, k].astype(F32)
                 rsf[l, 0] = tot[0:8]
                 rsf[l, 1] = tot[8:16]
 
-            rs_step(l, fix, One(rsf.at[l, ocore], rsr4.at[l], partner))
+            rs_step(l, fix, One(rsf.at[ix(l), ocore], rsr4.at[ix(l)], partner))
 
         def rs_s5(l):
             if not inside:
-                own_copy(stage[l], gwc.at[l])
+                own_copy(stage(l), gwc.at[l])
                 return
             for c in rs[l][-1]:
                 c.recv()
@@ -861,17 +929,21 @@
 
 
         gs2T = jnp.where(mine, gw2 / nc, 0.0).astype(BF)
-        node_weights(coarse, gs2T)
+        gs2 = by_parity(coarse, gs2T)
+        node_weights(coarse, gs2)
         acc2[...] = jnp.zeros(acc2.shape, F32)
-        edges_backward(coarse, acc2, 0, coarse.steps)
-        a2rows = jnp.concatenate([acc2[...], jnp.zeros(acc2.shape, F32)], axis=0)
-        acc2b[...] = a2rows.T.astype(BF).reshape(R, 2, NC, 128)
+        source_grads(coarse, acc2)
+        zero = jnp.zeros((C, 128), F32)
+        for k in range(coarse.parts):
+            rows = jnp.concatenate([acc2[k], zero], axis=0).T.astype(BF)
+            acc2b[per // 2 * k : per // 2 * (k + 1)] = rows.reshape(per // 2, 2, NC, 128)
         r2p = started(One(acc2b.at[:, ocore], rs2a, partner))
-        third_grad(coarse, gs2T[:, 0:NC])
+        weight_grads(coarse, 0, 1)
         r2p.recv()
         acc2b[:, core] = (acc2b[:, core].astype(F32) + rs2a[...].astype(F32)).astype(BF)
         r2 = started(chip_ring(lambda d: acc2b.at[lax.rem(r + d, R), core], lambda d: rs2buf.at[d - 1]))
-        rs_s0(2)
+        weight_grads(coarse, 1, coarse.steps)
+        third_grad(coarse, gs2)
         r2.recv()
 
         def add2(k, acc):
@@ -882,24 +954,26 @@
         gv2 = jnp.where(mine, (gw2 + own2) / cnt2, 0.0)
         tx_b[0] = gv2
         ex_b = started(Sides(tx_b.at[0], tx_b.at[0], rx_b))
-        rs_s1(2)
+        rs_s0(2)
         ex_b.recv()
         gv2win = gv2 + roll_pick(rx_b[0], rx_b[1], NC, NC, NC + 8)
         gw1 = gy1 + join3(dot(split3(gv2win), ohq[:, 0:NM]))
 
         gs1T = (gw1 / nm).astype(BF)
-        node_weights(mid, gs1T)
+        gs1 = by_parity(mid, gs1T)
+        node_weights(mid, gs1)
         acc1[...] = jnp.zeros(acc1.shape, F32)
-        edges_backward(mid, acc1, 0, mid.steps)
-        for k in range(T):
-            acc1b[k // 2, k % 2] = acc1[:, NM * k : NM * (k + 1)].astype(BF)
+        rs_s1(2)
+        source_grads(mid, acc1, [(5, lambda: rs_s2(2))])
+        acc1b[...] = acc1[...].astype(BF).reshape(acc1b.shape)
         r1p = started(One(acc1b.at[:, ocore], rs1a, partner))
-        rs_s2(2)
+        half = mid.steps // 2
+        third_grad(mid, gs1)
         r1p.recv()
         acc1b[:, core] = (acc1b[:, core].astype(F32) + rs1a[...].astype(F32)).astype(BF)
         r1 = started(chip_ring(lambda d: acc1b.at[lax.rem(r + d, R), core], lambda d: rs1buf.at[d - 1]))
-        third_grad(mid, gs1T)
         rs_s0(1)
+        weight_grads(mid, 0, half)
         r1.recv()
 
         def add1(k, acc):
@@ -909,8 +983,9 @@
         gv1 = (gw1 + own1) * inv1
         tx_f[0] = gv1
         ex_f = started(Sides(tx_f.at[0], tx_f.at[0], rx_f))
-        gs_start(1, 3)
         rs_s1(1)
+        rs_s3(2)
+        weight_grads(mid, half, mid.steps)
         ex_f.recv()
         gv1win = jnp.concatenate([gv1, roll_pick(rx_f[0], rx_f[1], NM, 0, 8)], axis=1)
         gv0 = gys[...] + join3(dot(split3(gv1win), ohp[...]))
@@ -918,41 +993,35 @@
 
         gs0 = gv0 / nf
         gs0T = gs0.astype(BF)
-        third_grad(fine, gs0T)
+        gs0 = by_parity(fine, gs0T)
+        rs_s2(1)
+        third_grad(fine, gs0)
         rs_s0(0)
-        rs_s3(2)
-        rs_s2(1)
-        node_weights(fine, gs0T)
-        acc0[...] = jnp.zeros(acc0.shape, F32)
+        node_weights(fine, gs0)
         rs_s1(0)
-        gs_ring(1, 3)
-        edges_backward(fine, acc0, cuts[0], cuts[1])
-        rs_s2(0)
         rs_s3(1)
         rs_s4(2)
-        edges_backward(fine, acc0, cuts[1], cuts[2])
-        rs_s3(0)
-        rs_s4(1)
-        rs_s5(2)
-        edges_backward(fine, acc0, cuts[2], cuts[3])
-        rs_s4(0)
-        rs_s5(1)
-        gs_end(1, 3)
-        edges_backward(fine, acc0, cuts[3], cuts[4])
-        tx_h[0] = acc0[:, fine.nodes : fine.nodes + 2 * halo]
+        weight_grads(
+            fine, 0, fine.steps,
+            [(1, lambda: gs_start(1, 3)), (5, lambda: rs_s2(0)), (6, lambda: rs_s4(1)), (7, lambda: rs_s5(2)),
+             (8, lambda: gs_ring(1, 3)), (9, lambda: rs_s5(1)), (13, lambda: rs_s3(0))],
+        )
+        gs_start(0, 1)
+        acc0[...] = jnp.zeros(acc0.shape, F32)
+        source_grads(
+            fine, acc0, [(2, lambda: gs_ring(0, 1)), (6, lambda: gs_end(1, 3)), (12, lambda: rs_s4(0))]
+        )
+        tx_h[0] = acc0[fine.parts - 1]
         ex_h = started(Sides(tx_h.at[0], tx_h.at[0], rx_h))
-
-        gs_start(0, 1)
         rs_s5(0)
+        gs_end(0, 1)
         ex_h.recv()
         lane1 = iota((1, 128), 1)
         back = jnp.where(lane1 < halo, pltpu.roll(rx_h[0], halo, 1), pltpu.roll(rx_h[1], halo, 1))
         ohs2 = one_hot(send[...], 0, n0)
-        gf = gys[...] + acc0[:, 0 : fine.nodes] + join3(dot(split3(back), ohs2, NT))
+        own0 = jnp.concatenate([acc0[k] for k in range(fine.parts - 1)], axis=1)
+        gf = gys[...] + own0 + join3(dot(split3(back), ohs2, NT))
         gradf[...] = gf.astype(BF)
-        gs_ring(0, 1)
-        gs_end(0, 1)
-
         finish()
 
     n_sems = (
@@ -961,6 +1030,7 @@
     )
     V = pltpu.VMEM
     ls = 3 if inside else 1
+    by_group = lambda n: V((C // 2, n // GROUP, 2 * GROUP, KW), BF)
     nf, nm_, nc_ = fine.nodes, NM, NC
     scratch = [
         V((C, nf), BF), V((C, nf), F32), V((3, nf), BF), V((3, mid.sources), BF), V((3, coarse.sources), BF),
@@ -968,12 +1038,13 @@
         V((mid.slots, nm_), I32), V((1, nm_), I32), V((nc_, coarse.slots), I32), V((1, nc_), I32),
         V((3, 6, 8), F32), V((3, 2, 8), F32), V((3, 8, KW), F32), V((ls, 8, HALF), F32),
         V((3, nm_), BF), V((128, coarse.slots), F32), V((1, 128), I32),
-        V((nf, 128), BF), V((nm_, 128), BF), V((128, 128), BF), V((16, mid.sources), BF), V((16, coarse.sources), BF),
+        V((nf, 128), BF), V((nm_, 128), BF), V((128, 128), BF), V((mid.parts, 8, 128), F32), V((coarse.parts, 8, 128), F32),
         V((80, nf + 2 * halo), BF),
-        V((3, 2, A, 2, NG, 16, HALF), BF), V((2, A, 2, NG, 16, HALF), BF), V((ls, 8, HALF), F32),
-        V((3, NB, 2, 8, SMW), F32), V((3, KW, 8), BF), V((3, KW, KW), BF), V((3, KW, KW), BF), V((3, KW, 128), F32),
-        V((C, nf, KW), BF), V((C, nm_, KW), BF), V((C, nc_, KW), BF), V((C, nm_, KW), BF), V((C, nc_, KW), BF),
-        V((mid.steps, KW, LANES), BF), V((coarse.steps, KW, LANES), BF),
+        V((3, 2, A, 2, NG, 16, BW if inside else HALF), BF), V((2, A, 2, NG, 16, HALF), BF), V((ls, 8, HALF), F32),
+        V((2, 8, KW), F32), V((2, 2, 8, KW), F32),
+        V((NB, 2, 8, SMW), F32), V((1 if inside else 3, 1 if inside else NB, 2, 8, SMW), F32), V((3, KW, 8), BF), V((3, KW, KW), BF), V((3, KW, KW), BF), V((3, KW, 128), F32),
+        by_group(nf), by_group(nm_), by_group(nc_), by_group(nm_), by_group(nc_),
+        V((fine.steps, KW, LANES), BF), V((mid.steps, KW, LANES), BF), V((coarse.steps, KW, LANES), BF),
         V((fine.steps, C, LANES), BF), V((mid.steps, C, LANES), BF), V((coarse.steps, C, LANES), BF),
         V((fine.steps, 8, LANES), F32), V((mid.steps, 8, LANES), F32), V((coarse.steps, 8, LANES), F32),
         V((2 * NM, nf), BF),
@@ -985,11 +1056,11 @@
         V((1, C, 128), F32), V((2, C, 128), F32),
         V((1, C, 128), F32), V((2, C, 128), F32),
         V((1, C, 128), F32), V((2, C, 128), F32),
-        V((C, mid.sources), BF), V((R, 2, C, 128), BF), V((C, coarse.sources), BF), V((R, 2, C, 128), BF),
-        V((C, nf + 2 * halo), F32), V((C, mid.sources), F32), V((C, coarse.sources), F32),
+        V((R, 2, C, 128), BF), V((coarse.parts, C, 128), BF), V((R, 2, C, 128), BF),
+        V((fine.parts, C, 128), F32), V((mid.parts, C, 128), F32), V((coarse.parts, C, 128), F32),
         V((R, 2, C, 128), BF), V((R, 2, NC, 128), BF), V((R, C, 128), BF), V((R, NC, 128), BF),
         V((R - 1, C, 128), BF), V((R - 1, NC, 128), BF), V((C, nf), F32), V((C, nf), F32),
-        V((ls, A, 2, NG, 16, HALF), BF), V((ls, 2, A, 16, QH), BF), V((ls, 2, A, 16, HALF), BF),
+        V((min(ls, 2), A, 2, NG, 16, HALF), BF), V((ls, 2, A, 16, QH), BF), V((ls, 2, A, 16, HALF), BF),
         V((ls, A - 1, 16, HALF), BF), V((ls, 2, 8, HALF), F32), V((ls, 8, HALF), F32),
         V((3, NB, 2, 8, SMW), F32), V((ls, NB, 8, SMW), F32), V((NB - 1, 3, 8, SMW), F32),
         pltpu.SemaphoreType.DMA((n_sems,)),
@@ -1012,7 +1083,10 @@
     rates = (RATE_FIRST, RATE_MAIN, RATE_MAIN, RATE_MAIN)
 
     def kernel(*refs):
-        far_in, far_out, near_in, near_out, sems = refs[0:14], refs[14:26], refs[26:40], refs[40:52], refs[52]
+        far_in, far_out, near_in, near_out, sems = refs[0:14], refs[16:28], refs[30:44], refs[44:56], refs[56]
+        out = [pltpu.make_async_copy(refs[14 + k], refs[28 + k], sems.at[26 + k]) for k in range(2)]
+        for c in out:
+            c.start()
         copies = [pltpu.make_async_copy(a, b, sems.at[k]) for k, (a, b) in enumerate(zip(far_in, near_in))]
         for c in copies:
             c.start()
@@ -1020,7 +1094,6 @@
             c.wait()
         gwc, gsmall = near_in[0:2]
         order = column_order(KW, NG, False)
-        out = []
 
         def update(k, index, grad):
             new = adamw(*(near_in[2 + 4 * m + k][index] for m in range(3)), grad, rates[k])
@@ -1116,15 +1189,15 @@
     state = (kernel_in, kernel_bias, kernel_mid, kernel_out) + moments
     new = pl.pallas_call(
         make_update(KW, NG, per, inside),
-        out_shape=tuple(S(v.shape, F32) for v in state),
-        in_specs=[far] * 14,
-        out_specs=(far,) * 12,
+        out_shape=tuple(S(v.shape, F32) for v in state) + (S((C, nf), BF),) * 2,
+        in_specs=[far] * 16,
+        out_specs=(far,) * 14,
         scratch_shapes=[pltpu.VMEM(v.shape, F32) for v in (gwc, gsmall) + state]
-        + [pltpu.VMEM(v.shape, F32) for v in state] + [pltpu.SemaphoreType.DMA((26,))],
+        + [pltpu.VMEM(v.shape, F32) for v in state] + [pltpu.SemaphoreType.DMA((28,))],
         compiler_params=pltpu.CompilerParams(vmem_limit_bytes=63 << 20),
         name="update",
-    )(gwc, gsmall, *state)
-    return (layer.swapaxes(0, 1)[None], gradf.swapaxes(0, 1)[None]) + tuple(new)
+    )(gwc, gsmall, *state, layer, gradf)
+    return tuple(v.swapaxes(0, 1)[None] for v in new[12:]) + tuple(new[:12])
 
 
 def solution(mesh):

time: 221 us -> 188 us (0.85)
  Pallas kernels: 211 us -> 181 us
    pallas_call x1, Pallas kernels: 208 us -> 175 us  [per_device(): pl.pallas_call(kernel, out_shape=(S((C, nf), BF), S((C, nf), BF), S((3, 2...]
where the time goes in v3:
time: 188 us; the launch traced here: 187 us
  Pallas kernels  181 us (96%)
  local copies, waits for them, and re-layouts  6.03 us (3%)
    pallas_call x1, Pallas kernels, per_device(): pl.pallas_call(kernel, out_shape=(S((C, nf), BF), S((C, nf), BF), S((3, 2...  175 us
    pallas_call x1, Pallas kernels, per_device(): pl.pallas_call(make_update(KW, NG, per, inside), out_shape=tuple((S(v.sha...  5.34 us

profile of v3, /device:TPU:1, one launch (start us, length us, event | category | flops | bytes accessed | tf_op | source)
XLA Modules:
  0.0 187.4 jit_solution(6435495144082182627)
XLA Ops:
  0.6 1.3 reshape.40
  2.0 0.3 copy.40
  2.2 0.4 reshape.41
  2.6 1.0 copy.45
  3.6 175.2 %layer.1 = (bf16[64,512]{1,0:T(8,128)(2,1)}, bf16[64,512]{1,0:T(8,128)(2,1)}, f32[3,2,8,2048]{3,2,1,0:T(8,128)}, f32[3,8,384]{2,1,0:T(8,128)}) custom-call(bf16[64,512]{1,0:T(8,128)(2,1)} %bitcast.45, f32[64,512]{1,0:T(8,128)} %bitcast.44, bf16[3,512]{1,0:T(4,128)(2,1)} %bitcast.50, bf16[3,2048]{1,0:T(4,128)(2,1)} %bitcast.47, bf16[3,512]{1,0:T(4,128)(2,1)} %bitcast.51, ...), custom_call_target="tpu_custom_call" | custom-call | tf_op jit(solution)/shard_map/layer/pallas_call | solution.py:1172
  178.8 1.3 copy.42
  180.1 0.5 reshape.42
  180.6 0.3 copy.43
  180.9 1.0 reshape.43.refs_0_
  181.9 5.3 %update.1 = (f32[3,6,8]{2,1,0:T(8,128)}, f32[3,2,8]{2,1,0:T(2,128)}, f32[3,8,256]{2,1,0:T(8,128)}, f32[3,8,4096]{2,1,0:T(8,128)}, f32[3,6,8]{2,1,0:T(8,128)}, /*...) custom-call(f32[3,8,4096]{2,1,0:T(8,128)} %reshape.43.refs_0_, ...), custom_call_target="tpu_custom_call" | custom-call | tf_op jit(solution)/shard_map/update/pallas_call | solution.py:1190

commit v4 on v3

--- a/solution.py
+++ b/solution.py
@@ -22,7 +22,6 @@
 NN = ((1,), (0,))
 NT = ((1,), (1,))
 TN = ((0,), (0,))
-LANES = 512
 GROUP = 8
 
 
@@ -85,11 +84,12 @@
 
 
 class Level:
-    def __init__(self, index, nodes, slots, sources):
+    def __init__(self, index, nodes, slots, sources, lanes):
+        self.lanes = lanes
         self.index, self.nodes, self.slots, self.sources = index, nodes, slots, sources
-        self.steps = nodes * slots // LANES
+        self.steps = nodes * slots // lanes
         self.width = GROUP * slots
-        self.blocks = LANES // self.width
+        self.blocks = lanes // self.width
         self.parts = sources // 128
 
 
@@ -112,12 +112,13 @@
         layer, gradf, gwc, gsmall,
         feat, cot, geof, geom, geoc, lkf, slf, send, parf, parm, lkm, slm, lkc, slc, kin, kb, kmid, ownw,
         geom_own, lkc_wide, slc_wide, pk0, pk1, pk2, gm, gc,
-        extT, agbuf, gbuf, s0buf, s0x, smx, smbuf, smfull, waT, wbT, wbr, bbc,
+        extT, agbuf, gbuf, s0buf, s0x, smx, smfull, waT, wbT, wbr, bbc,
         mt0, mt1, mt2, qt1, qt2, as0, as1, as2, xs0, xs1, xs2, zs0, zs1, zs2,
-        ohp, tx_s, rx_s, tx_w, rx_w, tx_q, rx_q, tx_u, rx_u, tx_g, rx_g, tx_b, rx_b, tx_f, rx_f, tx_h, rx_h,
-        x1b, x2T, x2b, acc0, acc1, acc2, acc1b, acc2b, rs1a, rs2a, rs1buf, rs2buf, v0s, gys,
-        rsr0, rsr1, rsr2, rsr3, rsf, rsr4, gsb, rcA, rcB, sems,
+        ohp, tx_s, rx_s, tx_w, rx_w, tx_q, rx_q, tx_u, rx_u, tx_g, rx_g, tx_f, rx_f,
+        x1b, x2T, x2b, acc0, acc1, acc2, acc2b, rs1a, rs2a, rs1buf, rs2buf, v0s, gys,
+        rsr0, rsr1, rsr2, rsr3, rsf, gsb, gp, rcA, rcB, sems,
     ):
+        smbuf, rsr4, acc1b, tx_b, rx_b, tx_h, rx_h = gsb.at[0], s0buf, x1b, tx_u, rx_u, tx_u, rx_u
         t = lax.axis_index("tile")
         g = lax.axis_index("grp")
         core = lax.rem(t, 2)
@@ -142,7 +143,7 @@
             return levels_at[k]
 
         counter = [0]
-        open_recv, open_send = [], []
+        open_recv, open_send, out_copies = [], [], []
 
         def sem_block(n):
             base = counter[0]
@@ -267,10 +268,13 @@
             return c
 
         def finish():
+            loaded(*loads)
             for c in tuple(open_recv):
                 c.recv()
             for c in tuple(open_send):
                 c.sent()
+            for src, dst, k in out_copies:
+                pltpu.make_async_copy(src, dst, sems.at[nil + k]).wait()
 
         barrier = pltpu.get_barrier_semaphore()
 
@@ -423,7 +427,7 @@
             wbr[l] = second.astype(BF)
             wbT[l] = second.T.astype(BF)
             waT[l] = first[:, 0:8].astype(BF)
-            bbc[l] = jnp.broadcast_to(first[:, 8:9], (KW, 128))
+            bbc[:, l : l + 1] = first[:, 8:9]
 
         mts, qts = (mt0, mt1, mt2), (mt0, qt1, qt2)
         xss, zss, pks, a2s = (xs0, xs1, xs2), (zs0, zs1, zs2), (pk0, pk1, pk2), (as0, as1, as2)
@@ -438,11 +442,11 @@
 
         def edge_columns(lv, i):
             k = lv.slots
-            n = LANES // k
+            n = lv.lanes // k
             at = pl.ds(pl.multiple_of(i * n, n), n)
-            nodes = (iota((n, LANES), 1) >> log2(k) == iota((n, LANES), 0)).astype(F32).astype(BF)
+            nodes = (iota((n, lv.lanes), 1) >> log2(k) == iota((n, lv.lanes), 0)).astype(F32).astype(BF)
             got = dot(pks[lv.index][at, :], nodes, TN)
-            slot = iota((k, LANES), 1) & (k - 1) == iota((k, LANES), 0)
+            slot = iota((k, lv.lanes), 1) & (k - 1) == iota((k, lv.lanes), 0)
             links = jnp.sum(jnp.where(slot, got[0:k] + got[k : 2 * k], 0.0), axis=0, keepdims=True)
             return links, got[2 * k : 2 * k + 8]
 
@@ -452,14 +456,14 @@
 
             def some(first):
                 got = dot(table(first, n), hot)
-                acc = jnp.zeros((rows, LANES), F32)
+                acc = jnp.zeros((rows, lv.lanes), F32)
                 for h in range(n):
                     acc = acc + jnp.where(top == first + h, got[rows * h : rows * (h + 1)], 0.0)
                 return acc
 
             if n == lv.parts:
                 return some(0)
-            return lax.fori_loop(0, lv.parts // n, lambda k, acc: acc + some(k * n), jnp.zeros((rows, LANES), F32))
+            return lax.fori_loop(0, lv.parts // n, lambda k, acc: acc + some(k * n), jnp.zeros((rows, lv.lanes), F32))
 
         def put(acc, values, row, lv):
             top, hot = row >> 7, one_hot(row & 127, 0, 128)
@@ -479,10 +483,18 @@
 
             lax.fori_loop(0, lv.parts // n, body, 0)
 
-        def edge_geometry(lv, x_table, g_table, first, last):
+        def at_step(i, events):
+            for when, call in events:
+
+                @pl.when(i == when)
+                def _():
+                    call()
+
+        def edge_geometry(lv, x_table, g_table, events=()):
             l = lv.index
 
             def body(i, _):
+                at_step(i, events)
                 links, z = edge_columns(lv, i)
                 row = links.astype(I32)
                 if g_table is None:
@@ -491,15 +503,15 @@
                     z = z + got[C : C + 8]
                 else:
                     z = z + take(g_table, row, lv, 8)
-                zss[l][i] = jnp.where(iota((8, LANES), 0) == 4, links, z)
+                zss[l][i] = jnp.where(iota((8, lv.lanes), 0) == 4, links, z)
                 return 0
 
-            lax.fori_loop(first, last, body, 0)
+            lax.fori_loop(0, lv.steps, body, 0)
 
         def hidden(l, z):
             t1 = dot(waT[l], z.astype(BF))
             a1 = (t1 * sig(t1)).astype(BF)
-            t2 = dot(wbT[l], a1) + bbc[l][:, 0:1]
+            t2 = dot(wbT[l], a1) + bbc[:, l : l + 1]
             return (t2 * sig(t2)).astype(BF)
 
         def edge_hidden(lv):
@@ -510,13 +522,6 @@
                 return 0
 
             lax.fori_loop(0, lv.steps, body, 0)
-
-        def at_step(i, events):
-            for when, call in events:
-
-                @pl.when(i == when)
-                def _():
-                    call()
 
         def edges_forward(lv, x_table, events=()):
             l = lv.index
@@ -547,7 +552,7 @@
 
         def node_sums(lv):
             l, n = lv.index, lv.nodes
-            each = 4
+            each = 8
 
             def body(i, acc):
                 w = jnp.concatenate([third(l, each * i + u) for u in range(each)], axis=0)
@@ -573,7 +578,7 @@
         def third_grad(lv, gs):
             l = lv.index
             n = C // 4
-            each = 4
+            each = 8
             turned = gs.T.astype(BF)
 
             def body(j, _):
@@ -588,7 +593,7 @@
 
         def node_weights(lv, gs):
             l = lv.index
-            each = 4
+            each = 8
             gs = gs.astype(BF)
 
             def body(j, _):
@@ -632,7 +637,7 @@
                 f1 = t1 * s1
                 d1 = s1 + f1 * (1.0 - s1)
                 a1 = f1.astype(BF)
-                t2 = dot(wbT[l], a1) + bbc[l][:, 0:1]
+                t2 = dot(wbT[l], a1) + bbc[:, l : l + 1]
                 s2 = sig(t2)
                 d2 = s2 + t2 * s2 * (1.0 - s2)
                 x = xss[l][i].astype(F32)
@@ -643,12 +648,11 @@
                     g2s.append((dot(q, spread(x[:, sl], mask), TN) * d2[:, sl]).astype(BF))
                 g2 = jnp.concatenate(g2s, axis=1)
                 g1 = (dot(wbr[l], g2) * d1).astype(BF)
-                sm2 = dot(a1, g2, NT)
-                p1 = dot(g1, zb, NT)
-                p2 = dot(g2, zb, NT)
-                gsb[l, :, :, :, 0:KW] += sm2.reshape(NB, 2, 8, KW)
-                gsb[l, :, :, :, KW : KW + 8] += p1.reshape(NB, 2, 8, 8)
-                gsb[l, :, :, :, KW + 8 : KW + 16] += p2.reshape(NB, 2, 8, 8)
+                zz = jnp.concatenate([zb, zb], axis=0)
+                both = dot(jnp.concatenate([a1, zz], axis=0), g2, NT)
+                gsb[l, :, :, :, 0:KW] += both[0:KW].reshape(NB, 2, 8, KW)
+                gp[l, 0] += dot(zz, g1, NT)[0:8]
+                gp[l, 1] += both[KW : KW + 8]
                 return 0
 
             lax.fori_loop(first, last, body, 0)
@@ -676,12 +680,22 @@
         halo_x.recv()
         near, far = (pltpu.roll(rx_s[k].astype(F32), halo, 1) for k in (0, 1))
         extT[:, n0:] = jnp.where(iota((1, 128), 1) < halo, near, far).astype(BF)
-        edge_geometry(fine, extT, None, 0, fine.steps)
+        small_b = []
+
+        def a0_next():
+            if inside:
+                sm_a0.recv()
+                small_b.append(started(One(smbuf.at[:, core], smbuf.at[:, core], partner)))
+
+        edge_geometry(fine, extT, None, [(2, lambda: ag_s2(0)), (2, lambda: ag_s1(1)), (4, a0_next)])
         if inside:
-            sm_a0.recv()
-            sm_b0 = started(One(smbuf.at[:, core], smbuf.at[:, core], partner))
-        ag_s2(0)
-        ag_s1(1)
+            sm_b0 = small_b[0]
+            sm_b0.recv()
+        unpack_small(0)
+        edges_forward(
+            fine, None,
+            [(3, lambda: ag_s3(0)), (3, lambda: ag_s1(2)), (6, lambda: ag_s4(0)), (6, lambda: ag_s2(1))],
+        )
         loaded("lkm", "slm", "own", "lkc", "slc", "geom", "geoc", "parm", "cot")
         pack_nodes(mid, lkm[...], slm[...], geom_own[...])
         lkc_wide[...] = jnp.zeros(lkc_wide.shape, F32)
@@ -708,16 +722,9 @@
         sides = jnp.where((lanes < 8) & (t > 0), before, jnp.where((lanes >= 8) & (lanes < 16) & (t < T - 1), after, -1.0))
         around = jnp.concatenate([blocks[1], sides], axis=1).astype(I32)
         pw = jnp.where(around < 0, -1, window(around, t * NC, NC, NC))
-        if inside:
-            sm_b0.recv()
-        unpack_small(0)
-        edges_forward(
-            fine, None,
-            [(8, lambda: ag_s3(0)), (8, lambda: ag_s1(2)), (12, lambda: ag_s4(0)), (12, lambda: ag_s2(1))],
-        )
         g_rows = lambda table: lambda first, n: table[pl.ds(first, n)].reshape(n * 8, 128).astype(BF)
-        edge_geometry(mid, None, g_rows(gm), 0, mid.steps)
-        edge_geometry(coarse, None, g_rows(gc), 0, coarse.steps)
+        edge_geometry(mid, None, g_rows(gm))
+        edge_geometry(coarse, None, g_rows(gc))
         ag_fin(0)
         v0 = extT[0:C, 0 : fine.nodes].astype(F32) + node_sums(fine) / nf
         v0s[...] = v0
@@ -749,7 +756,7 @@
         def x1_rows(first, n):
             return x1b[pl.ds(first // 2, n // 2)].reshape(n * C, 128)
 
-        edges_forward(mid, x1_rows, [(4, lambda: ag_s3(2))])
+        edges_forward(mid, x1_rows, [(2, lambda: ag_s3(2))])
         ag_fin(1)
         unpack_small(2)
         w1 = v1 + node_sums(mid) / nm
@@ -822,13 +829,16 @@
                 c.start()
             rs[l].append(copies)
 
+        def landing(l):
+            return gbuf.at[ix(2 - l)] if l and inside else rsr0
+
         def rs_s0(l):
-            rs_step(l, lambda: None, One(stage(l).at[ocore], rsr0.at[ix(l % 2)], partner))
+            rs_step(l, lambda: None, One(stage(l).at[ocore], landing(l), partner))
 
         def rs_s1(l):
             def fix():
                 def body(i, _):
-                    both = stage(l)[core, i].astype(F32) + rsr0[l % 2, i].astype(F32)
+                    both = stage(l)[core, i].astype(F32) + landing(l)[i].astype(F32)
                     stage(l)[core, i] = both.astype(BF)
                     return 0
 
@@ -836,16 +846,16 @@
 
             rs_step(
                 l, fix,
-                One(stage(l).at[core, :, olo, og, :, 0:QH], rsr1.at[ix(l), ix(0)], xn),
-                One(stage(l).at[core, :, olo, og, :, QH:HALF], rsr1.at[ix(l), ix(1)], yn),
+                One(stage(l).at[core, :, olo, og, :, 0:QH], rsr1.at[ix(l % 2), ix(0)], xn),
+                One(stage(l).at[core, :, olo, og, :, QH:HALF], rsr1.at[ix(l % 2), ix(1)], yn),
             )
 
         def rs_s2(l):
             def fix():
                 def body(i, _):
-                    a = stage(l)[core, i, lo, og, :, 0:QH].astype(F32) + rsr1[l, 0, i].astype(F32)
+                    a = stage(l)[core, i, lo, og, :, 0:QH].astype(F32) + rsr1[l % 2, 0, i].astype(F32)
                     stage(l)[core, i, lo, og, :, 0:QH] = a.astype(BF)
-                    b = stage(l)[core, i, olo, g, :, QH:HALF].astype(F32) + rsr1[l, 1, i].astype(F32)
+                    b = stage(l)[core, i, olo, g, :, QH:HALF].astype(F32) + rsr1[l % 2, 1, i].astype(F32)
                     stage(l)[core, i, olo, g, :, QH:HALF] = b.astype(BF)
                     return 0
 
@@ -853,14 +863,14 @@
 
             rs_step(
                 l, fix,
-                One(stage(l).at[core, :, lo, og], rsr2.at[ix(l), ix(0)], yn),
-                One(stage(l).at[core, :, olo, g], rsr2.at[ix(l), ix(1)], xn),
+                One(stage(l).at[core, :, lo, og], rsr2.at[ix(l % 2), ix(0)], yn),
+                One(stage(l).at[core, :, olo, g], rsr2.at[ix(l % 2), ix(1)], xn),
             )
 
         def rs_s3(l):
             def fix():
                 def body(i, _):
-                    a = stage(l)[core, i, lo, g].astype(F32) + rsr2[l, 0, i].astype(F32) + rsr2[l, 1, i].astype(F32)
+                    a = stage(l)[core, i, lo, g].astype(F32) + rsr2[l % 2, 0, i].astype(F32) + rsr2[l % 2, 1, i].astype(F32)
                     stage(l)[core, i, lo, g] = a.astype(BF)
                     return 0
 
@@ -871,7 +881,7 @@
                 Ring(
                     H,
                     lambda d: stage(l).at[core, lax.rem(hi + d, H), lo, g],
-                    lambda d: rsr3.at[ix(l), d - 1],
+                    lambda d: rsr3.at[ix(l % 2), d - 1],
                     lambda d: {"tile": tile_of(lax.rem(hi + d, H), lo, core), "grp": g},
                 ),
             )
@@ -880,7 +890,7 @@
             def fix():
                 tot = stage(l)[core, hi, lo, g].astype(F32)
                 for k in range(H - 1):
-                    tot = tot + rsr3[l, k].astype(F32)
+                    tot = tot + rsr3[l % 2, k].astype(F32)
                 rsf[l, 0] = tot[0:8]
                 rsf[l, 1] = tot[8:16]
 
@@ -892,13 +902,21 @@
                 return
             for c in rs[l][-1]:
                 c.recv()
-            gwc[l, core] = rsf[l, core]
-            gwc[l, ocore] = rsr4[l]
-
+            for src, dst in ((rsf.at[ix(l), core], gwc.at[ix(l), core]), (rsr4.at[ix(l)], gwc.at[ix(l), ocore])):
+                out_copies.append((src, dst, sem_block(1)))
+                pltpu.make_async_copy(src, dst, sems.at[nil + out_copies[-1][2]]).start()
+
+        if inside:
+            sm_a0.sent()
+            sm_b0.sent()
         gsb[...] = jnp.zeros(gsb.shape, F32)
+        gp[...] = jnp.zeros(gp.shape, F32)
         gs_copies = {}
 
         def gs_start(a, b):
+            for l in range(a, b):
+                tall = jnp.concatenate([gp[l, 0], gp[l, 1], jnp.zeros((112, KW), F32)], axis=0)
+                gsb[l, :, :, :, KW:] = tall.T.reshape(NB, 2, 8, 128)
             if inside:
                 gs_copies[a] = started(One(gsb.at[a:b, :, ocore], rcA.at[a:b], partner))
 
@@ -952,6 +970,7 @@
         own2 = lax.fori_loop(0, R - 1, add2, acc2b[r, core].astype(F32))
         own2 = jnp.concatenate([own2, jnp.zeros((128 - NC, 128), F32)], axis=0).T[0:C]
         gv2 = jnp.where(mine, (gw2 + own2) / cnt2, 0.0)
+        ex_u.sent()
         tx_b[0] = gv2
         ex_b = started(Sides(tx_b.at[0], tx_b.at[0], rx_b))
         rs_s0(2)
@@ -964,7 +983,9 @@
         node_weights(mid, gs1)
         acc1[...] = jnp.zeros(acc1.shape, F32)
         rs_s1(2)
-        source_grads(mid, acc1, [(5, lambda: rs_s2(2))])
+        source_grads(mid, acc1, [(2, lambda: rs_s2(2))])
+        ag1.sent()
+        ag1p.sent()
         acc1b[...] = acc1[...].astype(BF).reshape(acc1b.shape)
         r1p = started(One(acc1b.at[:, ocore], rs1a, partner))
         half = mid.steps // 2
@@ -999,18 +1020,20 @@
         rs_s0(0)
         node_weights(fine, gs0)
         rs_s1(0)
+        rs_s4(2)
         rs_s3(1)
-        rs_s4(2)
+        gs_start(1, 3)
         weight_grads(
             fine, 0, fine.steps,
-            [(1, lambda: gs_start(1, 3)), (5, lambda: rs_s2(0)), (6, lambda: rs_s4(1)), (7, lambda: rs_s5(2)),
-             (8, lambda: gs_ring(1, 3)), (9, lambda: rs_s5(1)), (13, lambda: rs_s3(0))],
+            [(1, lambda: rs_s4(1)), (2, lambda: rs_s5(2)), (3, lambda: rs_s2(0)), (4, lambda: gs_ring(1, 3)),
+             (5, lambda: rs_s5(1)), (6, lambda: rs_s3(0))],
         )
         gs_start(0, 1)
         acc0[...] = jnp.zeros(acc0.shape, F32)
         source_grads(
-            fine, acc0, [(2, lambda: gs_ring(0, 1)), (6, lambda: gs_end(1, 3)), (12, lambda: rs_s4(0))]
+            fine, acc0, [(1, lambda: gs_ring(0, 1)), (3, lambda: gs_end(1, 3)), (6, lambda: rs_s4(0))]
         )
+        ex_b.sent()
         tx_h[0] = acc0[fine.parts - 1]
         ex_h = started(Sides(tx_h.at[0], tx_h.at[0], rx_h))
         rs_s5(0)
@@ -1029,7 +1052,7 @@
         + 4 * 7 + 4 * (2 * (T - 1)) + 4 * NCH + 3 * (2 + 4 + 4 + 2 * (H - 1) + 2) + 2 + 2 * (NCH - 1) + 32
     )
     V = pltpu.VMEM
-    ls = 3 if inside else 1
+    ls, la = (3, A) if inside else (1, 1)
     by_group = lambda n: V((C // 2, n // GROUP, 2 * GROUP, KW), BF)
     nf, nm_, nc_ = fine.nodes, NM, NC
     scratch = [
@@ -1042,11 +1065,11 @@
         V((80, nf + 2 * halo), BF),
         V((3, 2, A, 2, NG, 16, BW if inside else HALF), BF), V((2, A, 2, NG, 16, HALF), BF), V((ls, 8, HALF), F32),
         V((2, 8, KW), F32), V((2, 2, 8, KW), F32),
-        V((NB, 2, 8, SMW), F32), V((1 if inside else 3, 1 if inside else NB, 2, 8, SMW), F32), V((3, KW, 8), BF), V((3, KW, KW), BF), V((3, KW, KW), BF), V((3, KW, 128), F32),
+        V((1 if inside else 3, 1 if inside else NB, 2, 8, SMW), F32), V((3, KW, 8), BF), V((3, KW, KW), BF), V((3, KW, KW), BF), V((KW, 128), F32),
         by_group(nf), by_group(nm_), by_group(nc_), by_group(nm_), by_group(nc_),
-        V((fine.steps, KW, LANES), BF), V((mid.steps, KW, LANES), BF), V((coarse.steps, KW, LANES), BF),
-        V((fine.steps, C, LANES), BF), V((mid.steps, C, LANES), BF), V((coarse.steps, C, LANES), BF),
-        V((fine.steps, 8, LANES), F32), V((mid.steps, 8, LANES), F32), V((coarse.steps, 8, LANES), F32),
+        V((fine.steps, KW, fine.lanes), BF), V((mid.steps, KW, fine.lanes), BF), V((coarse.steps, KW, fine.lanes), BF),
+        V((fine.steps, C, fine.lanes), BF), V((mid.steps, C, fine.lanes), BF), V((coarse.steps, C, fine.lanes), BF),
+        V((fine.steps, 8, fine.lanes), F32), V((mid.steps, 8, fine.lanes), F32), V((coarse.steps, 8, fine.lanes), F32),
         V((2 * NM, nf), BF),
         V((1, 80, 128), BF), V((2, 80, 128), BF),
         V((1, C + 8, 128), F32), V((2, C + 8, 128), F32),
@@ -1054,15 +1077,13 @@
         V((1, C, 128), F32), V((2, C, 128), F32),
         V((1, 2 * C, 128), F32), V((2, 2 * C, 128), F32),
         V((1, C, 128), F32), V((2, C, 128), F32),
-        V((1, C, 128), F32), V((2, C, 128), F32),
-        V((1, C, 128), F32), V((2, C, 128), F32),
         V((R, 2, C, 128), BF), V((coarse.parts, C, 128), BF), V((R, 2, C, 128), BF),
         V((fine.parts, C, 128), F32), V((mid.parts, C, 128), F32), V((coarse.parts, C, 128), F32),
-        V((R, 2, C, 128), BF), V((R, 2, NC, 128), BF), V((R, C, 128), BF), V((R, NC, 128), BF),
+        V((R, 2, NC, 128), BF), V((R, C, 128), BF), V((R, NC, 128), BF),
         V((R - 1, C, 128), BF), V((R - 1, NC, 128), BF), V((C, nf), F32), V((C, nf), F32),
-        V((min(ls, 2), A, 2, NG, 16, HALF), BF), V((ls, 2, A, 16, QH), BF), V((ls, 2, A, 16, HALF), BF),
-        V((ls, A - 1, 16, HALF), BF), V((ls, 2, 8, HALF), F32), V((ls, 8, HALF), F32),
-        V((3, NB, 2, 8, SMW), F32), V((ls, NB, 8, SMW), F32), V((NB - 1, 3, 8, SMW), F32),
+        V((la, 2, NG, 16, HALF), BF), V((2, 2, la, 16, QH), BF), V((2, 2, la, 16, HALF), BF),
+        V((2, A - 1, 16, HALF), BF), V((ls, 2, 8, HALF), F32),
+        V((3, NB, 2, 8, SMW), F32), V((3, 2, 8, KW), F32), V((ls, NB, 8, SMW), F32), V((NB - 1, 3, 8, SMW), F32),
         pltpu.SemaphoreType.DMA((n_sems,)),
     ]
     return kernel, scratch
@@ -1084,12 +1105,18 @@
 
     def kernel(*refs):
         far_in, far_out, near_in, near_out, sems = refs[0:14], refs[16:28], refs[30:44], refs[44:56], refs[56]
-        out = [pltpu.make_async_copy(refs[14 + k], refs[28 + k], sems.at[26 + k]) for k in range(2)]
-        for c in out:
+        passing = refs[57:59]
+        first = [pltpu.make_async_copy(refs[14 + k], passing[k], sems.at[26 + k]) for k in range(2)]
+        for c in first:
             c.start()
+        out = []
         copies = [pltpu.make_async_copy(a, b, sems.at[k]) for k, (a, b) in enumerate(zip(far_in, near_in))]
         for c in copies:
             c.start()
+        for k in range(2):
+            first[k].wait()
+            out.append(pltpu.make_async_copy(passing[k], refs[28 + k], sems.at[28 + k]))
+            out[-1].start()
         for c in copies:
             c.wait()
         gwc, gsmall = near_in[0:2]
@@ -1138,11 +1165,12 @@
     NM, NC = links_mid.shape[1], links_coarse.shape[1]
     halo = send_lists.shape[1] // 2
     nf = features.shape[1]
-    fine = Level(0, nf, links_fine.shape[2], nf + 2 * halo)
-    mid = Level(1, NM, links_mid.shape[2], geom_mid.shape[1])
-    coarse = Level(2, NC, links_coarse.shape[2], geom_coarse.shape[1])
     per = kernel_mid.shape[1]
     inside = per == 8
+    lanes = 1024 if inside else 512
+    fine = Level(0, nf, links_fine.shape[2], nf + 2 * halo, lanes)
+    mid = Level(1, NM, links_mid.shape[2], geom_mid.shape[1], lanes)
+    coarse = Level(2, NC, links_coarse.shape[2], geom_coarse.shape[1], lanes)
     everyone = ("tile", "grp")
     half = C * C // 2
     grid = (3, 2, KW // (32 * NG), 2, NG, 16, half)
@@ -1174,10 +1202,10 @@
         out_shape=(S((C, nf), BF), S((C, nf), BF), S((3, 2, 8, half), F32) if inside else S(grid, BF),
                    S((3, 8, KW + 128) if inside else (3, KW // 16, 2, 8, KW + 128), F32)),
         in_specs=[far] * len(operands),
-        out_specs=(vm, vm, vm if inside else far, vm),
+        out_specs=(vm, vm, far, vm),
         scratch_shapes=scratch,
         compiler_params=pltpu.CompilerParams(
-            collective_id=0, has_side_effects=True, vmem_limit_bytes=63 << 20
+            collective_id=0, has_side_effects=True, vmem_limit_bytes=(64 << 20) - (1 << 16)
         ),
         name="layer",
     )(*operands)
@@ -1193,7 +1221,7 @@
         in_specs=[far] * 16,
         out_specs=(far,) * 14,
         scratch_shapes=[pltpu.VMEM(v.shape, F32) for v in (gwc, gsmall) + state]
-        + [pltpu.VMEM(v.shape, F32) for v in state] + [pltpu.SemaphoreType.DMA((28,))],
+        + [pltpu.VMEM(v.shape, F32) for v in state] + [pltpu.SemaphoreType.DMA((30,))] + [pltpu.VMEM((C, nf), BF)] * 2,
         compiler_params=pltpu.CompilerParams(vmem_limit_bytes=63 << 20),
         name="update",
     )(gwc, gsmall, *state, layer, gradf)

time: 188 us -> 170 us (0.904)
  Pallas kernels: 181 us -> 163 us
    pallas_call x1, Pallas kernels: 175 us -> 159 us  [per_device(): pl.pallas_call(kernel, out_shape=(S((C, nf), BF), S((C, nf), BF), S((3, 2...]
where the time goes in v4:
time: 170 us
  Pallas kernels  163 us (96%)
  local copies, waits for them, and re-layouts  6.03 us (4%)
    pallas_call x1, Pallas kernels, per_device(): pl.pallas_call(kernel, out_shape=(S((C, nf), BF), S((C, nf), BF), S((3, 2...  159 us
    pallas_call x1, Pallas kernels, per_device(): pl.pallas_call(make_update(KW, NG, per, inside), out_shape=tuple((S(v.sha...  3.54 us

profile of v4, /device:TPU:1, one launch (start us, length us, event | category | flops | bytes accessed | tf_op | source)
XLA Modules:
  0.0 169.5 jit_solution(17301781795954011470)
XLA Ops:
  0.6 1.3 reshape.40
  2.0 0.3 copy.40
  2.2 0.4 reshape.41
  2.6 1.0 copy.45
  3.6 159.1 %layer.1 = (bf16[64,512]{1,0:T(8,128)(2,1)}, bf16[64,512]{1,0:T(8,128)(2,1)}, f32[3,2,8,2048]{3,2,1,0:T(8,128)}, f32[3,8,384]{2,1,0:T(8,128)}) custom-call(bf16[64,512]{1,0:T(8,128)(2,1)} %bitcast.45, f32[64,512]{1,0:T(8,128)} %bitcast.44, bf16[3,512]{1,0:T(4,128)(2,1)} %bitcast.50, bf16[3,2048]{1,0:T(4,128)(2,1)} %bitcast.47, bf16[3,512]{1,0:T(4,128)(2,1)} %bitcast.51, ...), custom_call_target="tpu_custom_call" | custom-call | tf_op jit(solution)/shard_map/layer/pallas_call | solution.py:1200
  162.7 1.3 copy.42
  164.0 0.5 reshape.42
  164.5 0.3 copy.43
  164.8 1.0 reshape.43.refs_0_
  165.8 3.5 %update.1 = (f32[3,6,8]{2,1,0:T(8,128)}, f32[3,2,8]{2,1,0:T(2,128)}, f32[3,8,256]{2,1,0:T(8,128)}, f32[3,8,4096]{2,1,0:T(8,128)}, f32[3,6,8]{2,1,0:T(8,128)}, /*...) custom-call(f32[3,8,4096]{2,1,0:T(8,128)} %reshape.43.refs_0_, ...), custom_call_target="tpu_custom_call" | custom-call | tf_op jit(solution)/shard_map/update/pallas_call | solution.py:1218

commit v5 on v4

--- a/solution.py
+++ b/solution.py
@@ -591,12 +591,13 @@
 
             lax.fori_loop(0, C // 2 // each, body, 0)
 
-        def node_weights(lv, gs):
+        def node_weights(lv, gs, events=()):
             l = lv.index
             each = 8
             gs = gs.astype(BF)
 
             def body(j, _):
+                at_step(j, events)
                 for u in range(each):
                     i = each * j + u
                     q = dot(gs, third(l, i), NT)
@@ -676,7 +677,6 @@
         ag_s1(0)
         loaded("lkf", "slf", "parf")
         pack_nodes(fine, lkf[...], slf[...], geof[...])
-        ohp[...] = one_hot(window(parf[...], t * NM, NM, NM), 0, 2 * NM)
         halo_x.recv()
         near, far = (pltpu.roll(rx_s[k].astype(F32), halo, 1) for k in (0, 1))
         extT[:, n0:] = jnp.where(iota((1, 128), 1) < halo, near, far).astype(BF)
@@ -694,8 +694,19 @@
         unpack_small(0)
         edges_forward(
             fine, None,
-            [(3, lambda: ag_s3(0)), (3, lambda: ag_s1(2)), (6, lambda: ag_s4(0)), (6, lambda: ag_s2(1))],
+            [(2, lambda: ag_s3(0)), (2, lambda: ag_s1(2)), (5, lambda: ag_s4(0)), (5, lambda: ag_s2(1))],
         )
+        ohp[...] = one_hot(window(parf[...], t * NM, NM, NM), 0, 2 * NM)
+        nf = slf[...].astype(F32)
+        ag_fin(0)
+        v0 = extT[0:C, 0 : fine.nodes].astype(F32) + node_sums(fine) / nf
+        v0s[...] = v0
+
+        ones8 = jnp.ones((8, fine.nodes), BF)
+        part = dot(jnp.concatenate([split3(v0), ones8], axis=0), ohp[...], NT)
+        sums = jnp.concatenate([join3(part[0 : 3 * C]), part[3 * C :]], axis=0)
+        tx_w[0] = sums[:, NM:]
+        ex_w = started(Sides(tx_w.at[0], tx_w.at[0], rx_w))
         loaded("lkm", "slm", "own", "lkc", "slc", "geom", "geoc", "parm", "cot")
         pack_nodes(mid, lkm[...], slm[...], geom_own[...])
         lkc_wide[...] = jnp.zeros(lkc_wide.shape, F32)
@@ -715,25 +726,13 @@
             rows = dot(to_rows, source[...])
             for k in range(lv.parts):
                 table[k] = rows[:, 128 * k : 128 * (k + 1)]
-        nf, nm, nc = (v[...].astype(F32) for v in (slf, slm, slc_wide))
+        nm, nc = (v[...].astype(F32) for v in (slm, slc_wide))
         blocks = [parm[:, pl.ds(pl.multiple_of(b * NM, NM), NM)].astype(F32)
                   for b in (jnp.maximum(t - 1, 0), t, jnp.minimum(t + 1, T - 1))]
         before, after = (pltpu.roll(jnp.broadcast_to(v, (8, NM)), 8, 1)[0:1] for v in (blocks[0], blocks[2]))
         sides = jnp.where((lanes < 8) & (t > 0), before, jnp.where((lanes >= 8) & (lanes < 16) & (t < T - 1), after, -1.0))
         around = jnp.concatenate([blocks[1], sides], axis=1).astype(I32)
         pw = jnp.where(around < 0, -1, window(around, t * NC, NC, NC))
-        g_rows = lambda table: lambda first, n: table[pl.ds(first, n)].reshape(n * 8, 128).astype(BF)
-        edge_geometry(mid, None, g_rows(gm))
-        edge_geometry(coarse, None, g_rows(gc))
-        ag_fin(0)
-        v0 = extT[0:C, 0 : fine.nodes].astype(F32) + node_sums(fine) / nf
-        v0s[...] = v0
-
-        ones8 = jnp.ones((8, fine.nodes), BF)
-        part = dot(jnp.concatenate([split3(v0), ones8], axis=0), ohp[...], NT)
-        sums = jnp.concatenate([join3(part[0 : 3 * C]), part[3 * C :]], axis=0)
-        tx_w[0] = sums[:, NM:]
-        ex_w = started(Sides(tx_w.at[0], tx_w.at[0], rx_w))
         unpack_small(1)
         ag_s3(1)
         ex_w.recv()
@@ -747,6 +746,8 @@
 
         ag1 = started(chip_ring(lambda d: x1b.at[r, core], lambda d: x1b.at[r, core]))
         ag_s2(2)
+        g_rows = lambda table: lambda first, n: table[pl.ds(first, n)].reshape(n * 8, 128).astype(BF)
+        edge_geometry(mid, None, g_rows(gm))
         edge_hidden(mid)
         ag_s4(1)
         ag1.recv()
@@ -765,6 +766,7 @@
         part = dot(jnp.concatenate([split3(w1), jnp.ones((8, NM), BF)], axis=0), ohq[:, 0:NM], NT)
         tx_q[0, C : 2 * C + 8] = jnp.concatenate([join3(part[0 : 3 * C]), part[3 * C :]], axis=0)
         ex_q = started(Sides(tx_q.at[0], tx_q.at[0], rx_q))
+        edge_geometry(coarse, None, g_rows(gc))
         edge_hidden(coarse)
         ag_s4(2)
         ex_q.recv()
@@ -1007,6 +1009,7 @@
         rs_s1(1)
         rs_s3(2)
         weight_grads(mid, half, mid.steps)
+        gs_start(1, 3)
         ex_f.recv()
         gv1win = jnp.concatenate([gv1, roll_pick(rx_f[0], rx_f[1], NM, 0, 8)], axis=1)
         gv0 = gys[...] + join3(dot(split3(gv1win), ohp[...]))
@@ -1016,22 +1019,20 @@
         gs0T = gs0.astype(BF)
         gs0 = by_parity(fine, gs0T)
         rs_s2(1)
+        gs_ring(1, 3)
         third_grad(fine, gs0)
         rs_s0(0)
-        node_weights(fine, gs0)
-        rs_s1(0)
+        node_weights(fine, gs0, [(1, lambda: rs_s1(0))])
         rs_s4(2)
         rs_s3(1)
-        gs_start(1, 3)
         weight_grads(
             fine, 0, fine.steps,
-            [(1, lambda: rs_s4(1)), (2, lambda: rs_s5(2)), (3, lambda: rs_s2(0)), (4, lambda: gs_ring(1, 3)),
-             (5, lambda: rs_s5(1)), (6, lambda: rs_s3(0))],
+            [(2, lambda: rs_s2(0)), (3, lambda: rs_s5(2)), (5, lambda: rs_s4(1)), (7, lambda: rs_s3(0))],
         )
         gs_start(0, 1)
         acc0[...] = jnp.zeros(acc0.shape, F32)
         source_grads(
-            fine, acc0, [(1, lambda: gs_ring(0, 1)), (3, lambda: gs_end(1, 3)), (6, lambda: rs_s4(0))]
+            fine, acc0, [(1, lambda: gs_ring(0, 1)), (2, lambda: rs_s5(1)), (3, lambda: gs_end(1, 3)), (6, lambda: rs_s4(0))]
         )
         ex_b.sent()
         tx_h[0] = acc0[fine.parts - 1]

time: 170 us -> 160 us (0.941)
  Pallas kernels: 163 us -> 153 us
    pallas_call x1, Pallas kernels: 159 us -> 150 us  [per_device(): pl.pallas_call(kernel, out_shape=(S((C, nf), BF), S((C, nf), BF), S((3, 2...]
where the time goes in v5:
time: 160 us
  Pallas kernels  153 us (96%)
  local copies, waits for them, and re-layouts  6.03 us (4%)
    pallas_call x1, Pallas kernels, per_device(): pl.pallas_call(kernel, out_shape=(S((C, nf), BF), S((C, nf), BF), S((3, 2...  150 us
    pallas_call x1, Pallas kernels, per_device(): pl.pallas_call(make_update(KW, NG, per, inside), out_shape=tuple((S(v.sha...  3.54 us

profile of v5, /device:TPU:1, one launch (start us, length us, event | category | flops | bytes accessed | tf_op | source)
XLA Modules:
  0.0 160.1 jit_solution(2079126093206740838)
XLA Ops:
  0.6 1.3 reshape.40
  2.0 0.3 copy.40
  2.2 0.4 reshape.41
  2.6 1.0 copy.45
  3.6 149.7 %layer.1 = (bf16[64,512]{1,0:T(8,128)(2,1)}, bf16[64,512]{1,0:T(8,128)(2,1)}, f32[3,2,8,2048]{3,2,1,0:T(8,128)}, f32[3,8,384]{2,1,0:T(8,128)}) custom-call(bf16[64,512]{1,0:T(8,128)(2,1)} %bitcast.45, f32[64,512]{1,0:T(8,128)} %bitcast.44, bf16[3,512]{1,0:T(4,128)(2,1)} %bitcast.50, bf16[3,2048]{1,0:T(4,128)(2,1)} %bitcast.47, bf16[3,512]{1,0:T(4,128)(2,1)} %bitcast.51, ...), custom_call_target="tpu_custom_call" | custom-call | tf_op jit(solution)/shard_map/layer/pallas_call | solution.py:1201
  153.3 1.3 copy.42
  154.6 0.5 reshape.42
  155.1 0.3 copy.43
  155.4 1.0 reshape.43.refs_0_
  156.4 3.5 %update.1 = (f32[3,6,8]{2,1,0:T(8,128)}, f32[3,2,8]{2,1,0:T(2,128)}, f32[3,8,256]{2,1,0:T(8,128)}, f32[3,8,4096]{2,1,0:T(8,128)}, f32[3,6,8]{2,1,0:T(8,128)}, /*...) custom-call(f32[3,8,4096]{2,1,0:T(8,128)} %reshape.43.refs_0_, ...), custom_call_target="tpu_custom_call" | custom-call | tf_op jit(solution)/shard_map/update/pallas_call | solution.py:1219

commit v6 on v5

--- a/solution.py
+++ b/solution.py
@@ -778,18 +778,29 @@
         cnt2 = jnp.maximum(own[C : C + 1], 1.0)
         v2 = jnp.where(mine, own[0:C] / cnt2, 0.0)
 
-        x2b[r, core] = v2.astype(BF)
+        per = 128 // NC
+        group = C // per
+        packed = v2[0:group]
+        for q in range(1, per):
+            packed = packed + pltpu.roll(v2[group * q : group * (q + 1)], NC * q, 1)
+        x2b[r, core] = packed.astype(BF)
         ag2 = started(chip_ring(lambda d: x2b.at[r, core], lambda d: x2b.at[r, core]))
         ag2.recv()
         ag2p = started(One(x2b.at[:, core], x2b.at[:, core], partner))
         ag2p.recv()
-        per = 128 // NC
         cols = []
+        spot = iota((1, 128), 1) >> log2(NC)
         for k in range(coarse.sources // 128):
-            block = x2b[per * k // 2, 0].astype(F32)
-            for u in range(1, per):
-                block = block + pltpu.roll(x2b[(per * k + u) // 2, (per * k + u) % 2].astype(F32), NC * u, 1)
-            cols.append(block.astype(BF))
+            parts = [x2b[(per * k + u) // 2, (per * k + u) % 2].astype(F32) for u in range(per)]
+            rows = []
+            for q in range(per):
+                row = jnp.zeros((group, 128), F32)
+                for u in range(per):
+                    shift = NC * (u - q) % 128
+                    moved = pltpu.roll(parts[u], shift, 1) if shift else parts[u]
+                    row = jnp.where(spot == u, moved, row)
+                rows.append(row)
+            cols.append(jnp.concatenate(rows, axis=0).astype(BF))
         for k, block in enumerate(cols):
             x2T[k] = block
         edges_forward(coarse, lambda first, n: x2T[pl.ds(first, n)].reshape(n * C, 128))
@@ -958,12 +969,11 @@
             rows = jnp.concatenate([acc2[k], zero], axis=0).T.astype(BF)
             acc2b[per // 2 * k : per // 2 * (k + 1)] = rows.reshape(per // 2, 2, NC, 128)
         r2p = started(One(acc2b.at[:, ocore], rs2a, partner))
-        weight_grads(coarse, 0, 1)
         r2p.recv()
         acc2b[:, core] = (acc2b[:, core].astype(F32) + rs2a[...].astype(F32)).astype(BF)
         r2 = started(chip_ring(lambda d: acc2b.at[lax.rem(r + d, R), core], lambda d: rs2buf.at[d - 1]))
-        weight_grads(coarse, 1, coarse.steps)
         third_grad(coarse, gs2)
+        weight_grads(coarse, 0, coarse.steps)
         r2.recv()
 
         def add2(k, acc):
@@ -991,10 +1001,10 @@
         acc1b[...] = acc1[...].astype(BF).reshape(acc1b.shape)
         r1p = started(One(acc1b.at[:, ocore], rs1a, partner))
         half = mid.steps // 2
-        third_grad(mid, gs1)
         r1p.recv()
         acc1b[:, core] = (acc1b[:, core].astype(F32) + rs1a[...].astype(F32)).astype(BF)
         r1 = started(chip_ring(lambda d: acc1b.at[lax.rem(r + d, R), core], lambda d: rs1buf.at[d - 1]))
+        third_grad(mid, gs1)
         rs_s0(1)
         weight_grads(mid, 0, half)
         r1.recv()
@@ -1078,7 +1088,7 @@
         V((1, C, 128), F32), V((2, C, 128), F32),
         V((1, 2 * C, 128), F32), V((2, 2 * C, 128), F32),
         V((1, C, 128), F32), V((2, C, 128), F32),
-        V((R, 2, C, 128), BF), V((coarse.parts, C, 128), BF), V((R, 2, C, 128), BF),
+        V((R, 2, C, 128), BF), V((coarse.parts, C, 128), BF), V((R, 2, C * NC // 128, 128), BF),
         V((fine.parts, C, 128), F32), V((mid.parts, C, 128), F32), V((coarse.parts, C, 128), F32),
         V((R, 2, NC, 128), BF), V((R, C, 128), BF), V((R, NC, 128), BF),
         V((R - 1, C, 128), BF), V((R - 1, NC, 128), BF), V((C, nf), F32), V((C, nf), F32),
@@ -1111,15 +1121,18 @@
         for c in first:
             c.start()
         out = []
-        copies = [pltpu.make_async_copy(a, b, sems.at[k]) for k, (a, b) in enumerate(zip(far_in, near_in))]
-        for c in copies:
+        large = (0, 5, 9, 13)
+        copies = [pltpu.make_async_copy(far_in[k], near_in[k], sems.at[k]) for k in range(14) if k not in large]
+        levels = [
+            [pltpu.make_async_copy(far_in[k].at[l], near_in[k].at[l], sems.at[30 + 4 * l + m]) for m, k in enumerate(large)]
+            for l in range(3)
+        ]
+        for c in sum(levels, []) + copies:
             c.start()
         for k in range(2):
             first[k].wait()
             out.append(pltpu.make_async_copy(passing[k], refs[28 + k], sems.at[28 + k]))
             out[-1].start()
-        for c in copies:
-            c.wait()
         gwc, gsmall = near_in[0:2]
         order = column_order(KW, NG, False)
 
@@ -1135,8 +1148,15 @@
                 out.append(c)
 
         for l in range(3):
+            for c in levels[l]:
+                c.wait()
             update(3, l, gwc[l])
-        done(3)
+            for m in range(3):
+                k = 4 * m + 3
+                out.append(pltpu.make_async_copy(near_out[k].at[l], far_out[k].at[l], sems.at[42 + 3 * l + m]))
+                out[-1].start()
+        for c in copies:
+            c.wait()
         for l in range(3):
             grad = gsmall[l, :, 0:KW]
             update(2, l, join3(dot(split3(grad), order)) if inside else grad)
@@ -1222,7 +1242,7 @@
         in_specs=[far] * 16,
         out_specs=(far,) * 14,
         scratch_shapes=[pltpu.VMEM(v.shape, F32) for v in (gwc, gsmall) + state]
-        + [pltpu.VMEM(v.shape, F32) for v in state] + [pltpu.SemaphoreType.DMA((30,))] + [pltpu.VMEM((C, nf), BF)] * 2,
+        + [pltpu.VMEM(v.shape, F32) for v in state] + [pltpu.SemaphoreType.DMA((51,))] + [pltpu.VMEM((C, nf), BF)] * 2,
         compiler_params=pltpu.CompilerParams(vmem_limit_bytes=63 << 20),
         name="update",
     )(gwc, gsmall, *state, layer, gradf)

time: 160 us -> 159 us (level)
  no operation moved by 1% of the time
where the time goes in v6:
time: 159 us
  Pallas kernels  152 us (96%)
  local copies, waits for them, and re-layouts  6.03 us (4%)
    pallas_call x1, Pallas kernels, per_device(): pl.pallas_call(kernel, out_shape=(S((C, nf), BF), S((C, nf), BF), S((3, 2...  149 us

profile of v6, /device:TPU:1, one launch (start us, length us, event | category | flops | bytes accessed | tf_op | source)
XLA Modules:
  0.0 158.8 jit_solution(13747116194271276742)
XLA Ops:
  0.6 1.3 reshape.40
  2.0 0.3 copy.40
  2.2 0.4 reshape.41
  2.6 1.0 copy.45
  3.6 149.0 %layer.1 = (bf16[64,512]{1,0:T(8,128)(2,1)}, bf16[64,512]{1,0:T(8,128)(2,1)}, f32[3,2,8,2048]{3,2,1,0:T(8,128)}, f32[3,8,384]{2,1,0:T(8,128)}) custom-call(bf16[64,512]{1,0:T(8,128)(2,1)} %bitcast.45, f32[64,512]{1,0:T(8,128)} %bitcast.44, bf16[3,512]{1,0:T(4,128)(2,1)} %bitcast.50, bf16[3,2048]{1,0:T(4,128)(2,1)} %bitcast.47, bf16[3,512]{1,0:T(4,128)(2,1)} %bitcast.51, ...), custom_call_target="tpu_custom_call" | custom-call | tf_op jit(solution)/shard_map/layer/pallas_call | solution.py:1221
  152.6 1.3 copy.42
  153.9 0.5 reshape.42
  154.4 0.3 copy.43
  154.7 1.0 reshape.43.refs_0_
  155.7 2.9 %update.1 = (f32[3,6,8]{2,1,0:T(8,128)}, f32[3,2,8]{2,1,0:T(2,128)}, f32[3,8,256]{2,1,0:T(8,128)}, f32[3,8,4096]{2,1,0:T(8,128)}, f32[3,6,8]{2,1,0:T(8,128)}, /*...) custom-call(f32[3,8,4096]{2,1,0:T(8,128)} %reshape.43.refs_0_, ...), custom_call_target="tpu_custom_call" | custom-call | tf_op jit(solution)/shard_map/update/pallas_call | solution.py:1239
